TPU v7x, 32 devices: a whole 2x2x4 slice. The times are simulated.
32 devices in a mesh: dp: 4 (over x, core), ctx: 8 (over z, y).
Axes of the slice: x: 2, y: 2, z: 4, core: 2. Of those that a mesh axis runs over, the one named last changes fastest.
Arguments:
- feats: bfloat16 [4, 1024, 12288], P('dp', 'ctx'), may hold values from -6 to 6
- short_weight: float32 [3, 12288], replicated, may hold values from -3 to 3
- grad_out: bfloat16 [4, 1024, 4096], P('dp', 'ctx'), may hold values from -6 to 6
- filt: float32 [1024, 4096], P(None, 'ctx'), may hold values from -6 to 6
Outputs:
- grad_feats: bfloat16 [4, 1024, 12288], P('dp', 'ctx')
- grad_filt: float32 [1024, 4096], P('dp', 'ctx')
All inputs are finite; a program needn't handle non-finite values.
Results may differ from a plain program's by a relative error of at most 0.0057.
Values may be sent and summed in bfloat16 or wider, within the bound.
No kernel may reach another device: no remote copies, remote signals or barrier semaphores. Data moves between devices by JAX's collectives and lax.ppermute only.
A program may use at most 128 MiB of HBM per device.

v0:
```python
import math

import jax
import jax.numpy as jnp
from jax import lax
from jax.sharding import PartitionSpec as P

full_precision = lax.Precision.HIGHEST
split_precision = lax.Precision.HIGH


def from_behind(block, axis, distance):
    devices = range(lax.axis_size(axis))
    route = [(i - distance, i) for i in devices if i - distance in devices]
    return lax.ppermute(block, axis, route)


def angle_table(count_rows, count_cols, period):
    product = (
        jnp.arange(count_rows, dtype=jnp.int32)[:, None]
        * jnp.arange(count_cols, dtype=jnp.int32)[None, :]
        % period
    )
    theta = product.astype(jnp.float32) * (2.0 * math.pi / period)
    return (jnp.cos(theta), jnp.sin(theta))


def make_tables(length):
    total = 2 * length
    outer = 128
    inner = total // outer
    half = outer // 2
    freq = jnp.arange(outer, dtype=jnp.int32)[:, None, None]
    spot = (
        jnp.arange(half, dtype=jnp.int32)[None, :, None] * inner
        + jnp.arange(inner, dtype=jnp.int32)[None, None, :]
    )
    theta = (freq * spot % total).astype(jnp.float32) * (2.0 * math.pi / total)
    first = jnp.stack([jnp.cos(theta), -jnp.sin(theta)], axis=0)
    cos_b, sin_b = angle_table(inner, inner, inner)
    forward_b = jnp.stack(
        [jnp.stack([cos_b, -sin_b], axis=1), jnp.stack([sin_b, cos_b], axis=1)], axis=0
    )
    inverse_b = jnp.stack(
        [jnp.stack([cos_b, sin_b], axis=1), jnp.stack([-sin_b, cos_b], axis=1)], axis=0
    )
    return (first, forward_b, inverse_b)


def finish_forward(partial_spec, tables, accuracy):
    return jnp.einsum("sckrb,rbxq->sckxq", partial_spec, tables[1], precision=accuracy)


def data_forward(signal, tables, accuracy):
    first = tables[0]
    inner = first.shape[3]
    seqs, chans, length = signal.shape
    grid = signal.reshape(seqs, chans, length // inner, inner)
    partial_spec = jnp.einsum("rknb,scnb->sckrb", first, grid, precision=accuracy)
    return finish_forward(partial_spec, tables, accuracy)


def filter_forward(columns, tables):
    first = tables[0]
    inner = first.shape[3]
    length, chans = columns.shape
    grid = columns.reshape(length // inner, inner, chans)
    partial_spec = jnp.einsum("rknb,nbc->ckrb", first, grid, precision=full_precision)[None]
    return finish_forward(partial_spec, tables, full_precision)


def start_inverse(spectrum, tables):
    return jnp.einsum("sckxq,xqrb->sckrb", spectrum, tables[2], precision=full_precision)


def data_inverse(spectrum, tables, length):
    partial_sig = start_inverse(spectrum, tables)
    signal = jnp.einsum("sckrb,rknb->scnb", partial_sig, tables[0], precision=full_precision)
    return signal.reshape(signal.shape[0], signal.shape[1], length) / (2.0 * length)


def filter_inverse(spectrum, tables, length):
    partial_sig = start_inverse(spectrum, tables)[0]
    signal = jnp.einsum("ckrb,rknb->nbc", partial_sig, tables[0], precision=full_precision)
    return signal.reshape(length, signal.shape[2]) / (2.0 * length)


def spectral(gated_sig, grad_sig, filter_cols, tables, length):
    g_spec = data_forward(gated_sig, tables, split_precision)
    d_spec = data_forward(grad_sig, tables, split_precision)
    h_spec = filter_forward(filter_cols, tables)
    g_re, g_im = (g_spec[:, :, :, 0], g_spec[:, :, :, 1])
    d_re, d_im = (d_spec[:, :, :, 0], d_spec[:, :, :, 1])
    h_re, h_im = (h_spec[:, :, :, 0], h_spec[:, :, :, 1])
    conv_spec = jnp.stack([h_re * g_re - h_im * g_im, h_re * g_im + h_im * g_re], axis=3)
    grad_spec = jnp.stack([h_re * d_re + h_im * d_im, h_re * d_im - h_im * d_re], axis=3)
    prod_re = jnp.sum(g_re * d_re + g_im * d_im, axis=0, keepdims=True)
    prod_im = jnp.sum(g_re * d_im - g_im * d_re, axis=0, keepdims=True)
    prod_spec = jnp.stack([prod_re, prod_im], axis=3)
    conv_out = data_inverse(conv_spec, tables, length)
    gated_grad = data_inverse(grad_spec, tables, length)
    filt_grad = filter_inverse(prod_spec, tables, length)
    return (conv_out, gated_grad, filt_grad)


def shards(feats, short_weight, grad_out, filt):
    rows = feats.shape[1]
    width = feats.shape[2] // 3
    length = filt.shape[0]
    block = filt.shape[1]
    ctx_count = lax.axis_size("ctx")
    replicas = lax.axis_size("dp")
    scale_inv = 1.0 / math.sqrt(length)
    tables = make_tables(length)
    prior = from_behind(feats[:, rows - 2 :, :], "ctx", 1)
    extended = jnp.concatenate([prior, feats], axis=1).astype(jnp.float32)
    mixed = (
        short_weight[0] * extended[:, 2:]
        + short_weight[1] * extended[:, 1 : rows + 1]
        + short_weight[2] * extended[:, :rows]
    )
    query_rows = mixed[:, :, :width]
    key_rows = mixed[:, :, width : 2 * width]
    value_rows = mixed[:, :, 2 * width :]
    gated = (key_rows * value_rows).astype(jnp.bfloat16)
    out_grad = grad_out.astype(jnp.float32)
    conv_grad = (out_grad * query_rows).astype(jnp.bfloat16)
    narrow = block // replicas

    def spread(array):
        return array[0].reshape(rows, ctx_count, replicas, narrow).transpose(1, 2, 3, 0)[:, :, None]

    wide_gated, wide_grad = (
        lax.all_to_all(
            lax.all_to_all(spread(gated), "dp", split_axis=1, concat_axis=2, tiled=True),
            "ctx",
            split_axis=0,
            concat_axis=4,
            tiled=True,
        ),
        lax.all_to_all(
            lax.all_to_all(spread(conv_grad), "dp", split_axis=1, concat_axis=2, tiled=True),
            "ctx",
            split_axis=0,
            concat_axis=4,
            tiled=True,
        ),
    )
    wide_gated = wide_gated.reshape(replicas, narrow, length)
    wide_grad = wide_grad.reshape(replicas, narrow, length)
    offset = lax.axis_index("dp") * narrow
    filt_cols = lax.dynamic_slice_in_dim(filt, offset, narrow, 1)
    conv_out, gated_grad, filt_grad = spectral(
        wide_gated, wide_grad, filt_cols * scale_inv, tables, length
    )
    back_conv, back_grad = (
        lax.all_to_all(
            lax.all_to_all(
                conv_out.astype(jnp.bfloat16)[None, None],
                "dp",
                split_axis=2,
                concat_axis=1,
                tiled=True,
            ),
            "ctx",
            split_axis=4,
            concat_axis=0,
            tiled=True,
        ),
        lax.all_to_all(
            lax.all_to_all(
                gated_grad.astype(jnp.bfloat16)[None, None],
                "dp",
                split_axis=2,
                concat_axis=1,
                tiled=True,
            ),
            "ctx",
            split_axis=4,
            concat_axis=0,
            tiled=True,
        ),
    )

    def gather_positions(array):
        return (
            array.reshape(ctx_count, replicas, narrow, rows)
            .transpose(3, 0, 1, 2)
            .reshape(1, rows, width)
        )

    conv_rows = gather_positions(back_conv)
    grad_rows = gather_positions(back_grad)
    parts = filt_grad.reshape(replicas, length // replicas, 1, narrow)
    owned = lax.all_to_all(parts, "dp", split_axis=0, concat_axis=2, tiled=True)
    filt_out = owned.reshape(length // replicas, block) * scale_inv
    grad_query = out_grad * conv_rows.astype(jnp.float32)
    grad_key = grad_rows.astype(jnp.float32) * value_rows
    grad_value = grad_rows.astype(jnp.float32) * key_rows
    grad_mixed = jnp.concatenate([grad_query, grad_key, grad_value], axis=2)
    following = from_behind(grad_mixed[:, :2, :].astype(jnp.bfloat16), "ctx", -1).astype(
        jnp.float32
    )
    ahead = jnp.concatenate([grad_mixed, following], axis=1)
    grad_in = (
        short_weight[0] * grad_mixed
        + short_weight[1] * ahead[:, 1 : rows + 1]
        + short_weight[2] * ahead[:, 2 : rows + 2]
    )
    return (grad_in.astype(jnp.bfloat16), filt_out)


def solution(mesh):
    return jax.shard_map(
        shards,
        mesh=mesh,
        in_specs=(P("dp", "ctx", None), P(), P("dp", "ctx", None), P(None, "ctx")),
        out_specs=(P("dp", "ctx", None), P("dp", "ctx")),
        check_vma=False,
    )
```

profile of v0, /device:TPU:0, one launch (start us, length us, event | category | flops | bytes accessed | tf_op | source)
XLA Modules:
  0.0 351.7 jit_solution(16861493260558920214)
XLA Ops:
  1.6 4.9 %collective-permute-start = (bf16[1,2,12288]{2,1,0:T(2,128)(2,1)S(1)}, bf16[1,2,12288]{2,1,0:T(2,128)(2,1)S(1)}, u32[]{:S(2)}, u32[]{:S(2)}) collective-permute-start(bf16[1,2,12288]{2,1,0:T(2,128)(2,1)S(1)} %slice.63), channel_id=1, source_target_pairs={{0,1},{1,2},{2,3},{3,4},{4,5},{5,6},{6,7},{8,9},{9,10},{10,11},{11... | collective-permute-start | bytes 147464 | tf_op jit(solution)/shard_map/ppermute | solution.py:15
  20.4 9.5 %fusion.21 = f32[1,128,12288]{1,2,0:T(8,128)S(1)} fusion(f32[1,130,12288]{1,2,0:T(8,128)S(1)} %maximum_convert_fusion, f32[12288]{0:T(1024)S(1)} %bitcast.222, f32[12288]{0:T(1024)S(1)} %bitcast.224, f32[12288]{0:T(1024)S(1)} %bitcast.220), kind=kLoop, calls=%fused_computation.26 | loop fusion | flops 7864320 | bytes 25313280 | tf_op jit(solution)/shard_map/add | solution.py:118
  38.2 13.4 %all-to-all-done = bf16[8,4,1,128,128]{4,3,0,2,1:T(8,128)(2,1)S(1)} async-done(((bf16[8,4,1,128,128]{4,3,0,2,1:T(8,128)(2,1)}), bf16[8,4,1,128,128]{4,3,0,2,1:T(8,128)(2,1)S(1)}, u32[]{:S(2)}, u32[]{:S(2)}) %all-to-all-start) | async-done | bytes 1048608 | tf_op jit(solution)/shard_map/all_to_all | solution.py:135
  58.3 12.1 %all-to-all-done.4 = bf16[8,4,1,128,128]{4,3,0,2,1:T(8,128)(2,1)S(1)} async-done(((bf16[8,4,1,128,128]{4,3,0,2,1:T(8,128)(2,1)}), bf16[8,4,1,128,128]{4,3,0,2,1:T(8,128)(2,1)S(1)}, u32[]{:S(2)}, u32[]{:S(2)}) %all-to-all-start.4) | async-done | bytes 1048608 | tf_op jit(solution)/shard_map/all_to_all | solution.py:142
  70.5 4.9 %all-to-all-start.1 = ((bf16[8,1,4,128,128]{4,3,2,1,0:T(8,128)(2,1)}), bf16[8,1,4,128,128]{4,3,2,1,0:T(8,128)(2,1)S(1)}, u32[]{:S(2)}, u32[]{:S(2)}) async-start(bf16[8,1,4,128,128]{4,3,2,1,0:T(8,128)(2,1)} %copy.69), calls=%async_computation.1 | async-start | bytes 2097152 | tf_op jit(solution)/shard_map/all_to_all | solution.py:134
  78.4 22.6 %all-to-all-done.1 = bf16[8,1,4,128,128]{4,3,2,1,0:T(8,128)(2,1)S(1)} async-done(((bf16[8,1,4,128,128]{4,3,2,1,0:T(8,128)(2,1)}), bf16[8,1,4,128,128]{4,3,2,1,0:T(8,128)(2,1)S(1)}, u32[]{:S(2)}, u32[]{:S(2)}) %all-to-all-start.1) | async-done | bytes 1048608 | tf_op jit(solution)/shard_map/all_to_all | solution.py:134
  101.0 4.4 %all-to-all-start.5 = ((bf16[8,1,4,128,128]{4,3,2,1,0:T(8,128)(2,1)}), bf16[8,1,4,128,128]{4,3,2,1,0:T(8,128)(2,1)}, u32[]{:S(2)}, u32[]{:S(2)}) async-start(bf16[8,1,4,128,128]{4,3,2,1,0:T(8,128)(2,1)} %copy.81), calls=%async_computation.5 | async-start | bytes 2097152 | tf_op jit(solution)/shard_map/all_to_all | solution.py:141
  119.6 9.9 %fusion.23 = f32[4,128,128,2,16]{2,4,3,1,0:T(8,128)} fusion(f32[4,128,128,2,16,1]{2,1,3,0,4,5:T(8,128)S(1)} %convolution_bitcast_fusion.1, f32[1,16,2,16]{1,3,0,2:T(8,128)S(1)} %get-tuple-element.28, f32[1,16,2,16]{1,3,0,2:T(8,128)S(1)} %get-tuple-element.31), kind=kOutput, calls=%fused_computation.40 | convolution fusion | flops 402654208 | bytes 16781312 | tf_op jit(solution)/shard_map/sckrb,rbxq->sckxq/dot_general | solution.py:51
  135.2 9.8 %fusion.26 = f32[4,128,128,2,16]{2,4,3,1,0:T(8,128)} fusion(f32[4,128,128,2,16,1]{2,1,3,0,4,5:T(8,128)S(1)} %convolution_bitcast_fusion, f32[1,16,2,16]{1,3,0,2:T(8,128)S(1)} %get-tuple-element.28, f32[1,16,2,16]{1,3,0,2:T(8,128)S(1)} %get-tuple-element.31), kind=kOutput, calls=%fused_computation.41 | convolution fusion | flops 402654208 | bytes 16781312 | tf_op jit(solution)/shard_map/sckrb,rbxq->sckxq/dot_general | solution.py:51
  145.1 10.1 %add_reduce_fusion = (f32[128,128,16]{1,2,0:T(8,128)S(1)}, f32[128,128,16]{1,2,0:T(8,128)S(1)}, f32[4,128,128,1,16]{2,4,3,1,0:T(8,128)}, f32[4,128,128,1,16]{2,4...) fusion(f32[4,128,128,2,16]{2,4,3,1,0:T(8,128)} %fusion.26, ...), kind=kLoop, calls=%fused_computation.33 | loop fusion | flops 20447232 | bytes 37748736 | tf_op jit(solution)/shard_map/reduce_sum | solution.py:97
  165.8 9.9 %fusion.32 = f32[4,128,128,2,16]{2,4,3,1,0:T(8,128)S(1)} fusion(f32[4,128,128,1,16]{2,4,3,1,0:T(8,128)} %get-tuple-element.16, f32[4,128,128,1,16]{2,4,3,1,0:T(8,128)} %get-tuple-element.17, f32[1,16,2,16]{1,3,2,0:T(8,128)S(1)} %get-tuple-element.32, f32[1,16,2,16]{1,3,2,0:T(8,128)S(1)} %get-tuple-element.27), kind=kOutput, calls=%fused_computation.43 | convolution fusion | flops 807404544 | bytes 16781312 | tf_op jit(solution)/shard_map/sckxq,xqrb->sckrb/dot_general | solution.py:73
  175.7 13.1 %fusion.56 = bf16[4,128,64,16]{1,2,0,3:T(8,128)(2,1)S(1)} fusion(f32[4,128,128,2,16]{2,4,3,1,0:T(8,128)S(1)} %fusion.32, f32[1,128,64,16]{1,2,0,3:T(8,128)S(1)} %get-tuple-element.34, f32[1,128,64,16]{1,2,0,3:T(8,128)S(1)} %get-tuple-element.33), kind=kOutput, calls=%fused_computation.68 | convolution fusion | flops 1611923456 | bytes 10485760 | tf_op jit(solution)/shard_map/sckrb,rknb->scnb/dot_general | solution.py:78
  195.1 9.7 %fusion.29 = f32[4,128,128,2,16]{2,4,3,1,0:T(8,128)S(1)} fusion(f32[4,128,128,1,16]{2,4,3,1,0:T(8,128)} %get-tuple-element.14, f32[4,128,128,1,16]{2,4,3,1,0:T(8,128)} %get-tuple-element.15, f32[1,16,2,16]{1,3,2,0:T(8,128)S(1)} %get-tuple-element.32, f32[1,16,2,16]{1,3,2,0:T(8,128)S(1)} %get-tuple-element.27), kind=kOutput, calls=%fused_computation.42 | convolution fusion | flops 807404544 | bytes 16781312 | tf_op jit(solution)/shard_map/sckxq,xqrb->sckrb/dot_general | solution.py:73
  204.8 13.1 %fusion.53 = bf16[4,128,64,16]{1,2,0,3:T(8,128)(2,1)S(1)} fusion(f32[4,128,128,2,16]{2,4,3,1,0:T(8,128)S(1)} %fusion.29, f32[1,128,64,16]{1,2,0,3:T(8,128)S(1)} %get-tuple-element.34, f32[1,128,64,16]{1,2,0,3:T(8,128)S(1)} %get-tuple-element.33), kind=kOutput, calls=%fused_computation.67 | convolution fusion | flops 1611923456 | bytes 10485760 | tf_op jit(solution)/shard_map/sckrb,rknb->scnb/dot_general | solution.py:78
  226.2 11.4 %all-to-all-done.2 = bf16[1,1,4,128,1024]{3,4,1,0,2:T(8,128)(2,1)S(1)} async-done(((bf16[1,1,4,128,1024]{3,4,1,0,2:T(8,128)(2,1)}), bf16[1,1,4,128,1024]{3,4,1,0,2:T(8,128)(2,1)S(1)}, u32[]{:S(2)}, u32[]{:S(2)}) %all-to-all-start.2) | async-done | bytes 1048608 | tf_op jit(solution)/shard_map/all_to_all | solution.py:158
  237.6 4.6 %all-to-all-start.7 = ((bf16[1,4,1,128,1024]{3,1,2,0,4:T(4,128)(2,1)}), bf16[1,4,1,128,1024]{3,1,2,0,4:T(4,128)(2,1)S(1)}, u32[]{:S(2)}, u32[]{:S(2)}) async-start(bf16[1,4,1,128,1024]{3,1,2,0,4:T(4,128)(2,1)} %copy.89), calls=%async_computation.7 | async-start | bytes 2097152 | tf_op jit(solution)/shard_map/all_to_all | solution.py:170
  244.0 23.9 %all-to-all-done.7 = bf16[1,4,1,128,1024]{3,1,2,0,4:T(4,128)(2,1)S(1)} async-done(((bf16[1,4,1,128,1024]{3,1,2,0,4:T(4,128)(2,1)}), bf16[1,4,1,128,1024]{3,1,2,0,4:T(4,128)(2,1)S(1)}, u32[]{:S(2)}, u32[]{:S(2)}) %all-to-all-start.7) | async-done | bytes 1048608 | tf_op jit(solution)/shard_map/all_to_all | solution.py:170
  267.9 4.2 %all-to-all-start.3 = ((bf16[1,4,1,128,1024]{3,1,2,0,4:T(4,128)(2,1)}), bf16[1,4,1,128,1024]{3,1,2,0,4:T(4,128)(2,1)}, u32[]{:S(2)}, u32[]{:S(2)}) async-start(bf16[1,4,1,128,1024]{3,1,2,0,4:T(4,128)(2,1)} %copy.77), calls=%async_computation.3 | async-start | bytes 2097152 | tf_op jit(solution)/shard_map/all_to_all | solution.py:157
  276.4 4.6 %slice_multiply_fusion.5 = (f32[1,128,4096]{1,2,0:T(8,128)S(1)}, f32[1,128,4096]{1,2,0:T(8,128)}) fusion(f32[1,128,4096]{1,2,0:T(8,128)} %bitcast.204, f32[1,128,12288]{1,2,0:T(8,128)} %copy-done), kind=kLoop, calls=%fused_computation.62 | loop fusion | flops 1048576 | bytes 10485760 | tf_op jit(solution)/shard_map/mul | solution.py:198
  281.0 16.7 %all-to-all-done.3 = bf16[1,4,1,128,1024]{3,1,2,0,4:T(4,128)(2,1)} async-done(((bf16[1,4,1,128,1024]{3,1,2,0,4:T(4,128)(2,1)}), bf16[1,4,1,128,1024]{3,1,2,0,4:T(4,128)(2,1)}, u32[]{:S(2)}, u32[]{:S(2)}) %all-to-all-start.3) | async-done | bytes 1048608 | tf_op jit(solution)/shard_map/all_to_all | solution.py:157
  305.7 6.7 %pad_maximum_fusion.1 = bf16[1,128,12288]{1,2,0:T(8,128)(2,1)} fusion(f32[1,128,4096]{1,2,0:T(8,128)S(1)} %copy-done.1, f32[1,128,4096]{1,2,0:T(8,128)S(1)} %get-tuple-element.18, f32[1,128,4096]{1,2,0:T(8,128)S(1)} %convert_multiply_fusion.1), kind=kLoop, calls=%fused_computation.31 | loop fusion | flops 9437184 | bytes 9437184 | tf_op jit(solution)/shard_map/concatenate | solution.py:200
  325.2 7.3 %pad_maximum_fusion = f32[1,130,12288]{1,2,0:T(8,128)S(1)} fusion(f32[1,2,12288]{1,2,0:T(8,128)} %copy.93, f32[1,128,4096]{1,2,0:T(8,128)} %get-tuple-element.19, f32[1,128,4096]{1,2,0:T(8,128)S(1)} %get-tuple-element.18, f32[1,128,4096]{1,2,0:T(8,128)} %copy-done.3), kind=kLoop, calls=%fused_computation | loop fusion | flops 4792320 | bytes 12779520 | tf_op jit(solution)/shard_map/concatenate | solution.py:204
  332.5 14.3 %fusion.19 = bf16[1,128,12288]{1,2,0:T(8,128)(2,1)} fusion(f32[1,130,12288]{1,2,0:T(8,128)S(1)} %pad_maximum_fusion, f32[12288]{0:T(1024)S(1)} %bitcast.223, f32[12288]{0:T(1024)S(1)} %bitcast.225, f32[12288]{0:T(1024)S(1)} %bitcast.221, f32[1,128,4096]{1,2,0:T(8,128)S(1)} %copy-done.2, f32[1,128,4096]{1,2,0:T(8,128)S(1)} %get-tuple-element.18, ...), kind=kLoop, calls=%fused_computation.21 | loop fusion | flops 12582912 | bytes 22167552 | tf_op jit(solution)/shard_map/convert_element_type | solution.py:210
  346.8 4.6 %copy.99 = bf16[1,128,12288]{2,1,0:T(8,128)(2,1)} copy(bf16[1,128,12288]{1,2,0:T(8,128)(2,1)} %fusion.19) | data formatting | bytes 6291456
  (82 shorter events, 104.6 us)
Async XLA Ops:
  1.6 11.9 %collective-permute-start = (bf16[1,2,12288]{2,1,0:T(2,128)(2,1)S(1)}, bf16[1,2,12288]{2,1,0:T(2,128)(2,1)S(1)}, u32[]{:S(2)}, u32[]{:S(2)}) collective-permute-start(bf16[1,2,12288]{2,1,0:T(2,128)(2,1)S(1)} %slice.63), channel_id=1, source_target_pairs={{0,1},{1,2},{2,3},{3,4},{4,5},{5,6},{6,7},{8,9},{9,10},{10,11},{11... | collective-permute-start | bytes 147464 | tf_op jit(solution)/shard_map/ppermute | solution.py:15
  20.3 9.6 %copy-start.5 = (bf16[1,128,4096]{1,2,0:T(8,128)(2,1)S(1)}, bf16[1,128,4096]{1,2,0:T(8,128)(2,1)}, u32[]{:S(2)}) copy-start(bf16[1,128,4096]{1,2,0:T(8,128)(2,1)} %copy.62) | copy-start | bytes 3145732
  29.9 2.6 copy-start
  33.6 18.0 %all-to-all-start = ((bf16[8,4,1,128,128]{4,3,0,2,1:T(8,128)(2,1)}), bf16[8,4,1,128,128]{4,3,0,2,1:T(8,128)(2,1)S(1)}, u32[]{:S(2)}, u32[]{:S(2)}) async-start(bf16[8,4,1,128,128]{4,3,0,2,1:T(8,128)(2,1)} %copy.68), calls=%async_computation | async-start | bytes 2097152 | tf_op jit(solution)/shard_map/all_to_all | solution.py:135
  51.5 1.0 copy-start.9
  52.5 18.0 %all-to-all-start.4 = ((bf16[8,4,1,128,128]{4,3,0,2,1:T(8,128)(2,1)}), bf16[8,4,1,128,128]{4,3,0,2,1:T(8,128)(2,1)S(1)}, u32[]{:S(2)}, u32[]{:S(2)}) async-start(bf16[8,4,1,128,128]{4,3,0,2,1:T(8,128)(2,1)} %copy.80), calls=%async_computation.4 | async-start | bytes 2097152 | tf_op jit(solution)/shard_map/all_to_all | solution.py:142
  70.5 30.5 %all-to-all-start.1 = ((bf16[8,1,4,128,128]{4,3,2,1,0:T(8,128)(2,1)}), bf16[8,1,4,128,128]{4,3,2,1,0:T(8,128)(2,1)S(1)}, u32[]{:S(2)}, u32[]{:S(2)}) async-start(bf16[8,1,4,128,128]{4,3,2,1,0:T(8,128)(2,1)} %copy.69), calls=%async_computation.1 | async-start | bytes 2097152 | tf_op jit(solution)/shard_map/all_to_all | solution.py:134
  101.0 4.4 %copy-start.6 = (bf16[8,1,4,128,128]{4,3,2,1,0:T(8,128)(2,1)}, bf16[8,1,4,128,128]{4,3,2,1,0:T(8,128)(2,1)S(1)}, u32[]{:S(2)}) copy-start(bf16[8,1,4,128,128]{4,3,2,1,0:T(8,128)(2,1)S(1)} %all-to-all-done.1) | copy-start | bytes 3145732
  101.0 29.9 %all-to-all-start.5 = ((bf16[8,1,4,128,128]{4,3,2,1,0:T(8,128)(2,1)}), bf16[8,1,4,128,128]{4,3,2,1,0:T(8,128)(2,1)}, u32[]{:S(2)}, u32[]{:S(2)}) async-start(bf16[8,1,4,128,128]{4,3,2,1,0:T(8,128)(2,1)} %copy.81), calls=%async_computation.5 | async-start | bytes 2097152 | tf_op jit(solution)/shard_map/all_to_all | solution.py:141
  132.6 12.5 %slice-start = ((s8[8388608]{0:T(1024)(128)(4,1)}), s8[4194304]{0:T(1024)(128)(4,1)S(1)}, s32[]{:S(2)}) async-start(s8[8388608]{0:T(1024)(128)(4,1)} %bitcast.201), calls=%async_computation.9 | async-start | bytes 8388608
  135.2 9.9 %slice-start.1 = ((s8[8388608]{0:T(1024)(128)(4,1)}), s8[4194304]{0:T(1024)(128)(4,1)S(1)}, s32[]{:S(2)}) async-start(s8[8388608]{0:T(1024)(128)(4,1)} %bitcast.201), calls=%async_computation.10 | async-start | bytes 8388608
  135.2 9.9 %copy-start.7 = (f32[128,128,16]{1,2,0:T(8,128)S(1)}, f32[128,128,16]{1,2,0:T(8,128)}, u32[]{:S(2)}) copy-start(f32[128,128,16]{1,2,0:T(8,128)} %get-tuple-element.22) | copy-start | bytes 3145732
  135.2 9.9 %copy-start.8 = (f32[128,128,16]{1,2,0:T(8,128)S(1)}, f32[128,128,16]{1,2,0:T(8,128)}, u32[]{:S(2)}) copy-start(f32[128,128,16]{1,2,0:T(8,128)} %get-tuple-element.23) | copy-start | bytes 3145732
  161.6 29.2 %all-to-all-start.8 = ((f32[4,256,1,128]{3,1,2,0:T(8,128)}), f32[4,256,1,128]{3,1,2,0:T(8,128)}, u32[]{:S(2)}, u32[]{:S(2)}) async-start(f32[4,256,1,128]{3,1,2,0:T(8,128)} %bitcast.92), calls=%async_computation.8 | async-start | bytes 1048576 | tf_op jit(solution)/shard_map/all_to_all | solution.py:195
  190.8 28.9 %all-to-all-start.6 = ((bf16[1,1,4,128,1024]{3,4,1,0,2:T(8,128)(2,1)}), bf16[1,1,4,128,1024]{3,4,1,0,2:T(8,128)(2,1)}, u32[]{:S(2)}, u32[]{:S(2)}) async-start(bf16[1,1,4,128,1024]{3,4,1,0,2:T(8,128)(2,1)} %bitcast.213), calls=%async_computation.6 | async-start | bytes 2097152 | tf_op jit(solution)/shard_map/all_to_all | solution.py:171
  219.7 18.0 %all-to-all-start.2 = ((bf16[1,1,4,128,1024]{3,4,1,0,2:T(8,128)(2,1)}), bf16[1,1,4,128,1024]{3,4,1,0,2:T(8,128)(2,1)S(1)}, u32[]{:S(2)}, u32[]{:S(2)}) async-start(bf16[1,1,4,128,1024]{3,4,1,0,2:T(8,128)(2,1)} %bitcast.44), calls=%async_computation.2 | async-start | bytes 2097152 | tf_op jit(solution)/shard_map/all_to_all | solution.py:158
  237.6 30.2 %all-to-all-start.7 = ((bf16[1,4,1,128,1024]{3,1,2,0,4:T(4,128)(2,1)}), bf16[1,4,1,128,1024]{3,1,2,0,4:T(4,128)(2,1)S(1)}, u32[]{:S(2)}, u32[]{:S(2)}) async-start(bf16[1,4,1,128,1024]{3,1,2,0,4:T(4,128)(2,1)} %copy.89), calls=%async_computation.7 | async-start | bytes 2097152 | tf_op jit(solution)/shard_map/all_to_all | solution.py:170
  267.9 29.8 %all-to-all-start.3 = ((bf16[1,4,1,128,1024]{3,1,2,0,4:T(4,128)(2,1)}), bf16[1,4,1,128,1024]{3,1,2,0,4:T(4,128)(2,1)}, u32[]{:S(2)}, u32[]{:S(2)}) async-start(bf16[1,4,1,128,1024]{3,1,2,0,4:T(4,128)(2,1)} %copy.77), calls=%async_computation.3 | async-start | bytes 2097152 | tf_op jit(solution)/shard_map/all_to_all | solution.py:157
  303.5 2.2 copy-start.1
  305.4 7.0 %copy-start.3 = (f32[1,128,4096]{1,2,0:T(8,128)}, f32[1,128,4096]{1,2,0:T(8,128)S(1)}, u32[]{:S(2)}) copy-start(f32[1,128,4096]{1,2,0:T(8,128)S(1)} %convert_multiply_fusion.1) | copy-start | bytes 6291460
  305.7 11.2 %copy-start.10 = (f32[4,256,1,128]{1,3,0,2:T(8,128)S(1)}, f32[4,256,1,128]{1,3,0,2:T(8,128)}, u32[]{:S(2)}) copy-start(f32[4,256,1,128]{1,3,0,2:T(8,128)} %copy.98) | copy-start | bytes 1572868
  315.6 6.0 %collective-permute-start.1 = (bf16[1,2,12288]{2,1,0:T(2,128)(2,1)S(1)}, bf16[1,2,12288]{2,1,0:T(2,128)(2,1)S(1)}, u32[]{:S(2)}, u32[]{:S(2)}) collective-permute-start(bf16[1,2,12288]{2,1,0:T(2,128)(2,1)S(1)} %copy.92), channel_id=1, source_target_pairs={{1,0},{2,1},{3,2},{4,3},{5,4},{6,5},{7,6},{9,8},{10,9},{11,10},{12... | collective-permute-start | bytes 147464 | tf_op jit(solution)/shard_map/ppermute | solution.py:15
  325.2 7.3 %copy-start.2 = (f32[1,128,4096]{1,2,0:T(8,128)S(1)}, f32[1,128,4096]{1,2,0:T(8,128)}, u32[]{:S(2)}) copy-start(f32[1,128,4096]{1,2,0:T(8,128)} %get-tuple-element.19) | copy-start | bytes 6291460
  325.2 7.3 %copy-start.4 = (f32[1,128,4096]{1,2,0:T(8,128)S(1)}, f32[1,128,4096]{1,2,0:T(8,128)}, u32[]{:S(2)}) copy-start(f32[1,128,4096]{1,2,0:T(8,128)} %copy-done.3) | copy-start | bytes 6291460
where the time goes:
time: 356 us; the launch traced here: 352 us
  waiting for transfers between devices  105 us (29%)
  matrix products  82.3 us (23%)
  other arithmetic  65 us (18%)
  local copies, waits for them, and re-layouts  54.9 us (15%)
  starting transfers between devices  43.2 us (12%)
    dot_general x2, matrix products, data_inverse(): jnp.einsum('sckrb,rknb->scnb', partial_sig, tables[0], precision=full_pre...  26.2 us
    all_to_all x1, waiting for transfers between devices, shards(): lax.all_to_all(lax.all_to_all(gated_grad.astype(jnp.bfloat16)[None, None]...  23.9 us
    dot_general x3, matrix products, finish_forward(): jnp.einsum('sckrb,rbxq->sckxq', partial_spec, tables[1], precision=accuracy)  23 us
    all_to_all x1, waiting for transfers between devices, shards(): lax.all_to_all(lax.all_to_all(spread(gated), 'dp', split_axis=1, concat_a...  22.6 us
    dot_general x3, matrix products, start_inverse(): jnp.einsum('sckxq,xqrb->sckrb', spectrum, tables[2], precision=full_preci...  21.5 us
    all_to_all x1, waiting for transfers between devices, shards(): lax.all_to_all(lax.all_to_all(conv_out.astype(jnp.bfloat16)[None, None],...  16.7 us
    unnamed x30, local copies, waits for them, and re-layouts  14.8 us
    convert_element_type x1, other arithmetic, shards(): return (grad_in.astype(jnp.bfloat16), filt_out)  14.3 us
  transfers between devices with their start and end apart: 11, of which 8 were waited for; matrix products, arithmetic and copies ran while one was open for 29% of the time, Pallas kernels for 0%

commit v1 on v0

--- a/solution.py
+++ b/solution.py
@@ -1,9 +1,383 @@
+import functools
 import math
 
 import jax
 import jax.numpy as jnp
+import numpy as np
 from jax import lax
+from jax.experimental import pallas as pl
+from jax.experimental.pallas import tpu as pltpu
 from jax.sharding import PartitionSpec as P
+
+CHUNKS = 2
+EXTRA = 8
+TILE = 256
+VMEM_LIMIT = 48 * 1024 * 1024
+
+
+def odd_tables(length):
+    freq = 2 * np.arange(length, dtype=np.int64)[:, None] + 1
+    spot = np.arange(length, dtype=np.int64)[None, :]
+    theta = (freq * spot % (4 * length)).astype(np.float64) * (2.0 * math.pi / (4 * length))
+    full = np.concatenate([np.cos(theta), -np.sin(theta)], axis=0).astype(np.float32)
+    high = full.astype(jnp.bfloat16)
+    low = (full - high.astype(np.float32)).astype(jnp.bfloat16)
+    return high, low
+
+
+def conv_rows(values, before, taps):
+    rows = values.shape[0]
+    ext = jnp.concatenate([before, values], axis=0)
+    off = ext.shape[0] - rows
+    return (
+        taps[0:1] * values
+        + taps[1:2] * ext[off - 1 : off - 1 + rows]
+        + taps[2:3] * ext[off - 2 : off - 2 + rows]
+    )
+
+
+def gate_kernel(count, me_ref, q_ref, k_ref, v_ref, bq_ref, bk_ref, bv_ref, tq_ref, tk_ref, tv_ref, go_ref, *outs):
+    step = pl.program_id(0)
+
+    def mixed(x_ref, b_ref, t_ref):
+        return conv_rows(x_ref[...].astype(jnp.float32), b_ref[...].astype(jnp.float32), t_ref[...])
+
+    query = mixed(q_ref, bq_ref, tq_ref)
+    key = mixed(k_ref, bk_ref, tk_ref)
+    value = mixed(v_ref, bv_ref, tv_ref)
+    gated = (key * value).astype(jnp.bfloat16)
+    grad = (go_ref[...].astype(jnp.float32) * query).astype(jnp.bfloat16)
+    both = jnp.concatenate([gated, grad], axis=1)
+    for j in range(count):
+
+        @pl.when(step == j)
+        def _(j=j):
+            outs[j][...] = both
+
+
+def gate(me, feats, before, taps, grad_out, chunk, chunks, count, cols):
+    rows = feats.shape[0]
+    parts = count * chunks
+
+    def at(region):
+        return lambda k, m: (0, region * parts + (m[0] ^ k) * chunks + chunk)
+
+    spec = pltpu.PrefetchScalarGridSpec(
+        num_scalar_prefetch=1,
+        grid=(count,),
+        in_specs=[pl.BlockSpec((rows, cols), at(r)) for r in range(3)]
+        + [pl.BlockSpec((before.shape[0], cols), at(r)) for r in range(3)]
+        + [pl.BlockSpec((3, cols), at(r)) for r in range(3)]
+        + [pl.BlockSpec((rows, cols), at(0))],
+        out_specs=[pl.BlockSpec((rows, 2 * cols), lambda k, m: (0, 0))] * count,
+    )
+    return pl.pallas_call(
+        functools.partial(gate_kernel, count),
+        grid_spec=spec,
+        out_shape=[jax.ShapeDtypeStruct((rows, 2 * cols), jnp.bfloat16)] * count,
+        compiler_params=pltpu.CompilerParams(vmem_limit_bytes=VMEM_LIMIT),
+        cost_estimate=pl.CostEstimate(
+            flops=20 * rows * cols * count, bytes_accessed=12 * rows * cols * count, transcendentals=0
+        ),
+        name=f"gate{chunk}",
+    )(me, feats, feats, feats, before, before, before, taps, taps, taps, grad_out)
+
+
+def filter_kernel(scale, filt_ref, high_ref, low_ref, out_ref):
+    now = filt_ref[...] * scale
+    high = now.astype(jnp.bfloat16)
+    low = (now - high.astype(jnp.float32)).astype(jnp.bfloat16)
+
+    def dot(a, b):
+        return jnp.dot(a, b, preferred_element_type=jnp.float32)
+
+    out_ref[...] = dot(high_ref[...], high) + dot(high_ref[...], low) + dot(low_ref[...], high)
+
+
+def filter_spectrum(filt, high, low, scale):
+    length, cols = filt.shape
+    rows = high.shape[0]
+    return pl.pallas_call(
+        functools.partial(filter_kernel, scale),
+        grid=(rows // TILE,),
+        in_specs=[
+            pl.BlockSpec((length, cols), lambda i: (0, 0)),
+            pl.BlockSpec((TILE, length), lambda i: (i, 0)),
+            pl.BlockSpec((TILE, length), lambda i: (i, 0)),
+        ],
+        out_specs=pl.BlockSpec((TILE, cols), lambda i: (i, 0)),
+        out_shape=jax.ShapeDtypeStruct((rows, cols), jnp.float32),
+        compiler_params=pltpu.CompilerParams(vmem_limit_bytes=VMEM_LIMIT),
+        cost_estimate=pl.CostEstimate(
+            flops=6 * rows * length * cols,
+            bytes_accessed=4 * length * cols + 4 * rows * length + 4 * rows * cols,
+            transcendentals=0,
+        ),
+        name="filter_spectrum",
+    )(filt, high, low)
+
+
+def spectral_kernel(count, rows, scale, me_ref, spec_ref, forward_ref, inverse_ref, *rest):
+    pieces = rest[:count]
+    outs = rest[count : 2 * count]
+    corr_send, corr_keep = rest[2 * count : 2 * count + 2]
+    data, fwd, inv, prod, res, corr, piece_sem, fwd_sem, inv_sem = rest[2 * count + 2 :]
+    me = me_ref[0]
+    core = me_ref[1]
+    length = data.shape[0]
+    cols = data.shape[1] // 2
+
+    def piece_copy(j):
+        place = pl.multiple_of((me ^ j) * rows, rows)
+        return pltpu.make_async_copy(pieces[j], data.at[pl.ds(place, rows)], piece_sem.at[j])
+
+    fwd_copy = pltpu.make_async_copy(forward_ref, fwd, fwd_sem)
+    inv_copy = pltpu.make_async_copy(inverse_ref, inv, inv_sem)
+    for j in range(count):
+        piece_copy(j).start()
+    fwd_copy.start()
+    inv_copy.start()
+    for j in range(count):
+        piece_copy(j).wait()
+    fwd_copy.wait()
+
+    def forward(i, carry):
+        low = pl.ds(pl.multiple_of(i * TILE, TILE), TILE)
+        high = pl.ds(pl.multiple_of(length + i * TILE, TILE), TILE)
+        re = jnp.dot(fwd[low, :], data[...], preferred_element_type=jnp.float32)
+        im = jnp.dot(fwd[high, :], data[...], preferred_element_type=jnp.float32)
+        g_re, d_re = re[:, :cols], re[:, cols:]
+        g_im, d_im = im[:, :cols], im[:, cols:]
+        h_re, h_im = spec_ref[low, :], spec_ref[high, :]
+        prod[low, :cols] = (h_re * g_re - h_im * g_im).astype(jnp.bfloat16)
+        prod[high, :cols] = (h_re * g_im + h_im * g_re).astype(jnp.bfloat16)
+        prod[low, cols : 2 * cols] = (h_re * d_re + h_im * d_im).astype(jnp.bfloat16)
+        prod[high, cols : 2 * cols] = (h_re * d_im - h_im * d_re).astype(jnp.bfloat16)
+        prod[low, 2 * cols :] = (g_re * d_re + g_im * d_im).astype(jnp.bfloat16)
+        prod[high, 2 * cols :] = (g_re * d_im - g_im * d_re).astype(jnp.bfloat16)
+        return carry
+
+    lax.fori_loop(0, length // TILE, forward, 0)
+    inv_copy.wait()
+
+    def inverse(i, carry):
+        here = pl.ds(pl.multiple_of(i * TILE, TILE), TILE)
+        out = jnp.dot(inv[here, :], prod[...], preferred_element_type=jnp.float32)
+        res[here, :] = out[:, : 2 * cols].astype(jnp.bfloat16)
+        corr[here, :] = out[:, 2 * cols :] * scale
+        return carry
+
+    lax.fori_loop(0, length // TILE, inverse, 0)
+    res[length:, :] = jnp.zeros((res.shape[0] - length, 2 * cols), jnp.bfloat16)
+    for j in range(count):
+        place = pl.multiple_of((me ^ j) * rows, rows)
+        outs[j][:rows, :] = res[pl.ds(place, rows), :]
+        outs[j][rows:, :] = res[pl.ds(place + rows, 16), :][:EXTRA]
+    half = corr_send.shape[0] // 2
+    for x in range(2):
+        corr_keep[x * half : (x + 1) * half, :] = corr[
+            pl.ds(pl.multiple_of((2 * x + core) * half, half), half), :
+        ]
+        corr_send[x * half : (x + 1) * half, :] = corr[
+            pl.ds(pl.multiple_of((2 * x + 1 - core) * half, half), half), :
+        ]
+
+
+def spectral(place, spectrum, forward, inverse, pieces, chunk, scale):
+    count = len(pieces)
+    rows, width = pieces[0].shape
+    cols = width // 2
+    length = count * rows
+    vmem = pl.BlockSpec(memory_space=pltpu.VMEM)
+    return pl.pallas_call(
+        functools.partial(spectral_kernel, count, rows, scale),
+        grid=(1,),
+        in_specs=[
+            pl.BlockSpec(memory_space=pltpu.SMEM),
+            pl.BlockSpec((2 * length, cols), lambda i: (0, chunk)),
+        ]
+        + [pl.BlockSpec(memory_space=pl.ANY)] * (2 + count),
+        out_specs=[vmem] * (count + 2),
+        out_shape=[jax.ShapeDtypeStruct((rows + EXTRA, width), jnp.bfloat16)] * count
+        + [jax.ShapeDtypeStruct((length // 2, cols), jnp.float32)] * 2,
+        scratch_shapes=[
+            pltpu.VMEM((length, width), jnp.bfloat16),
+            pltpu.VMEM((2 * length, length), jnp.bfloat16),
+            pltpu.VMEM((length, 2 * length), jnp.bfloat16),
+            pltpu.VMEM((2 * length, 3 * cols), jnp.bfloat16),
+            pltpu.VMEM((length + 16, width), jnp.bfloat16),
+            pltpu.VMEM((length, cols), jnp.float32),
+            pltpu.SemaphoreType.DMA((count,)),
+            pltpu.SemaphoreType.DMA,
+            pltpu.SemaphoreType.DMA,
+        ],
+        compiler_params=pltpu.CompilerParams(vmem_limit_bytes=VMEM_LIMIT),
+        cost_estimate=pl.CostEstimate(
+            flops=20 * length * length * cols,
+            bytes_accessed=8 * length * length + 20 * length * cols,
+            transcendentals=0,
+        ),
+        name=f"spectral{chunk}",
+    )(place, spectrum, forward, inverse, *pieces)
+
+
+def final_kernel(count, cols, width, chunk, chunks, aliased, *refs):
+    me_ref = refs[0]
+    k_ref, v_ref, bk_ref, bv_ref, ak_ref, av_ref, go_ref, ag_ref, tq_ref, tk_ref, tv_ref = refs[1:12]
+    pieces = refs[12 : 12 + count]
+    refs = refs[12 + count + (1 if aliased else 0) :]
+    out_ref, back, stage, in_sem, out_sem = refs
+    step = pl.program_id(0)
+    me = me_ref[0]
+    rows = k_ref.shape[0]
+
+    def in_copy(j):
+        return pltpu.make_async_copy(pieces[j], back.at[j], in_sem.at[j])
+
+    @pl.when(step == 0)
+    def _():
+        for j in range(count):
+            in_copy(j).start()
+
+    def out_copy(j, region):
+        col = pl.multiple_of(region * width + ((me ^ j) * chunks + chunk) * cols, cols)
+        return pltpu.make_async_copy(
+            stage.at[j, region], out_ref.at[:, pl.ds(col, cols)], out_sem.at[j, region]
+        )
+
+    def wide(x_ref, b_ref, a_ref):
+        return jnp.concatenate(
+            [b_ref[...], x_ref[...], a_ref[...], jnp.zeros((EXTRA - 2, cols), jnp.bfloat16)], axis=0
+        ).astype(jnp.float32)
+
+    def mixed(ext, taps):
+        n = rows + EXTRA
+        return taps[0:1] * ext[2 : n + 2] + taps[1:2] * ext[1 : n + 1] + taps[2:3] * ext[:n]
+
+    def unmixed(dz, taps):
+        return (
+            taps[0:1] * dz[:rows] + taps[1:2] * dz[1 : rows + 1] + taps[2:3] * dz[2 : rows + 2]
+        ).astype(jnp.bfloat16)
+
+    key = mixed(wide(k_ref, bk_ref, ak_ref), tk_ref[...])
+    value = mixed(wide(v_ref, bv_ref, av_ref), tv_ref[...])
+    cotan = jnp.concatenate(
+        [go_ref[...], ag_ref[...], jnp.zeros((EXTRA - 2, cols), jnp.bfloat16)], axis=0
+    ).astype(jnp.float32)
+    for j in range(count):
+
+        @pl.when(step == j)
+        def _(j=j):
+            in_copy(j).wait()
+
+    both = back[step].astype(jnp.float32)
+    conv, grad = both[:, :cols], both[:, cols:]
+    stage[step, 0] = unmixed(cotan * conv, tq_ref[...])
+    stage[step, 1] = unmixed(grad * value, tk_ref[...])
+    stage[step, 2] = unmixed(grad * key, tv_ref[...])
+    for region in range(3):
+        out_copy(step, region).start()
+
+    @pl.when(step == count - 1)
+    def _():
+        for j in range(count):
+            for region in range(3):
+                out_copy(j, region).wait()
+
+
+def final(me, feats, before, after, grad_out, after_out, taps, pieces, so_far, chunk, chunks):
+    count = len(pieces)
+    rows = feats.shape[0]
+    cols = pieces[0].shape[1] // 2
+    parts = count * chunks
+    width = parts * cols
+
+    def at(region):
+        return lambda k, m: (0, region * parts + (m[0] ^ k) * chunks + chunk)
+
+    any_spec = pl.BlockSpec(memory_space=pl.ANY)
+    in_specs = (
+        [pl.BlockSpec((rows, cols), at(r)) for r in (1, 2)]
+        + [pl.BlockSpec((before.shape[0], cols), at(r)) for r in (1, 2)]
+        + [pl.BlockSpec((after.shape[0], cols), at(r)) for r in (1, 2)]
+        + [pl.BlockSpec((rows, cols), at(0)), pl.BlockSpec((after_out.shape[0], cols), at(0))]
+        + [pl.BlockSpec((3, cols), at(r)) for r in range(3)]
+        + [any_spec] * count
+    )
+    args = [me, feats, feats, before, before, after, after, grad_out, after_out, taps, taps, taps, *pieces]
+    aliases = {}
+    if so_far is not None:
+        in_specs.append(any_spec)
+        args.append(so_far)
+        aliases = {len(args) - 1: 0}
+    return pl.pallas_call(
+        functools.partial(final_kernel, count, cols, width, chunk, chunks, so_far is not None),
+        grid_spec=pltpu.PrefetchScalarGridSpec(
+            num_scalar_prefetch=1,
+            grid=(count,),
+            in_specs=in_specs,
+            out_specs=any_spec,
+            scratch_shapes=[
+                pltpu.VMEM((count, rows + EXTRA, 2 * cols), jnp.bfloat16),
+                pltpu.VMEM((count, 3, rows, cols), jnp.bfloat16),
+                pltpu.SemaphoreType.DMA((count,)),
+                pltpu.SemaphoreType.DMA((count, 3)),
+            ],
+        ),
+        out_shape=jax.ShapeDtypeStruct((rows, 3 * width), jnp.bfloat16),
+        input_output_aliases=aliases,
+        compiler_params=pltpu.CompilerParams(vmem_limit_bytes=VMEM_LIMIT),
+        cost_estimate=pl.CostEstimate(
+            flops=30 * rows * cols * count, bytes_accessed=16 * rows * cols * count, transcendentals=0
+        ),
+        name=f"final{chunk}",
+    )(*args)
+
+
+def exchange(pieces, axis):
+    devices = range(lax.axis_size(axis))
+    return [pieces[0]] + [
+        lax.ppermute(pieces[j], axis, [(i, i ^ j) for i in devices]) for j in range(1, len(pieces))
+    ]
+
+
+def dense_shards(feats, short_weight, grad_out, filt):
+    length, block = filt.shape
+    count = lax.axis_size("ctx")
+    feats, grad_out = feats[0], grad_out[0]
+    rows = feats.shape[0]
+    chunks = CHUNKS
+    cols = block // chunks
+    scale_inv = 1.0 / math.sqrt(length)
+    high, low = odd_tables(length)
+    inverse = np.ascontiguousarray(high.T)
+    me = lax.axis_index("ctx")
+    dp = lax.axis_index("dp")
+    core, x = dp % 2, dp // 2
+    place = jnp.stack([me, core]).astype(jnp.int32)
+    before = from_behind(feats[rows - 2 :], "ctx", 1)
+    after = from_behind(feats[:2], "ctx", -1)
+    after_out = from_behind(grad_out[:2], "ctx", -1)
+    spectrum = filter_spectrum(filt, high, low, scale_inv / length)
+
+    backs, filts = [], []
+    for c in range(chunks):
+        pieces = gate(place, feats, before, short_weight, grad_out, c, chunks, count, cols)
+        pieces = exchange(pieces, "ctx")
+        *outs, send, keep = spectral(place, spectrum, high, inverse, pieces, c, scale_inv / length)
+        backs.append(exchange(outs, "ctx"))
+        summed = keep + lax.ppermute(send, "dp", [(i, i ^ 1) for i in range(4)])
+        half = length // 4
+        other = lax.dynamic_slice_in_dim(summed, (1 - x) * half, half, 0)
+        mine = lax.dynamic_slice_in_dim(summed, x * half, half, 0)
+        filts.append(mine + lax.ppermute(other, "dp", [(i, i ^ 2) for i in range(4)]))
+    result = None
+    for c in range(chunks):
+        result = final(
+            place, feats, before, after, grad_out, after_out, short_weight, backs[c], result, c, chunks
+        )
+    return (result[None], jnp.concatenate(filts, axis=1))
+
 
 full_precision = lax.Precision.HIGHEST
 split_precision = lax.Precision.HIGH
@@ -85,7 +459,7 @@
     return signal.reshape(length, signal.shape[2]) / (2.0 * length)
 
 
-def spectral(gated_sig, grad_sig, filter_cols, tables, length):
+def long_spectral(gated_sig, grad_sig, filter_cols, tables, length):
     g_spec = data_forward(gated_sig, tables, split_precision)
     d_spec = data_forward(grad_sig, tables, split_precision)
     h_spec = filter_forward(filter_cols, tables)
@@ -103,7 +477,7 @@
     return (conv_out, gated_grad, filt_grad)
 
 
-def shards(feats, short_weight, grad_out, filt):
+def long_shards(feats, short_weight, grad_out, filt):
     rows = feats.shape[1]
     width = feats.shape[2] // 3
     length = filt.shape[0]
@@ -150,7 +524,7 @@
     wide_grad = wide_grad.reshape(replicas, narrow, length)
     offset = lax.axis_index("dp") * narrow
     filt_cols = lax.dynamic_slice_in_dim(filt, offset, narrow, 1)
-    conv_out, gated_grad, filt_grad = spectral(
+    conv_out, gated_grad, filt_grad = long_spectral(
         wide_gated, wide_grad, filt_cols * scale_inv, tables, length
     )
     back_conv, back_grad = (
@@ -210,6 +584,21 @@
     return (grad_in.astype(jnp.bfloat16), filt_out)
 
 
+def shards(feats, short_weight, grad_out, filt):
+    count = lax.axis_size("ctx")
+    length, block = filt.shape
+    fits = (
+        length <= 1024
+        and length % (2 * TILE) == 0
+        and count & (count - 1) == 0
+        and feats.shape[1] % 128 == 0
+        and block % (128 * CHUNKS) == 0
+        and lax.axis_size("dp") == 4
+    )
+    plan = dense_shards if fits else long_shards
+    return plan(feats, short_weight, grad_out, filt)
+
+
 def solution(mesh):
     return jax.shard_map(
         shards,

time: 356 us -> 173 us (0.49)
  matrix products: 82.3 us -> 0 us
  waiting for transfers between devices: 105 us -> 27.4 us
  other arithmetic: 65 us -> 5.47 us
  Pallas kernels: 0 us -> 56.6 us
  local copies, waits for them, and re-layouts: 54.9 us -> 22.5 us
  starting transfers between devices: 43.2 us -> 58.9 us
    all_to_all x9 -> x0, waiting for transfers between devices: 102 us -> none  [the longest x1 23.9 us: shards(): lax.all_to_all(lax.all_to_all(gated_grad.astype(jnp.bfloat16)[None, None]...]
    dot_general x12 -> x0, matrix products: 82.3 us -> none  [the longest x2 26.2 us: data_inverse(): jnp.einsum('sckrb,rknb->scnb', partial_sig, tables[0], precision=full_pre...]
    pallas_call x0 -> x7, Pallas kernels: none -> 56.6 us  [the longest x2 27.7 us: spectral(): pl.pallas_call(functools.partial(spectral_kernel, count, rows, scale), gr...]
    ppermute x0 -> x32, starting transfers between devices: none -> 51.3 us  [the longest x28 48.6 us: exchange(): lax.ppermute(pieces[j], axis, [(i, i ^ j) for i in devices])]
    all_to_all x9 -> x0, starting transfers between devices: 37 us -> none  [the longest x1 4.88 us: shards(): lax.all_to_all(lax.all_to_all(spread(gated), 'dp', split_axis=1, concat_a...]
    ppermute x0 -> x32, waiting for transfers between devices: none -> 24 us  [the longest x28 24 us: exchange(): lax.ppermute(pieces[j], axis, [(i, i ^ j) for i in devices])]
    convert_element_type x5 -> x0, other arithmetic: 20.6 us -> none  [the longest x1 14.3 us: shards(): return (grad_in.astype(jnp.bfloat16), filt_out)]
    all_to_all x9 -> x0, local copies, waits for them, and re-layouts: 14.9 us -> none  [the longest x1 3.01 us: shards(): lax.all_to_all(gated_grad.astype(jnp.bfloat16)[None, None], 'dp', split_a...]
  transfers between devices with their start and end apart: 11 -> 35, of which waited for: 8 -> 8; matrix products, arithmetic and copies ran while one was open for 29% -> 3% of each run, Pallas kernels for 0% -> 31%
where the time goes in v1:
time: 173 us; the launch traced here: 172 us
  starting transfers between devices  58.9 us (34%)
  Pallas kernels  56.6 us (33%)
  waiting for transfers between devices  27.4 us (16%)
  local copies, waits for them, and re-layouts  22.5 us (13%)
  other arithmetic  5.47 us (3%)
    ppermute x28, starting transfers between devices, exchange(): lax.ppermute(pieces[j], axis, [(i, i ^ j) for i in devices])  48.6 us
    pallas_call x2, Pallas kernels, spectral(): pl.pallas_call(functools.partial(spectral_kernel, count, rows, scale), gr...  27.7 us
    ppermute x28, waiting for transfers between devices, exchange(): lax.ppermute(pieces[j], axis, [(i, i ^ j) for i in devices])  24 us
    unnamed x72, local copies, waits for them, and re-layouts  20 us
    pallas_call x1, Pallas kernels, filter_spectrum(): pl.pallas_call(functools.partial(filter_kernel, scale), grid=(rows // TIL...  11.6 us
    pallas_call x2, Pallas kernels, final(): pl.pallas_call(functools.partial(final_kernel, count, cols, width, chunk,...  11.5 us
    ppermute x3, starting transfers between devices, from_behind(): return lax.ppermute(block, axis, route)  7.58 us
    pallas_call x2, Pallas kernels, gate(): pl.pallas_call(functools.partial(gate_kernel, count), grid_spec=spec, out...  5.73 us
  transfers between devices with their start and end apart: 35, of which 8 were waited for; matrix products, arithmetic and copies ran while one was open for 3% of the time, Pallas kernels for 31%

profile of v1, /device:TPU:0, one launch (start us, length us, event | category | flops | bytes accessed | tf_op | source)
XLA Modules:
  0.0 171.8 jit_solution(11793075403841562435)
XLA Ops:
  1.7 4.9 %collective-permute-start = (bf16[2,12288]{1,0:T(2,128)(2,1)S(1)}, bf16[2,12288]{1,0:T(2,128)(2,1)S(1)}, u32[]{:S(2)}, u32[]{:S(2)}) collective-permute-start(bf16[2,12288]{1,0:T(2,128)(2,1)S(1)} %get-tuple-element.75), channel_id=1, source_target_pairs={{0,1},{1,2},{2,3},{3,4},{4,5},{5,6},{6,7},{8,9},{9,10},{10,11},{11... | collective-permute-start | bytes 147464 | tf_op jit(solution)/shard_map/ppermute | solution.py:389
  12.4 2.9 %gate0.1 = (bf16[128,512]{1,0:T(8,128)(2,1)S(1)}, bf16[128,512]{1,0:T(8,128)(2,1)S(1)}, bf16[128,512]{1,0:T(8,128)(2,1)S(1)}, bf16[128,512]{1,0:T(8,128)(2,1)S(1...) custom-call(s32[2]{0:T(128)S(1)} %pad_add_fusion.me_ref.refs_0_, ...), custom_call_target="tpu_custom_call" | custom-call | flops 5242880 | bytes 3145728 | tf_op jit(solution)/shard_map/gate0/pallas_call | solution.py:74
  15.3 2.4 %collective-permute-start.17 = (bf16[128,512]{1,0:T(8,128)(2,1)S(1)}, bf16[128,512]{1,0:T(8,128)(2,1)S(1)}, u32[]{:S(2)}, u32[]{:S(2)}) collective-permute-start(bf16[128,512]{1,0:T(8,128)(2,1)S(1)} %get-tuple-element.55), channel_id=1, source_target_pairs={{0,1},{1,0},{2,3},{3,2},{4,5},{5,4},{6,7},{7,6},{8,9},{9,8},{10,11... | collective-permute-start | bytes 393224 | tf_op jit(solution)/shard_map/ppermute | solution.py:340
  20.1 3.0 %collective-permute-start.20 = (bf16[128,512]{1,0:T(8,128)(2,1)S(1)}, bf16[128,512]{1,0:T(8,128)(2,1)S(1)}, u32[]{:S(2)}, u32[]{:S(2)}) collective-permute-start(bf16[128,512]{1,0:T(8,128)(2,1)S(1)} %get-tuple-element.58), channel_id=1, source_target_pairs={{0,4},{1,5},{2,6},{3,7},{4,0},{5,1},{6,2},{7,3},{8,12},{9,13},{10,... | collective-permute-start | bytes 393224 | tf_op jit(solution)/shard_map/ppermute | solution.py:340
  23.5 2.9 %gate1.1 = (bf16[128,512]{1,0:T(8,128)(2,1)S(1)}, bf16[128,512]{1,0:T(8,128)(2,1)S(1)}, bf16[128,512]{1,0:T(8,128)(2,1)S(1)}, bf16[128,512]{1,0:T(8,128)(2,1)S(1...) custom-call(s32[2]{0:T(128)S(1)} %pad_add_fusion.me_ref.refs_0_, ...), custom_call_target="tpu_custom_call" | custom-call | flops 5242880 | bytes 3145728 | tf_op jit(solution)/shard_map/gate1/pallas_call | solution.py:74
  26.4 3.7 %collective-permute-start.22 = (bf16[128,512]{1,0:T(8,128)(2,1)S(1)}, bf16[128,512]{1,0:T(8,128)(2,1)S(1)}, u32[]{:S(2)}, u32[]{:S(2)}) collective-permute-start(bf16[128,512]{1,0:T(8,128)(2,1)S(1)} %get-tuple-element.60), channel_id=1, source_target_pairs={{0,6},{1,7},{2,4},{3,5},{4,2},{5,3},{6,0},{7,1},{8,14},{9,15},{10,... | collective-permute-start | bytes 393224 | tf_op jit(solution)/shard_map/ppermute | solution.py:340
  31.8 5.5 %collective-permute-done.20.rest_4_ = bf16[128,512]{1,0:T(8,128)(2,1)S(1)} collective-permute-done((bf16[128,512]{1,0:T(8,128)(2,1)S(1)}, bf16[128,512]{1,0:T(8,128)(2,1)S(1)}, u32[]{:S(2)}, u32[]{:S(2)}) %collective-permute-start.20) | collective-permute-done | bytes 131104 | tf_op jit(solution)/shard_map/ppermute | solution.py:340
  38.1 11.6 %filter_spectrum.1.spec_ref = f32[2048,512]{1,0:T(8,128)} custom-call(f32[1024,512]{1,0:T(8,128)S(1)} %copy-done.26, bf16[2048,1024]{1,0:T(8,128)(2,1)} %constant.44.clone.high_ref.forward_ref, bf16[2048,1024]{1,0:T(8,128)(2,1)} %constant.45.clone.low_ref), custom_call_target="tpu_custom_call" | custom-call | flops 6442450944 | bytes 14680064 | tf_op jit(solution)/shard_map/filter_spectrum/pallas_call | solution.py:100
  50.3 3.3 %collective-permute-start.6 = (bf16[128,512]{1,0:T(8,128)(2,1)S(1)}, bf16[128,512]{1,0:T(8,128)(2,1)S(1)}, u32[]{:S(2)}, u32[]{:S(2)}) collective-permute-start(bf16[128,512]{1,0:T(8,128)(2,1)S(1)} %get-tuple-element.42), channel_id=1, source_target_pairs={{0,4},{1,5},{2,6},{3,7},{4,0},{5,1},{6,2},{7,3},{8,12},{9,13},{10,... | collective-permute-start | bytes 393224 | tf_op jit(solution)/shard_map/ppermute | solution.py:340
  54.8 3.8 %collective-permute-start.8 = (bf16[128,512]{1,0:T(8,128)(2,1)S(1)}, bf16[128,512]{1,0:T(8,128)(2,1)S(1)}, u32[]{:S(2)}, u32[]{:S(2)}) collective-permute-start(bf16[128,512]{1,0:T(8,128)(2,1)S(1)} %get-tuple-element.44), channel_id=1, source_target_pairs={{0,6},{1,7},{2,4},{3,5},{4,2},{5,3},{6,0},{7,1},{8,14},{9,15},{10,... | collective-permute-start | bytes 393224 | tf_op jit(solution)/shard_map/ppermute | solution.py:340
  59.0 13.8 %spectral0.1 = (bf16[136,512]{1,0:T(8,128)(2,1)S(1)}, bf16[136,512]{1,0:T(8,128)(2,1)S(1)}, bf16[136,512]{1,0:T(8,128)(2,1)S(1)}, bf16[136,512]{1,0:T(8,128)(2,1...) custom-call(s32[2]{0:T(128)S(1)} %pad_add_fusion.me_ref.refs_0_, ...), custom_call_target="tpu_custom_call" | custom-call | flops 5368709120 | bytes 13631488 | tf_op jit(solution)/shard_map/spectral0/pallas_call | solution.py:192
  75.7 13.9 %spectral1.1 = (bf16[136,512]{1,0:T(8,128)(2,1)S(1)}, bf16[136,512]{1,0:T(8,128)(2,1)S(1)}, bf16[136,512]{1,0:T(8,128)(2,1)S(1)}, bf16[136,512]{1,0:T(8,128)(2,1...) custom-call(s32[2]{0:T(128)S(1)} %pad_add_fusion.me_ref.refs_0_, ...), custom_call_target="tpu_custom_call" | custom-call | flops 5368709120 | bytes 13631488 | tf_op jit(solution)/shard_map/spectral1/pallas_call | solution.py:192
  95.6 3.3 %collective-permute-start.24 = (bf16[136,512]{1,0:T(8,128)(2,1)S(1)}, bf16[136,512]{1,0:T(8,128)(2,1)S(1)}, u32[]{:S(2)}, u32[]{:S(2)}) collective-permute-start(bf16[136,512]{1,0:T(8,128)(2,1)S(1)} %get-tuple-element.63), channel_id=1, source_target_pairs={{0,1},{1,0},{2,3},{3,2},{4,5},{5,4},{6,7},{7,6},{8,9},{9,8},{10,11... | collective-permute-start | bytes 417800 | tf_op jit(solution)/shard_map/ppermute | solution.py:340
  100.7 2.6 %collective-permute-start.25 = (bf16[136,512]{1,0:T(8,128)(2,1)S(1)}, bf16[136,512]{1,0:T(8,128)(2,1)S(1)}, u32[]{:S(2)}, u32[]{:S(2)}) collective-permute-start(bf16[136,512]{1,0:T(8,128)(2,1)S(1)} %get-tuple-element.64), channel_id=1, source_target_pairs={{0,2},{1,3},{2,0},{3,1},{4,6},{5,7},{6,4},{7,5},{8,10},{9,11},{10,... | collective-permute-start | bytes 417800 | tf_op jit(solution)/shard_map/ppermute | solution.py:340
  108.3 2.8 %collective-permute-start.28 = (bf16[136,512]{1,0:T(8,128)(2,1)}, bf16[136,512]{1,0:T(8,128)(2,1)}, u32[]{:S(2)}, u32[]{:S(2)}) collective-permute-start(bf16[136,512]{1,0:T(8,128)(2,1)} %get-tuple-element.67), channel_id=1, source_target_pairs={{0,5},{1,4},{2,7},{3,6},{4,1},{5,0},{6,3},{7,2},{8,13},{9,12},{10,... | collective-permute-start | bytes 417800 | tf_op jit(solution)/shard_map/ppermute | solution.py:340
  111.1 2.6 %collective-permute-done.26.refs_15_ = bf16[136,512]{1,0:T(8,128)(2,1)S(1)} collective-permute-done((bf16[136,512]{1,0:T(8,128)(2,1)S(1)}, bf16[136,512]{1,0:T(8,128)(2,1)S(1)}, u32[]{:S(2)}, u32[]{:S(2)}) %collective-permute-start.26) | collective-permute-done | bytes 139296 | tf_op jit(solution)/shard_map/ppermute | solution.py:340
  115.2 2.1 %collective-permute-start.30 = (bf16[136,512]{1,0:T(8,128)(2,1)}, bf16[136,512]{1,0:T(8,128)(2,1)}, u32[]{:S(2)}, u32[]{:S(2)}) collective-permute-start(bf16[136,512]{1,0:T(8,128)(2,1)} %get-tuple-element.69), channel_id=1, source_target_pairs={{0,7},{1,6},{2,5},{3,4},{4,3},{5,2},{6,1},{7,0},{8,15},{9,14},{10,... | collective-permute-start | bytes 417800 | tf_op jit(solution)/shard_map/ppermute | solution.py:340
  118.6 6.3 %collective-permute-done.27.refs_16_ = bf16[136,512]{1,0:T(8,128)(2,1)} collective-permute-done((bf16[136,512]{1,0:T(8,128)(2,1)}, bf16[136,512]{1,0:T(8,128)(2,1)}, u32[]{:S(2)}, u32[]{:S(2)}) %collective-permute-start.27) | collective-permute-done | bytes 139296 | tf_op jit(solution)/shard_map/ppermute | solution.py:340
  125.2 2.4 %collective-permute-done.28.refs_17_ = bf16[136,512]{1,0:T(8,128)(2,1)} collective-permute-done((bf16[136,512]{1,0:T(8,128)(2,1)}, bf16[136,512]{1,0:T(8,128)(2,1)}, u32[]{:S(2)}, u32[]{:S(2)}) %collective-permute-start.28) | collective-permute-done | bytes 139296 | tf_op jit(solution)/shard_map/ppermute | solution.py:340
  127.6 3.5 %collective-permute-start.12 = (bf16[136,512]{1,0:T(8,128)(2,1)}, bf16[136,512]{1,0:T(8,128)(2,1)S(1)}, u32[]{:S(2)}, u32[]{:S(2)}) collective-permute-start(bf16[136,512]{1,0:T(8,128)(2,1)} %copy-done.28), channel_id=1, source_target_pairs={{0,3},{1,2},{2,1},{3,0},{4,7},{5,6},{6,5},{7,4},{8,11},{9,10},{10,... | collective-permute-start | bytes 417800 | tf_op jit(solution)/shard_map/ppermute | solution.py:340
  133.4 2.6 %collective-permute-start.13 = (bf16[136,512]{1,0:T(8,128)(2,1)}, bf16[136,512]{1,0:T(8,128)(2,1)S(1)}, u32[]{:S(2)}, u32[]{:S(2)}) collective-permute-start(bf16[136,512]{1,0:T(8,128)(2,1)} %copy-done.27), channel_id=1, source_target_pairs={{0,4},{1,5},{2,6},{3,7},{4,0},{5,1},{6,2},{7,3},{8,12},{9,13},{10,... | collective-permute-start | bytes 417800 | tf_op jit(solution)/shard_map/ppermute | solution.py:340
  145.1 6.0 %collective-permute-done.13.refs_16_ = bf16[136,512]{1,0:T(8,128)(2,1)S(1)} collective-permute-done((bf16[136,512]{1,0:T(8,128)(2,1)}, bf16[136,512]{1,0:T(8,128)(2,1)S(1)}, u32[]{:S(2)}, u32[]{:S(2)}) %collective-permute-start.13) | collective-permute-done | bytes 139296 | tf_op jit(solution)/shard_map/ppermute | solution.py:340
  157.3 5.7 %final0.1.refs_20_ = bf16[128,12288]{1,0:T(8,128)(2,1)} custom-call(s32[2]{0:T(128)S(1)} %pad_add_fusion.me_ref.refs_0_, bf16[128,12288]{1,0:T(8,128)(2,1)S(1)} %bitcast.17, bf16[128,12288]{1,0:T(8,128)(2,1)S(1)} %bitcast.18, bf16[2,12288]{1,0:T(2,128)(2,1)S(1)} %collective-permute-done.bq_ref.bk_ref.bv_ref.refs_3_.refs_4_, ...), custom_call_target="tpu_custom_call" | custom-call | flops 7864320 | bytes 4194304 | tf_op jit(solution)/shard_map/final0/pallas_call | solution.py:313
  163.1 5.9 %final1.1 = bf16[128,12288]{1,0:T(8,128)(2,1)} custom-call(s32[2]{0:T(128)S(1)} %pad_add_fusion.me_ref.refs_0_, bf16[128,12288]{1,0:T(8,128)(2,1)S(1)} %bitcast.19, bf16[128,12288]{1,0:T(8,128)(2,1)S(1)} %bitcast.20, bf16[2,12288]{1,0:T(2,128)(2,1)S(1)} %collective-permute-done.bq_ref.bk_ref.bv_ref.refs_3_.refs_4_, ...), custom_call_target="tpu_custom_call", output_to_operand_aliasing={{}: (20, {})} | custom-call | flops 7864320 | bytes 4194304 | tf_op jit(solution)/shard_map/final1/pallas_call | solution.py:313
  (135 shorter events, 53.3 us)
Async XLA Ops:
  20.1 17.2 %collective-permute-start.20 = (bf16[128,512]{1,0:T(8,128)(2,1)S(1)}, bf16[128,512]{1,0:T(8,128)(2,1)S(1)}, u32[]{:S(2)}, u32[]{:S(2)}) collective-permute-start(bf16[128,512]{1,0:T(8,128)(2,1)S(1)} %get-tuple-element.58), channel_id=1, source_target_pairs={{0,4},{1,5},{2,6},{3,7},{4,0},{5,1},{6,2},{7,3},{8,12},{9,13},{10,... | collective-permute-start | bytes 393224 | tf_op jit(solution)/shard_map/ppermute | solution.py:340
  23.1 26.7 %collective-permute-start.21 = (bf16[128,512]{1,0:T(8,128)(2,1)S(1)}, bf16[128,512]{1,0:T(8,128)(2,1)S(1)}, u32[]{:S(2)}, u32[]{:S(2)}) collective-permute-start(bf16[128,512]{1,0:T(8,128)(2,1)S(1)} %get-tuple-element.59), channel_id=1, source_target_pairs={{0,5},{1,4},{2,7},{3,6},{4,1},{5,0},{6,3},{7,2},{8,13},{9,12},{10,... | collective-permute-start | bytes 393224 | tf_op jit(solution)/shard_map/ppermute | solution.py:340
  26.4 23.9 %collective-permute-start.22 = (bf16[128,512]{1,0:T(8,128)(2,1)S(1)}, bf16[128,512]{1,0:T(8,128)(2,1)S(1)}, u32[]{:S(2)}, u32[]{:S(2)}) collective-permute-start(bf16[128,512]{1,0:T(8,128)(2,1)S(1)} %get-tuple-element.60), channel_id=1, source_target_pairs={{0,6},{1,7},{2,4},{3,5},{4,2},{5,3},{6,0},{7,1},{8,14},{9,15},{10,... | collective-permute-start | bytes 393224 | tf_op jit(solution)/shard_map/ppermute | solution.py:340
  30.1 23.6 %collective-permute-start.23 = (bf16[128,512]{1,0:T(8,128)(2,1)S(1)}, bf16[128,512]{1,0:T(8,128)(2,1)S(1)}, u32[]{:S(2)}, u32[]{:S(2)}) collective-permute-start(bf16[128,512]{1,0:T(8,128)(2,1)S(1)} %get-tuple-element.61), channel_id=1, source_target_pairs={{0,7},{1,6},{2,5},{3,4},{4,3},{5,2},{6,1},{7,0},{8,15},{9,14},{10,... | collective-permute-start | bytes 393224 | tf_op jit(solution)/shard_map/ppermute | solution.py:340
  31.0 23.8 %collective-permute-start.3 = (bf16[128,512]{1,0:T(8,128)(2,1)S(1)}, bf16[128,512]{1,0:T(8,128)(2,1)S(1)}, u32[]{:S(2)}, u32[]{:S(2)}) collective-permute-start(bf16[128,512]{1,0:T(8,128)(2,1)S(1)} %get-tuple-element.39), channel_id=1, source_target_pairs={{0,1},{1,0},{2,3},{3,2},{4,5},{5,4},{6,7},{7,6},{8,9},{9,8},{10,11... | collective-permute-start | bytes 393224 | tf_op jit(solution)/shard_map/ppermute | solution.py:340
  37.3 21.4 %collective-permute-start.4 = (bf16[128,512]{1,0:T(8,128)(2,1)S(1)}, bf16[128,512]{1,0:T(8,128)(2,1)S(1)}, u32[]{:S(2)}, u32[]{:S(2)}) collective-permute-start(bf16[128,512]{1,0:T(8,128)(2,1)S(1)} %get-tuple-element.40), channel_id=1, source_target_pairs={{0,2},{1,3},{2,0},{3,1},{4,6},{5,7},{6,4},{7,5},{8,10},{9,11},{10,... | collective-permute-start | bytes 393224 | tf_op jit(solution)/shard_map/ppermute | solution.py:340
  49.8 24.5 %collective-permute-start.5 = (bf16[128,512]{1,0:T(8,128)(2,1)S(1)}, bf16[128,512]{1,0:T(8,128)(2,1)S(1)}, u32[]{:S(2)}, u32[]{:S(2)}) collective-permute-start(bf16[128,512]{1,0:T(8,128)(2,1)S(1)} %get-tuple-element.41), channel_id=1, source_target_pairs={{0,3},{1,2},{2,1},{3,0},{4,7},{5,6},{6,5},{7,4},{8,11},{9,10},{10,... | collective-permute-start | bytes 393224 | tf_op jit(solution)/shard_map/ppermute | solution.py:340
  50.3 25.3 %collective-permute-start.6 = (bf16[128,512]{1,0:T(8,128)(2,1)S(1)}, bf16[128,512]{1,0:T(8,128)(2,1)S(1)}, u32[]{:S(2)}, u32[]{:S(2)}) collective-permute-start(bf16[128,512]{1,0:T(8,128)(2,1)S(1)} %get-tuple-element.42), channel_id=1, source_target_pairs={{0,4},{1,5},{2,6},{3,7},{4,0},{5,1},{6,2},{7,3},{8,12},{9,13},{10,... | collective-permute-start | bytes 393224 | tf_op jit(solution)/shard_map/ppermute | solution.py:340
  53.7 22.0 %collective-permute-start.7 = (bf16[128,512]{1,0:T(8,128)(2,1)S(1)}, bf16[128,512]{1,0:T(8,128)(2,1)S(1)}, u32[]{:S(2)}, u32[]{:S(2)}) collective-permute-start(bf16[128,512]{1,0:T(8,128)(2,1)S(1)} %get-tuple-element.43), channel_id=1, source_target_pairs={{0,5},{1,4},{2,7},{3,6},{4,1},{5,0},{6,3},{7,2},{8,13},{9,12},{10,... | collective-permute-start | bytes 393224 | tf_op jit(solution)/shard_map/ppermute | solution.py:340
  54.8 21.0 %collective-permute-start.8 = (bf16[128,512]{1,0:T(8,128)(2,1)S(1)}, bf16[128,512]{1,0:T(8,128)(2,1)S(1)}, u32[]{:S(2)}, u32[]{:S(2)}) collective-permute-start(bf16[128,512]{1,0:T(8,128)(2,1)S(1)} %get-tuple-element.44), channel_id=1, source_target_pairs={{0,6},{1,7},{2,4},{3,5},{4,2},{5,3},{6,0},{7,1},{8,14},{9,15},{10,... | collective-permute-start | bytes 393224 | tf_op jit(solution)/shard_map/ppermute | solution.py:340
  58.6 17.1 %collective-permute-start.9 = (bf16[128,512]{1,0:T(8,128)(2,1)S(1)}, bf16[128,512]{1,0:T(8,128)(2,1)S(1)}, u32[]{:S(2)}, u32[]{:S(2)}) collective-permute-start(bf16[128,512]{1,0:T(8,128)(2,1)S(1)} %get-tuple-element.45), channel_id=1, source_target_pairs={{0,7},{1,6},{2,5},{3,4},{4,3},{5,2},{6,1},{7,0},{8,15},{9,14},{10,... | collective-permute-start | bytes 393224 | tf_op jit(solution)/shard_map/ppermute | solution.py:340
  74.3 29.0 %collective-permute-start.1 = (bf16[2,12288]{1,0:T(2,128)(2,1)S(1)}, bf16[2,12288]{1,0:T(2,128)(2,1)S(1)}, u32[]{:S(2)}, u32[]{:S(2)}) collective-permute-start(bf16[2,12288]{1,0:T(2,128)(2,1)S(1)} %get-tuple-element.74), channel_id=1, source_target_pairs={{1,0},{2,1},{3,2},{4,3},{5,4},{6,5},{7,6},{9,8},{10,9},{11,10},{12... | collective-permute-start | bytes 147464 | tf_op jit(solution)/shard_map/ppermute | solution.py:389
  75.6 38.8 %collective-permute-start.31 = (f32[512,256]{1,0:T(8,128)S(1)}, f32[512,256]{1,0:T(8,128)S(1)}, u32[]{:S(2)}, u32[]{:S(2)}) collective-permute-start(f32[512,256]{1,0:T(8,128)S(1)} %get-tuple-element.71), channel_id=1, source_target_pairs={{0,8},{8,0},{16,24},{24,16},{1,9},{9,1},{17,25},{25,17},{2,10},{10... | collective-permute-start | bytes 1572872 | tf_op jit(solution)/shard_map/ppermute | solution.py:369
  93.7 39.6 %collective-permute-start.33 = (f32[512,256]{1,0:T(8,128)}, f32[512,256]{1,0:T(8,128)}, u32[]{:S(2)}, u32[]{:S(2)}) collective-permute-start(f32[512,256]{1,0:T(8,128)} %get-tuple-element.73), channel_id=1, source_target_pairs={{0,8},{8,0},{16,24},{24,16},{1,9},{9,1},{17,25},{25,17},{2,10},{10... | collective-permute-start | bytes 1572872 | tf_op jit(solution)/shard_map/ppermute | solution.py:369
  105.8 19.0 %collective-permute-start.27 = (bf16[136,512]{1,0:T(8,128)(2,1)}, bf16[136,512]{1,0:T(8,128)(2,1)}, u32[]{:S(2)}, u32[]{:S(2)}) collective-permute-start(bf16[136,512]{1,0:T(8,128)(2,1)} %get-tuple-element.66), channel_id=1, source_target_pairs={{0,4},{1,5},{2,6},{3,7},{4,0},{5,1},{6,2},{7,3},{8,12},{9,13},{10,... | collective-permute-start | bytes 417800 | tf_op jit(solution)/shard_map/ppermute | solution.py:340
  108.3 19.3 %collective-permute-start.28 = (bf16[136,512]{1,0:T(8,128)(2,1)}, bf16[136,512]{1,0:T(8,128)(2,1)}, u32[]{:S(2)}, u32[]{:S(2)}) collective-permute-start(bf16[136,512]{1,0:T(8,128)(2,1)} %get-tuple-element.67), channel_id=1, source_target_pairs={{0,5},{1,4},{2,7},{3,6},{4,1},{5,0},{6,3},{7,2},{8,13},{9,12},{10,... | collective-permute-start | bytes 417800 | tf_op jit(solution)/shard_map/ppermute | solution.py:340
  115.2 16.6 %collective-permute-start.30 = (bf16[136,512]{1,0:T(8,128)(2,1)}, bf16[136,512]{1,0:T(8,128)(2,1)}, u32[]{:S(2)}, u32[]{:S(2)}) collective-permute-start(bf16[136,512]{1,0:T(8,128)(2,1)} %get-tuple-element.69), channel_id=1, source_target_pairs={{0,7},{1,6},{2,5},{3,4},{4,3},{5,2},{6,1},{7,0},{8,15},{9,14},{10,... | collective-permute-start | bytes 417800 | tf_op jit(solution)/shard_map/ppermute | solution.py:340
  127.6 14.2 %collective-permute-start.12 = (bf16[136,512]{1,0:T(8,128)(2,1)}, bf16[136,512]{1,0:T(8,128)(2,1)S(1)}, u32[]{:S(2)}, u32[]{:S(2)}) collective-permute-start(bf16[136,512]{1,0:T(8,128)(2,1)} %copy-done.28), channel_id=1, source_target_pairs={{0,3},{1,2},{2,1},{3,0},{4,7},{5,6},{6,5},{7,4},{8,11},{9,10},{10,... | collective-permute-start | bytes 417800 | tf_op jit(solution)/shard_map/ppermute | solution.py:340
  131.9 37.1 %collective-permute-start.32 = (f32[256,256]{1,0:T(8,128)}, f32[256,256]{1,0:T(8,128)}, u32[]{:S(2)}, u32[]{:S(2)}) collective-permute-start(f32[256,256]{1,0:T(8,128)} %constant_dynamic-slice_fusion.1), channel_id=1, source_target_pairs={{0,16},{8,24},{16,0},{24,8},{1,17},{9,25},{17,1},{25,9},{2,18},{10... | collective-permute-start | bytes 786440 | tf_op jit(solution)/shard_map/ppermute | solution.py:373
  133.4 17.7 %collective-permute-start.13 = (bf16[136,512]{1,0:T(8,128)(2,1)}, bf16[136,512]{1,0:T(8,128)(2,1)S(1)}, u32[]{:S(2)}, u32[]{:S(2)}) collective-permute-start(bf16[136,512]{1,0:T(8,128)(2,1)} %copy-done.27), channel_id=1, source_target_pairs={{0,4},{1,5},{2,6},{3,7},{4,0},{5,1},{6,2},{7,3},{8,12},{9,13},{10,... | collective-permute-start | bytes 417800 | tf_op jit(solution)/shard_map/ppermute | solution.py:340
  138.0 25.0 %collective-permute-start.14 = (bf16[136,512]{1,0:T(8,128)(2,1)}, bf16[136,512]{1,0:T(8,128)(2,1)}, u32[]{:S(2)}, u32[]{:S(2)}) collective-permute-start(bf16[136,512]{1,0:T(8,128)(2,1)} %get-tuple-element.51), channel_id=1, source_target_pairs={{0,5},{1,4},{2,7},{3,6},{4,1},{5,0},{6,3},{7,2},{8,13},{9,12},{10,... | collective-permute-start | bytes 417800 | tf_op jit(solution)/shard_map/ppermute | solution.py:340
  140.0 22.9 %collective-permute-start.15 = (bf16[136,512]{1,0:T(8,128)(2,1)}, bf16[136,512]{1,0:T(8,128)(2,1)}, u32[]{:S(2)}, u32[]{:S(2)}) collective-permute-start(bf16[136,512]{1,0:T(8,128)(2,1)} %get-tuple-element.52), channel_id=1, source_target_pairs={{0,6},{1,7},{2,4},{3,5},{4,2},{5,3},{6,0},{7,1},{8,14},{9,15},{10,... | collective-permute-start | bytes 417800 | tf_op jit(solution)/shard_map/ppermute | solution.py:340
  142.4 20.6 %collective-permute-start.16 = (bf16[136,512]{1,0:T(8,128)(2,1)}, bf16[136,512]{1,0:T(8,128)(2,1)}, u32[]{:S(2)}, u32[]{:S(2)}) collective-permute-start(bf16[136,512]{1,0:T(8,128)(2,1)} %get-tuple-element.53), channel_id=1, source_target_pairs={{0,7},{1,6},{2,5},{3,4},{4,3},{5,2},{6,1},{7,0},{8,15},{9,14},{10,... | collective-permute-start | bytes 417800 | tf_op jit(solution)/shard_map/ppermute | solution.py:340
  151.8 18.2 %collective-permute-start.34 = (f32[256,256]{1,0:T(8,128)}, f32[256,256]{1,0:T(8,128)}, u32[]{:S(2)}, u32[]{:S(2)}) collective-permute-start(f32[256,256]{1,0:T(8,128)} %constant_dynamic-slice_fusion), channel_id=1, source_target_pairs={{0,16},{8,24},{16,0},{24,8},{1,17},{9,25},{17,1},{25,9},{2,18},{10... | collective-permute-start | bytes 786440 | tf_op jit(solution)/shard_map/ppermute | solution.py:373
  (47 other events, 335.2 us)

commit v2 on v0

--- a/solution.py
+++ b/solution.py
@@ -1,9 +1,559 @@
+import functools
 import math
 
 import jax
 import jax.numpy as jnp
+import numpy as np
 from jax import lax
+from jax.experimental import pallas as pl
+from jax.experimental.pallas import tpu as pltpu
 from jax.sharding import PartitionSpec as P
+
+VMEM_LIMIT = 56 * 1024 * 1024
+STEP = 128
+
+
+def params():
+    return pltpu.CompilerParams(vmem_limit_bytes=VMEM_LIMIT)
+
+
+def cost(flops, moved):
+    return pl.CostEstimate(flops=flops, bytes_accessed=moved, transcendentals=0)
+
+
+def odd_tables(size):
+    freq = 2 * np.arange(size, dtype=np.int64)[:, None] + 1
+    spot = np.arange(size, dtype=np.int64)[None, :]
+    theta = (freq * spot % (4 * size)).astype(np.float64) * (2.0 * math.pi / (4 * size))
+    full = np.concatenate([np.cos(theta), -np.sin(theta)], axis=0).astype(np.float32)
+    high = full.astype(jnp.bfloat16)
+    low = (full - high.astype(np.float32)).astype(jnp.bfloat16)
+    return high, low
+
+
+def dot(a, b):
+    return jnp.dot(a, b, preferred_element_type=jnp.float32)
+
+
+def conv_rows(x_ref, before_ref, taps_ref):
+    rows = x_ref.shape[0]
+    ext = jnp.concatenate([before_ref[...].astype(jnp.float32), x_ref[...].astype(jnp.float32)], axis=0)
+    return (
+        taps_ref[0:1] * ext[2 : 2 + rows]
+        + taps_ref[1:2] * ext[1 : 1 + rows]
+        + taps_ref[2:3] * ext[:rows]
+    )
+
+
+def gate_kernel(hc, crossing, m_ref, q_ref, k_ref, v_ref, bq_ref, bk_ref, bv_ref, tq_ref, tk_ref, tv_ref, go_ref, *outs):
+    step = pl.program_id(0)
+    query = conv_rows(q_ref, bq_ref, tq_ref)
+    key = conv_rows(k_ref, bk_ref, tk_ref)
+    value = conv_rows(v_ref, bv_ref, tv_ref)
+    gated = (key * value).astype(jnp.bfloat16)
+    grad = (go_ref[...].astype(jnp.float32) * query).astype(jnp.bfloat16)
+    cols = gated.shape[1]
+    for j in range(hc):
+
+        @pl.when(step == j)
+        def _(j=j):
+            outs[j][:, :cols] = gated
+            outs[j][:, cols:] = grad
+
+        if crossing:
+
+            @pl.when((step == j) & (m_ref[1] == 0))
+            def _(j=j):
+                outs[hc + j][...] = gated
+
+            @pl.when((step == j) & (m_ref[1] == 1))
+            def _(j=j):
+                outs[hc + j][...] = grad
+
+
+def block_at(region, count, base):
+    return lambda k, m: (0, region * count + (m[0] ^ (k + base)))
+
+
+def gate(place, feats, before, taps, grad_out, count, cols, base):
+    rows = feats.shape[0]
+    hc = count // 2
+    crossing = base > 0
+
+    def at(region):
+        return block_at(region, count, base)
+
+    shapes = [jax.ShapeDtypeStruct((rows, 2 * cols), jnp.bfloat16)] * hc
+    if crossing:
+        shapes = shapes + [jax.ShapeDtypeStruct((rows, cols), jnp.bfloat16)] * hc
+    spec = pltpu.PrefetchScalarGridSpec(
+        num_scalar_prefetch=1,
+        grid=(hc,),
+        in_specs=[pl.BlockSpec((rows, cols), at(r)) for r in range(3)]
+        + [pl.BlockSpec((before.shape[0], cols), at(r)) for r in range(3)]
+        + [pl.BlockSpec((3, cols), at(r)) for r in range(3)]
+        + [pl.BlockSpec((rows, cols), at(0))],
+        out_specs=[pl.BlockSpec(s.shape, lambda k, m: (0, 0)) for s in shapes],
+    )
+    return pl.pallas_call(
+        functools.partial(gate_kernel, hc, crossing),
+        grid_spec=spec,
+        out_shape=shapes,
+        compiler_params=params(),
+        cost_estimate=cost(20 * rows * cols * hc, 12 * rows * cols * hc),
+        name="gate_other" if crossing else "gate_home",
+    )(place, feats, feats, feats, before, before, before, taps, taps, taps, grad_out)
+
+
+def signs(first, rows):
+    odd = (lax.broadcasted_iota(jnp.int32, (rows, 1), 0) + first) % 2
+    return 1.0 - 2.0 * odd.astype(jnp.float32)
+
+
+def filter_home_kernel(scale, filt_ref, high_ref, low_ref, near_ref, far_ref):
+    size = filt_ref.shape[0] // 2
+
+    def spectrum(part):
+        now = part * scale
+        high = now.astype(jnp.bfloat16)
+        low = (now - high.astype(jnp.float32)).astype(jnp.bfloat16)
+        return dot(high_ref[...], high) + dot(high_ref[...], low) + dot(low_ref[...], high)
+
+    near = spectrum(filt_ref[:size, :])
+    far = spectrum(filt_ref[size:, :])
+    near_ref[...] = near
+    sign = signs(0, size)
+    far_ref[:size, :] = far[:size] - sign * near[size:]
+    far_ref[size:, :] = far[size:] + sign * near[:size]
+
+
+def filter_home(filt, high, low, scale):
+    length, cols = filt.shape
+    out = jax.ShapeDtypeStruct((length, cols), jnp.float32)
+    return pl.pallas_call(
+        functools.partial(filter_home_kernel, scale),
+        out_shape=[out, out],
+        compiler_params=params(),
+        cost_estimate=cost(6 * length * length * cols, 12 * length * cols + 2 * length * length),
+        name="filter_home",
+    )(filt, high, low)
+
+
+def filter_other_kernel(filt_ref, high_ref, low_ref, near_ref):
+    near_ref[...] = dot(high_ref[...], filt_ref[...]) + dot(low_ref[...], filt_ref[...])
+
+
+def filter_other(part, high, low):
+    size, cols = part.shape
+    return pl.pallas_call(
+        filter_other_kernel,
+        out_shape=jax.ShapeDtypeStruct((2 * size, cols), jnp.float32),
+        compiler_params=params(),
+        cost_estimate=cost(8 * size * size * cols, 10 * size * cols + 8 * size * size),
+        name="filter_other",
+    )(part, high, low)
+
+
+def times(a_re, a_im, b_re, b_im):
+    return a_re * b_re - a_im * b_im, a_re * b_im + a_im * b_re
+
+
+def conj_times(a_re, a_im, b_re, b_im):
+    return a_re * b_re + a_im * b_im, a_re * b_im - a_im * b_re
+
+
+def spectral_kernel(hc, rows, home, scale, *refs):
+    m_ref, near_ref = refs[:2]
+    refs = refs[2:]
+    far_ref = None
+    if home:
+        far_ref, refs = refs[0], refs[1:]
+    forward_ref, inverse_ref, refs = refs[0], refs[1], refs[2:]
+    pieces, refs = refs[:hc], refs[hc:]
+    crosses = ()
+    if home:
+        crosses, refs = refs[:hc], refs[hc:]
+    outs, refs = refs[:hc], refs[hc:]
+    cross_outs = ()
+    if home:
+        cross_outs, refs = refs[:hc], refs[hc:]
+    corr_send, corr_keep, data, spec, prod, res, piece_sem = refs
+    me, half, core = m_ref[0], m_ref[1], m_ref[2]
+    spot = me % hc
+    size = data.shape[0]
+    cols = near_ref.shape[1]
+
+    def place(j):
+        return pl.ds(pl.multiple_of((spot ^ j) * rows, rows), rows)
+
+    copies = [
+        pltpu.make_async_copy(pieces[j], data.at[place(j), : 2 * cols], piece_sem.at[j]) for j in range(hc)
+    ] + [
+        pltpu.make_async_copy(crosses[j], data.at[place(j), 2 * cols :], piece_sem.at[hc + j])
+        for j in range(len(crosses))
+    ]
+    for copy in copies:
+        copy.start()
+    for copy in copies:
+        copy.wait()
+    for part in range(data.shape[1] // cols):
+        here = slice(part * cols, (part + 1) * cols)
+        spec[:, here] = dot(forward_ref[...], data[:, here])
+
+    def products(side):
+        def body(i, carry):
+            low = pl.ds(pl.multiple_of(i * STEP, STEP), STEP)
+            high = pl.ds(pl.multiple_of(size + i * STEP, STEP), STEP)
+
+            def get(part):
+                here = slice(part * cols, (part + 1) * cols)
+                return spec[low, here], spec[high, here]
+
+            def put(part, value):
+                here = slice(part * cols, (part + 1) * cols)
+                prod[low, here] = value[0].astype(jnp.bfloat16)
+                prod[high, here] = value[1].astype(jnp.bfloat16)
+
+            g, d = get(0), get(1)
+            h = near_ref[low, :], near_ref[high, :]
+            conv = times(*h, *g)
+            grad = conj_times(*h, *d)
+            corr = conj_times(*g, *d)
+            if home:
+                f = far_ref[low, :], far_ref[high, :]
+                gx, dx = (g, get(2)) if side == 0 else (get(2), d)
+                far_conv = times(*f, *gx)
+                far_grad = conj_times(*f, *dx)
+                if side == 0:
+                    grad = (grad[0] + far_grad[0], grad[1] + far_grad[1])
+                else:
+                    conv = (conv[0] + far_conv[0], conv[1] + far_conv[1])
+                put(2, far_conv if side == 0 else far_grad)
+                far_corr = conj_times(*gx, *dx)
+                sign = signs(0, STEP)
+                corr = (corr[0] + sign * far_corr[1], corr[1] - sign * far_corr[0])
+                put(4, far_corr)
+                put(3, corr)
+            else:
+                put(2, corr)
+            put(0, conv)
+            put(1, grad)
+            return carry
+
+        lax.fori_loop(0, size // STEP, body, 0)
+
+    if home:
+
+        @pl.when(half == 0)
+        def _():
+            products(0)
+
+        @pl.when(half == 1)
+        def _():
+            products(1)
+
+    else:
+        products(0)
+
+    def back(part):
+        return dot(inverse_ref[...], prod[:, part * cols : (part + 1) * cols])
+
+    res[:, :cols] = back(0).astype(jnp.bfloat16)
+    res[:, cols : 2 * cols] = back(1).astype(jnp.bfloat16)
+    for j in range(hc):
+        outs[j][...] = res[place(j), : 2 * cols]
+    quarter = size // 2
+
+    def share(which, part):
+        return part[which * quarter : (which + 1) * quarter]
+
+    if home:
+        res[:, 2 * cols :] = back(2).astype(jnp.bfloat16)
+        for j in range(hc):
+            cross_outs[j][...] = res[place(j), 2 * cols :]
+        parts = [back(3) * scale, back(4) * scale]
+    else:
+        parts = [back(2) * scale]
+    for core_now in range(2):
+
+        @pl.when(core == core_now)
+        def _(core_now=core_now):
+            for x, part in enumerate(parts):
+                here = slice(x * quarter, (x + 1) * quarter)
+                corr_keep[here, :] = share(core_now, part)
+                corr_send[here, :] = share(1 - core_now, part)
+
+
+def spectral(place, near, far, forward, inverse, pieces, crosses, scale):
+    hc = len(pieces)
+    rows, width = pieces[0].shape
+    cols = width // 2
+    size = hc * rows
+    home = far is not None
+    vmem = pl.BlockSpec(memory_space=pltpu.VMEM)
+    hbm = pl.BlockSpec(memory_space=pl.ANY)
+    tables = [near, far, forward, inverse] if home else [near, forward, inverse]
+    arrived = [*pieces, *crosses]
+    ins = 3 if home else 2
+    parts = 5 if home else 3
+    shapes = [jax.ShapeDtypeStruct((rows, width), jnp.bfloat16)] * hc
+    if home:
+        shapes = shapes + [jax.ShapeDtypeStruct((rows, cols), jnp.bfloat16)] * hc
+    corr = jax.ShapeDtypeStruct((size if home else size // 2, cols), jnp.float32)
+    return pl.pallas_call(
+        functools.partial(spectral_kernel, hc, rows, home, scale),
+        in_specs=[pl.BlockSpec(memory_space=pltpu.SMEM)] + [vmem] * len(tables) + [hbm] * len(arrived),
+        out_specs=[vmem] * (len(shapes) + 2),
+        out_shape=shapes + [corr, corr],
+        scratch_shapes=[
+            pltpu.VMEM((size, ins * cols), jnp.bfloat16),
+            pltpu.VMEM((2 * size, ins * cols), jnp.float32),
+            pltpu.VMEM((2 * size, parts * cols), jnp.bfloat16),
+            pltpu.VMEM((size, ins * cols), jnp.bfloat16),
+            pltpu.SemaphoreType.DMA((len(arrived),)),
+        ],
+        compiler_params=params(),
+        cost_estimate=cost(4 * size * size * cols * (ins + parts), 8 * size * size + 30 * size * cols),
+        name="spectral_home" if home else "spectral_other",
+    )(place, *tables, *arrived)
+
+
+def final_kernel(hc, count, base, width, aliased, *refs):
+    m_ref = refs[0]
+    k_ref, v_ref, bk_ref, bv_ref, go_ref, tq_ref, tk_ref, tv_ref = refs[1:9]
+    pieces, refs = refs[9 : 9 + hc], refs[9 + hc :]
+    crosses = ()
+    if base > 0:
+        crosses, refs = refs[:hc], refs[hc:]
+    if aliased:
+        refs = refs[1:]
+    out_ref, edge_ref, last_ref, back, stage, in_sem, out_sem = refs
+    step = pl.program_id(0)
+    me, half = m_ref[0], m_ref[1]
+    rows, cols = k_ref.shape
+
+    def in_copies(j):
+        copies = [pltpu.make_async_copy(pieces[j], back.at[j, :, : 2 * cols], in_sem.at[j])]
+        if base > 0:
+            copies.append(pltpu.make_async_copy(crosses[j], back.at[j, :, 2 * cols :], in_sem.at[hc + j]))
+        return copies
+
+    @pl.when(step == 0)
+    def _():
+        for j in range(hc):
+            for copy in in_copies(j):
+                copy.start()
+
+    def out_copy(j, region):
+        col = pl.multiple_of(region * width + (me ^ (j + base)) * cols, cols)
+        return pltpu.make_async_copy(
+            stage.at[j, region], out_ref.at[:, pl.ds(col, cols)], out_sem.at[j, region]
+        )
+
+    def unmixed(region, dz, taps):
+        ext = jnp.concatenate([dz, jnp.zeros((8, cols), jnp.float32)], axis=0)
+        out = taps[0:1] * dz + taps[1:2] * ext[1 : rows + 1] + taps[2:3] * ext[2 : rows + 2]
+        edge_ref[0, region] = dz[:2].astype(jnp.bfloat16)
+        last_ref[0, region] = out[rows - 16 :]
+        stage[step, region] = out.astype(jnp.bfloat16)
+
+    key = conv_rows(k_ref, bk_ref, tk_ref)
+    value = conv_rows(v_ref, bv_ref, tv_ref)
+    for j in range(hc):
+
+        @pl.when(step == j)
+        def _(j=j):
+            for copy in in_copies(j):
+                copy.wait()
+
+    conv = back[step, :, :cols].astype(jnp.float32)
+    grad = back[step, :, cols : 2 * cols].astype(jnp.float32)
+    if base > 0:
+        extra = back[step, :, 2 * cols :].astype(jnp.float32)
+        conv = jnp.where(half == 1, conv + extra, conv)
+        grad = jnp.where(half == 0, grad + extra, grad)
+    unmixed(0, go_ref[...].astype(jnp.float32) * conv, tq_ref)
+    unmixed(1, grad * value, tk_ref)
+    unmixed(2, grad * key, tv_ref)
+    for region in range(3):
+        out_copy(step, region).start()
+
+    @pl.when(step == hc - 1)
+    def _():
+        for j in range(hc):
+            for region in range(3):
+                out_copy(j, region).wait()
+
+
+def final(place, feats, before, grad_out, taps, pieces, crosses, so_far, count, base):
+    hc = len(pieces)
+    rows = feats.shape[0]
+    cols = pieces[0].shape[1] // 2
+    width = count * cols
+
+    def at(region):
+        return block_at(region, count, base)
+
+    hbm = pl.BlockSpec(memory_space=pl.ANY)
+    arrived = [*pieces, *crosses]
+    in_specs = (
+        [pl.BlockSpec((rows, cols), at(r)) for r in (1, 2)]
+        + [pl.BlockSpec((before.shape[0], cols), at(r)) for r in (1, 2)]
+        + [pl.BlockSpec((rows, cols), at(0))]
+        + [pl.BlockSpec((3, cols), at(r)) for r in range(3)]
+        + [hbm] * len(arrived)
+    )
+    args = [place, feats, feats, before, before, grad_out, taps, taps, taps, *arrived]
+    aliases = {}
+    if so_far is not None:
+        in_specs.append(hbm)
+        args.append(so_far)
+        aliases = {len(args) - 1: 0}
+
+    def own(k, m):
+        return ((m[0] ^ k) % hc, 0, 0, 0)
+
+    return pl.pallas_call(
+        functools.partial(final_kernel, hc, count, base, width, so_far is not None),
+        grid_spec=pltpu.PrefetchScalarGridSpec(
+            num_scalar_prefetch=1,
+            grid=(hc,),
+            in_specs=in_specs,
+            out_specs=[
+                hbm,
+                pl.BlockSpec((1, 3, 2, cols), own),
+                pl.BlockSpec((1, 3, 16, cols), own),
+            ],
+            scratch_shapes=[
+                pltpu.VMEM((hc, rows, (3 if base > 0 else 2) * cols), jnp.bfloat16),
+                pltpu.VMEM((hc, 3, rows, cols), jnp.bfloat16),
+                pltpu.SemaphoreType.DMA((len(arrived),)),
+                pltpu.SemaphoreType.DMA((hc, 3)),
+            ],
+        ),
+        out_shape=[
+            jax.ShapeDtypeStruct((rows, 3 * width), jnp.bfloat16),
+            jax.ShapeDtypeStruct((hc, 3, 2, cols), jnp.bfloat16),
+            jax.ShapeDtypeStruct((hc, 3, 16, cols), jnp.float32),
+        ],
+        input_output_aliases=aliases,
+        compiler_params=params(),
+        cost_estimate=cost(30 * rows * cols * hc, 16 * rows * cols * hc),
+        name="final_other" if base > 0 else "final_home",
+    )(*args)
+
+
+def fix_kernel(hc, m_ref, taps_ref, eh_ref, eo_ref, lh_ref, lo_ref, _, out_ref, stage, sem):
+    me, half = m_ref[0], m_ref[1]
+    cols = eh_ref.shape[3]
+    width = out_ref.shape[1] // 3
+    turn = me == hc - 1
+    spot = lax.broadcasted_iota(jnp.int32, (16, 1), 0)
+    for slot, last in enumerate((lh_ref, lo_ref)):
+        mine, swapped = (eh_ref, eo_ref) if slot == 0 else (eo_ref, eh_ref)
+        first = jnp.where(half == slot, 0, hc)
+        for j in range(hc):
+            for region in range(3):
+                col = pl.ds(pl.multiple_of(region * width + (first + j) * cols, cols), cols)
+                ahead = jnp.where(
+                    turn, swapped[j, region].astype(jnp.float32), mine[j, region].astype(jnp.float32)
+                )
+                one, two = taps_ref[1:2, col], taps_ref[2:3, col]
+                add = jnp.where(
+                    spot == 14,
+                    two * ahead[0:1],
+                    jnp.where(spot == 15, one * ahead[0:1] + two * ahead[1:2], 0.0),
+                )
+                stage[:, col] = (last[j, region] + add).astype(jnp.bfloat16)
+    copy = pltpu.make_async_copy(stage, out_ref.at[pl.ds(out_ref.shape[0] - 16, 16)], sem)
+    copy.start()
+    copy.wait()
+
+
+def fix(place, taps, edge_home, edge_other, last_home, last_other, result):
+    hc = edge_home.shape[0]
+    vmem = pl.BlockSpec(memory_space=pltpu.VMEM)
+    hbm = pl.BlockSpec(memory_space=pl.ANY)
+    return pl.pallas_call(
+        functools.partial(fix_kernel, hc),
+        in_specs=[pl.BlockSpec(memory_space=pltpu.SMEM)] + [vmem] * 5 + [hbm],
+        out_specs=hbm,
+        out_shape=jax.ShapeDtypeStruct(result.shape, result.dtype),
+        scratch_shapes=[pltpu.VMEM((16, result.shape[1]), jnp.bfloat16), pltpu.SemaphoreType.DMA],
+        input_output_aliases={6: 0},
+        compiler_params=params(),
+        cost_estimate=cost(16 * 8 * result.shape[1], 128 * result.shape[1]),
+        name="fix",
+    )(place, taps, edge_home, edge_other, last_home, last_other, result)
+
+
+def exchange(pieces, base):
+    devices = range(lax.axis_size("ctx"))
+    return [
+        piece if base + j == 0 else lax.ppermute(piece, "ctx", [(i, i ^ (base + j)) for i in devices])
+        for j, piece in enumerate(pieces)
+    ]
+
+
+def half_shards(feats, short_weight, grad_out, filt):
+    length, block = filt.shape
+    count = lax.axis_size("ctx")
+    hc = count // 2
+    size = length // 2
+    quarter = length // 4
+    feats, grad_out = feats[0], grad_out[0]
+    rows = feats.shape[0]
+    high, low = odd_tables(size)
+    inverse = np.ascontiguousarray(high.T)
+    scale = 1.0 / (math.sqrt(length) * size)
+    me = lax.axis_index("ctx")
+    dp = lax.axis_index("dp")
+    core, x = dp % 2, dp // 2
+    place = jnp.stack([me, me // hc, core]).astype(jnp.int32)
+    before = from_behind(feats[rows - 2 :], "ctx", 1)
+
+    share = size // 4
+    part = (lax.dynamic_slice_in_dim(filt, dp * share, share, 0) * scale).astype(jnp.bfloat16)
+    part = lax.ppermute(part, "ctx", [(i, i ^ hc) for i in range(count)])
+    part = lax.all_gather(part, "dp", axis=0, tiled=True)
+
+    near, far = filter_home(filt, high, low, scale)
+    gated = gate(place, feats, before, short_weight, grad_out, count, block, hc)
+    home_pieces = gate(place, feats, before, short_weight, grad_out, count, block, 0)
+    home_pieces = exchange(home_pieces, 0)
+    crosses = exchange(gated[hc:], hc)
+    other_pieces = exchange(gated[:hc], 0)
+    near_other = filter_other(part, high, low)
+
+    outs = spectral(place, near, far, high, inverse, home_pieces, crosses, scale)
+    home_back = exchange(outs[:hc], 0)
+    cross_back = exchange(outs[hc : 2 * hc], hc)
+    send, keep = outs[2 * hc :]
+    summed = keep + lax.ppermute(send, "dp", [(i, i ^ 1) for i in range(4)])
+    there = lax.dynamic_slice_in_dim(summed, (1 - x) * quarter, quarter, 0).astype(jnp.bfloat16)
+    here = lax.dynamic_slice_in_dim(summed, x * quarter, quarter, 0)
+    filt_home = here + lax.ppermute(there, "dp", [(i, i ^ 2) for i in range(4)]).astype(jnp.float32)
+
+    outs = spectral(place, near_other, None, high, inverse, other_pieces, (), scale)
+    other_back = exchange(outs[:hc], 0)
+    send, keep = outs[hc:]
+    summed = keep + lax.ppermute(send, "dp", [(i, i ^ 1) for i in range(4)])
+    summed = summed + lax.ppermute(summed.astype(jnp.bfloat16), "dp", [(2, 0), (3, 1)]).astype(jnp.float32)
+    owners = [(d * count + i, d * count + (i ^ hc)) for d in range(2) for i in range(count)]
+    filt_other = lax.ppermute(summed.astype(jnp.bfloat16), ("dp", "ctx"), owners).astype(jnp.float32)
+    filt_out = filt_home + filt_other
+
+    result, edge_home, last_home = final(
+        place, feats, before, grad_out, short_weight, home_back, (), None, count, 0
+    )
+    result, edge_other, last_other = final(
+        place, feats, before, grad_out, short_weight, other_back, cross_back, result, count, hc
+    )
+    edge_home = from_behind(edge_home, "ctx", -1)
+    edge_other = from_behind(edge_other, "ctx", -1)
+    result = fix(place, short_weight, edge_home, edge_other, last_home, last_other, result)
+    return (result[None], filt_out)
+
 
 full_precision = lax.Precision.HIGHEST
 split_precision = lax.Precision.HIGH
@@ -85,7 +635,7 @@
     return signal.reshape(length, signal.shape[2]) / (2.0 * length)
 
 
-def spectral(gated_sig, grad_sig, filter_cols, tables, length):
+def long_spectral(gated_sig, grad_sig, filter_cols, tables, length):
     g_spec = data_forward(gated_sig, tables, split_precision)
     d_spec = data_forward(grad_sig, tables, split_precision)
     h_spec = filter_forward(filter_cols, tables)
@@ -103,7 +653,7 @@
     return (conv_out, gated_grad, filt_grad)
 
 
-def shards(feats, short_weight, grad_out, filt):
+def long_shards(feats, short_weight, grad_out, filt):
     rows = feats.shape[1]
     width = feats.shape[2] // 3
     length = filt.shape[0]
@@ -150,7 +700,7 @@
     wide_grad = wide_grad.reshape(replicas, narrow, length)
     offset = lax.axis_index("dp") * narrow
     filt_cols = lax.dynamic_slice_in_dim(filt, offset, narrow, 1)
-    conv_out, gated_grad, filt_grad = spectral(
+    conv_out, gated_grad, filt_grad = long_spectral(
         wide_gated, wide_grad, filt_cols * scale_inv, tables, length
     )
     back_conv, back_grad = (
@@ -210,6 +760,22 @@
     return (grad_in.astype(jnp.bfloat16), filt_out)
 
 
+def shards(feats, short_weight, grad_out, filt):
+    count = lax.axis_size("ctx")
+    length, block = filt.shape
+    fits = (
+        length <= 1024
+        and length % (4 * STEP) == 0
+        and count > 1
+        and count & (count - 1) == 0
+        and feats.shape[1] % 128 == 0
+        and block % 128 == 0
+        and lax.axis_size("dp") == 4
+    )
+    plan = half_shards if fits else long_shards
+    return plan(feats, short_weight, grad_out, filt)
+
+
 def solution(mesh):
     return jax.shard_map(
         shards,

time: 356 us -> 156 us (0.44); the launches traced: 352 us -> 156 us
  matrix products: 82.3 us -> 0 us
  waiting for transfers between devices: 105 us -> 27.7 us
  Pallas kernels: 0 us -> 62.6 us
  other arithmetic: 65 us -> 4.26 us
  local copies, waits for them, and re-layouts: 54.9 us -> 4.69 us
  blocking collectives: 0 us -> 7.61 us
  starting transfers between devices: 43.2 us -> 47.7 us
    all_to_all x9 -> x0, waiting for transfers between devices: 102 us -> none  [the longest x1 23.9 us: shards(): lax.all_to_all(lax.all_to_all(gated_grad.astype(jnp.bfloat16)[None, None]...]
    dot_general x12 -> x0, matrix products: 82.3 us -> none  [the longest x2 26.2 us: data_inverse(): jnp.einsum('sckrb,rknb->scnb', partial_sig, tables[0], precision=full_pre...]
    pallas_call x0 -> x9, Pallas kernels: none -> 62.6 us  [the longest x2 21.9 us: spectral(): pl.pallas_call(functools.partial(spectral_kernel, hc, rows, home, scale),...]
    ppermute x0 -> x26, starting transfers between devices: none -> 40.3 us  [the longest x20 32.6 us: exchange(): lax.ppermute(piece, 'ctx', [(i, i ^ base + j) for i in devices])]
    all_to_all x9 -> x0, starting transfers between devices: 37 us -> none  [the longest x1 4.88 us: shards(): lax.all_to_all(lax.all_to_all(spread(gated), 'dp', split_axis=1, concat_a...]
    ppermute x0 -> x26, waiting for transfers between devices: none -> 23.1 us  [the longest x20 23.1 us: exchange(): lax.ppermute(piece, 'ctx', [(i, i ^ base + j) for i in devices])]
    convert_element_type x5 -> x3, other arithmetic: 20.6 us -> 2.55 us  [the longest x2 1.57 us: half_shards(): summed.astype(jnp.bfloat16)]
    all_to_all x9 -> x0, local copies, waits for them, and re-layouts: 14.9 us -> none  [the longest x1 3.01 us: shards(): lax.all_to_all(gated_grad.astype(jnp.bfloat16)[None, None], 'dp', split_a...]
  transfers between devices with their start and end apart: 11 -> 29, of which waited for: 8 -> 9; matrix products, arithmetic and copies ran while one was open for 29% -> 2% of each run, Pallas kernels for 0% -> 40%
where the time goes in v2:
time: 156 us
  Pallas kernels  62.6 us (40%)
  starting transfers between devices  47.7 us (31%)
  waiting for transfers between devices  27.7 us (18%)
  blocking collectives  7.61 us (5%)
  local copies, waits for them, and re-layouts  4.69 us (3%)
  other arithmetic  4.26 us (3%)
    ppermute x20, starting transfers between devices, exchange(): lax.ppermute(piece, 'ctx', [(i, i ^ base + j) for i in devices])  32.6 us
    ppermute x20, waiting for transfers between devices, exchange(): lax.ppermute(piece, 'ctx', [(i, i ^ base + j) for i in devices])  23.1 us
    pallas_call x2, Pallas kernels, spectral(): pl.pallas_call(functools.partial(spectral_kernel, hc, rows, home, scale),...  21.9 us
    pallas_call x2, Pallas kernels, final(): pl.pallas_call(functools.partial(final_kernel, hc, count, base, width, so...  15.4 us
    pallas_call x2, Pallas kernels, gate(): pl.pallas_call(functools.partial(gate_kernel, hc, crossing), grid_spec=sp...  12 us
    all_gather x1, blocking collectives, half_shards(): part = lax.all_gather(part, 'dp', axis=0, tiled=True)  7.61 us
    ppermute x3, starting transfers between devices, from_behind(): return lax.ppermute(block, axis, route)  7.46 us
    pallas_call x1, Pallas kernels, filter_home(): pl.pallas_call(functools.partial(filter_home_kernel, scale), out_shape=[o...  6.96 us
  transfers between devices with their start and end apart: 29, of which 9 were waited for; matrix products, arithmetic and copies ran while one was open for 2% of the time, Pallas kernels for 40%

profile of v2, /device:TPU:0, one launch (start us, length us, event | category | flops | bytes accessed | tf_op | source)
XLA Modules:
  0.0 155.7 jit_solution(5486572887931123419)
XLA Ops:
  1.6 4.9 %collective-permute-start = (bf16[2,12288]{1,0:T(2,128)(2,1)S(1)}, bf16[2,12288]{1,0:T(2,128)(2,1)S(1)}, u32[]{:S(2)}, u32[]{:S(2)}) collective-permute-start(bf16[2,12288]{1,0:T(2,128)(2,1)S(1)} %slice_bitcast_fusion), channel_id=1, source_target_pairs={{0,1},{1,2},{2,3},{3,4},{4,5},{5,6},{6,7},{8,9},{9,10},{10,11},{11... | collective-permute-start | bytes 147464 | tf_op jit(solution)/shard_map/ppermute | solution.py:565
  7.5 2.7 %collective-permute-start.12 = (bf16[128,512]{1,0:T(8,128)(2,1)S(1)}, bf16[128,512]{1,0:T(8,128)(2,1)S(1)}, u32[]{:S(2)}, u32[]{:S(2)}) collective-permute-start(bf16[128,512]{1,0:T(8,128)(2,1)S(1)} %multiply_convert_fusion), channel_id=1, source_target_pairs={{0,4},{1,5},{2,6},{3,7},{4,0},{5,1},{6,2},{7,3},{8,12},{9,13},{10,... | collective-permute-start | bytes 393224 | tf_op jit(solution)/shard_map/ppermute | solution.py:517
  11.4 6.2 %gate_other.1 = (bf16[128,1024]{1,0:T(8,128)(2,1)}, bf16[128,1024]{1,0:T(8,128)(2,1)}, bf16[128,1024]{1,0:T(8,128)(2,1)}, bf16[128,1024]{1,0:T(8,128)(2,1)}, bf1...) custom-call(s32[3]{0:T(128)} %pad_add_fusion.m_ref.refs_0_, ...), custom_call_target="tpu_custom_call" | custom-call | flops 5242880 | bytes 3145728 | tf_op jit(solution)/shard_map/gate_other/pallas_call | solution.py:98
  19.2 7.0 %filter_home.1 = (f32[1024,512]{1,0:T(8,128)}, f32[1024,512]{1,0:T(8,128)}) custom-call(f32[1024,512]{1,0:T(8,128)} %filt_ref.1, bf16[1024,512]{1,0:T(8,128)(2,1)} %constant.60.clone.high_ref.refs_3_.refs_2_, bf16[1024,512]{1,0:T(8,128)(2,1)} %constant.61.clone.low_ref), custom_call_target="tpu_custom_call" | custom-call | flops 3221225472 | bytes 8388608 | tf_op jit(solution)/shard_map/filter_home/pallas_call | solution.py:133
  27.0 2.0 %collective-permute-start.5 = (bf16[128,512]{1,0:T(8,128)(2,1)S(1)}, bf16[128,512]{1,0:T(8,128)(2,1)S(1)}, u32[]{:S(2)}, u32[]{:S(2)}) collective-permute-start(bf16[128,512]{1,0:T(8,128)(2,1)S(1)} %copy-done.32), channel_id=1, source_target_pairs={{0,5},{1,4},{2,7},{3,6},{4,1},{5,0},{6,3},{7,2},{8,13},{9,12},{10,... | collective-permute-start | bytes 393224 | tf_op jit(solution)/shard_map/ppermute | solution.py:493
  29.0 2.2 %collective-permute-start.14 = (bf16[128,1024]{1,0:T(8,128)(2,1)S(1)}, bf16[128,1024]{1,0:T(8,128)(2,1)S(1)}, u32[]{:S(2)}, u32[]{:S(2)}) collective-permute-start(bf16[128,1024]{1,0:T(8,128)(2,1)S(1)} %copy-done.24), channel_id=1, source_target_pairs={{0,2},{1,3},{2,0},{3,1},{4,6},{5,7},{6,4},{7,5},{8,10},{9,11},{10,... | collective-permute-start | bytes 786440 | tf_op jit(solution)/shard_map/ppermute | solution.py:493
  31.2 5.8 %gate_home.1 = (bf16[128,1024]{1,0:T(8,128)(2,1)}, bf16[128,1024]{1,0:T(8,128)(2,1)}, bf16[128,1024]{1,0:T(8,128)(2,1)}, bf16[128,1024]{1,0:T(8,128)(2,1)}) custom-call(s32[3]{0:T(128)} %pad_add_fusion.m_ref.refs_0_, bf16[128,12288]{1,0:T(8,128)(2,1)} %bitcast.11, bf16[128,12288]{1,0:T(8,128)(2,1)} %bitcast.12, bf16[128,12288]{1,0:T(8,128)(2,1)} %bitcast.13, ...), custom_call_target="tpu_custom_call" | custom-call | flops 5242880 | bytes 3145728 | tf_op jit(solution)/shard_map/gate_home/pallas_call | solution.py:98
  37.9 7.6 %all_gather.3.filt_ref = bf16[512,512]{1,0:T(8,128)(2,1)} all-gather(bf16[128,512]{1,0:T(8,128)(2,1)S(1)} %collective-permute-done.12), channel_id=1, replica_groups=mesh['dp'=4,'ctx'=8] {'dp'}, dimensions={0}, use_global_device_ids=true | all-gather | bytes 655360 | tf_op jit(solution)/shard_map/all_gather | solution.py:518
  49.0 4.3 %filter_other.1.refs_1_ = f32[1024,512]{1,0:T(8,128)} custom-call(bf16[512,512]{1,0:T(8,128)(2,1)} %all_gather.3.filt_ref, bf16[1024,512]{1,0:T(8,128)(2,1)} %constant.60.clone.high_ref.refs_3_.refs_2_, bf16[1024,512]{1,0:T(8,128)(2,1)} %constant.61.clone.low_ref), custom_call_target="tpu_custom_call" | custom-call | flops 1073741824 | bytes 4718592 | tf_op jit(solution)/shard_map/filter_other/pallas_call | solution.py:148
  53.3 3.1 %collective-permute-start.6 = (bf16[128,512]{1,0:T(8,128)(2,1)S(1)}, bf16[128,512]{1,0:T(8,128)(2,1)S(1)}, u32[]{:S(2)}, u32[]{:S(2)}) collective-permute-start(bf16[128,512]{1,0:T(8,128)(2,1)S(1)} %copy-done.29), channel_id=1, source_target_pairs={{0,6},{1,7},{2,4},{3,5},{4,2},{5,3},{6,0},{7,1},{8,14},{9,15},{10,... | collective-permute-start | bytes 393224 | tf_op jit(solution)/shard_map/ppermute | solution.py:493
  57.9 8.8 %spectral_other.1 = (bf16[128,1024]{1,0:T(8,128)(2,1)}, bf16[128,1024]{1,0:T(8,128)(2,1)}, bf16[128,1024]{1,0:T(8,128)(2,1)}, bf16[128,1024]{1,0:T(8,128)(2,1)}, f32[256,512]{1,0:T(8,128)}, /*index=5*/f32[256,512]{1,0:T(8,128)}) custom-call(s32[3]{0:T(128)} %pad_add_fusion.m_ref.refs_0_, f32[1024,512]{1,0:T(8,128)} %filter_other.1.refs_1_, ...), custom_call_target="tpu_custom_call" | custom-call | flops 2684354560 | bytes 9961472 | tf_op jit(solution)/shard_map/spectral_other/pallas_call | solution.py:303
  69.8 13.2 %spectral_home.1 = (bf16[128,1024]{1,0:T(8,128)(2,1)}, bf16[128,1024]{1,0:T(8,128)(2,1)}, bf16[128,1024]{1,0:T(8,128)(2,1)}, bf16[128,1024]{1,0:T(8,128)(2,1)}, ...) custom-call(s32[3]{0:T(128)} %pad_add_fusion.m_ref.refs_0_, ...), custom_call_target="tpu_custom_call" | custom-call | flops 4294967296 | bytes 9961472 | tf_op jit(solution)/shard_map/spectral_home/pallas_call | solution.py:303
  86.5 3.9 %collective-permute-start.20 = (bf16[128,512]{1,0:T(8,128)(2,1)}, bf16[128,512]{1,0:T(8,128)(2,1)S(1)}, u32[]{:S(2)}, u32[]{:S(2)}) collective-permute-start(bf16[128,512]{1,0:T(8,128)(2,1)} %get-tuple-element.62), channel_id=1, source_target_pairs={{0,5},{1,4},{2,7},{3,6},{4,1},{5,0},{6,3},{7,2},{8,13},{9,12},{10,... | collective-permute-start | bytes 393224 | tf_op jit(solution)/shard_map/ppermute | solution.py:493
  90.3 6.7 %collective-permute-done.19.refs_13_ = bf16[128,512]{1,0:T(8,128)(2,1)S(1)} collective-permute-done((bf16[128,512]{1,0:T(8,128)(2,1)}, bf16[128,512]{1,0:T(8,128)(2,1)S(1)}, u32[]{:S(2)}, u32[]{:S(2)}) %collective-permute-start.19) | collective-permute-done | bytes 131104 | tf_op jit(solution)/shard_map/ppermute | solution.py:493
  97.0 3.0 %collective-permute-start.21 = (bf16[128,512]{1,0:T(8,128)(2,1)}, bf16[128,512]{1,0:T(8,128)(2,1)S(1)}, u32[]{:S(2)}, u32[]{:S(2)}) collective-permute-start(bf16[128,512]{1,0:T(8,128)(2,1)} %get-tuple-element.63), channel_id=1, source_target_pairs={{0,6},{1,7},{2,4},{3,5},{4,2},{5,3},{6,0},{7,1},{8,14},{9,15},{10,... | collective-permute-start | bytes 393224 | tf_op jit(solution)/shard_map/ppermute | solution.py:493
  101.0 2.7 %collective-permute-start.22 = (bf16[128,512]{1,0:T(8,128)(2,1)}, bf16[128,512]{1,0:T(8,128)(2,1)S(1)}, u32[]{:S(2)}, u32[]{:S(2)}) collective-permute-start(bf16[128,512]{1,0:T(8,128)(2,1)} %get-tuple-element.64), channel_id=1, source_target_pairs={{0,7},{1,6},{2,5},{3,4},{4,3},{5,2},{6,1},{7,0},{8,15},{9,14},{10,... | collective-permute-start | bytes 393224 | tf_op jit(solution)/shard_map/ppermute | solution.py:493
  103.8 3.1 %collective-permute-start.10 = (bf16[128,1024]{1,0:T(8,128)(2,1)}, bf16[128,1024]{1,0:T(8,128)(2,1)S(1)}, u32[]{:S(2)}, u32[]{:S(2)}) collective-permute-start(bf16[128,1024]{1,0:T(8,128)(2,1)} %get-tuple-element.51), channel_id=1, source_target_pairs={{0,3},{1,2},{2,1},{3,0},{4,7},{5,6},{6,5},{7,4},{8,11},{9,10},{10,... | collective-permute-start | bytes 786440 | tf_op jit(solution)/shard_map/ppermute | solution.py:493
  110.3 2.5 %collective-permute-start.17 = (bf16[128,1024]{1,0:T(8,128)(2,1)S(1)}, bf16[128,1024]{1,0:T(8,128)(2,1)S(1)}, u32[]{:S(2)}, u32[]{:S(2)}) collective-permute-start(bf16[128,1024]{1,0:T(8,128)(2,1)S(1)} %copy-done.16), channel_id=1, source_target_pairs={{0,2},{1,3},{2,0},{3,1},{4,6},{5,7},{6,4},{7,5},{8,10},{9,11},{10,... | collective-permute-start | bytes 786440 | tf_op jit(solution)/shard_map/ppermute | solution.py:493
  114.2 3.7 %collective-permute-start.28 = (bf16[256,512]{1,0:T(8,128)(2,1)}, bf16[256,512]{1,0:T(8,128)(2,1)S(1)}, u32[]{:S(2)}, u32[]{:S(2)}) collective-permute-start(bf16[256,512]{1,0:T(8,128)(2,1)} %add_convert_fusion), channel_id=1, source_target_pairs={{0,4},{1,5},{2,6},{3,7},{4,0},{5,1},{6,2},{7,3},{8,12},{9,13},{10,... | collective-permute-start | bytes 786440 | tf_op jit(solution)/shard_map/ppermute | solution.py:543
  117.9 8.5 %collective-permute-done.10.refs_12_ = bf16[128,1024]{1,0:T(8,128)(2,1)S(1)} collective-permute-done((bf16[128,1024]{1,0:T(8,128)(2,1)}, bf16[128,1024]{1,0:T(8,128)(2,1)S(1)}, u32[]{:S(2)}, u32[]{:S(2)}) %collective-permute-start.10) | collective-permute-done | bytes 262176 | tf_op jit(solution)/shard_map/ppermute | solution.py:493
  127.1 7.6 %final_home.1 = (bf16[128,12288]{1,0:T(8,128)(2,1)}, bf16[4,3,2,512]{3,2,1,0:T(2,128)(2,1)}, f32[4,3,16,512]{3,2,1,0:T(8,128)}) custom-call(s32[3]{0:T(128)} %pad_add_fusion.m_ref.refs_0_, bf16[128,12288]{1,0:T(8,128)(2,1)} %bitcast.14, bf16[128,12288]{1,0:T(8,128)(2,1)} %bitcast.15, bf16[2,12288]{1,0:T(2,128)(2,1)} %copy-done, bf16[2,12288]{1,0:T(2,128)(2,1)} %copy-done, ...), custom_call_target="tpu_custom_call" | custom-call | flops 7864320 | bytes 4194304 | tf_op jit(solution)/shard_map/final_home/pallas_call | solution.py:416
  138.4 7.8 %final_other.1 = (bf16[128,12288]{1,0:T(8,128)(2,1)}, bf16[4,3,2,512]{3,2,1,0:T(2,128)(2,1)}, f32[4,3,16,512]{3,2,1,0:T(8,128)}) custom-call(s32[3]{0:T(128)} %pad_add_fusion.m_ref.refs_0_, bf16[128,12288]{1,0:T(8,128)(2,1)} %bitcast.16, bf16[128,12288]{1,0:T(8,128)(2,1)} %bitcast.17, bf16[2,12288]{1,0:T(2,128)(2,1)} %copy-done, ...), custom_call_target="tpu_custom_call", output_to_operand_aliasing={{0}: (17, {})} | custom-call | flops 7864320 | bytes 4194304 | tf_op jit(solution)/shard_map/final_other/pallas_call | solution.py:416
  147.5 4.6 %collective-permute-done.23.eo_ref = bf16[4,3,2,512]{3,2,1,0:T(2,128)(2,1)S(1)} collective-permute-done((bf16[4,3,2,512]{3,2,1,0:T(2,128)(2,1)}, bf16[4,3,2,512]{3,2,1,0:T(2,128)(2,1)S(1)}, u32[]{:S(2)}, u32[]{:S(2)}) %collective-permute-start.23) | collective-permute-done | bytes 24608 | tf_op jit(solution)/shard_map/ppermute | solution.py:565
  152.7 2.1 %fix.1 = bf16[128,12288]{1,0:T(8,128)(2,1)} custom-call(s32[3]{0:T(128)} %pad_add_fusion.m_ref.refs_0_, f32[3,12288]{1,0:T(4,128)} %taps_ref.1, bf16[4,3,2,512]{3,2,1,0:T(2,128)(2,1)} %copy-done.13, bf16[4,3,2,512]{3,2,1,0:T(2,128)(2,1)} %copy-done.14, f32[4,3,16,512]{3,2,1,0:T(8,128)} %get-tuple-element.67.lh_ref, ...), custom_call_target="tpu_custom_call", output_to_operand_aliasing={{}: (6, {})} | custom-call | flops 1572864 | bytes 1572864 | tf_op jit(solution)/shard_map/fix/pallas_call | solution.py:477
  (120 shorter events, 30.9 us)
Async XLA Ops:
  7.5 29.5 %collective-permute-start.12 = (bf16[128,512]{1,0:T(8,128)(2,1)S(1)}, bf16[128,512]{1,0:T(8,128)(2,1)S(1)}, u32[]{:S(2)}, u32[]{:S(2)}) collective-permute-start(bf16[128,512]{1,0:T(8,128)(2,1)S(1)} %multiply_convert_fusion), channel_id=1, source_target_pairs={{0,4},{1,5},{2,6},{3,7},{4,0},{5,1},{6,2},{7,3},{8,12},{9,13},{10,... | collective-permute-start | bytes 393224 | tf_op jit(solution)/shard_map/ppermute | solution.py:517
  17.6 30.6 %collective-permute-start.13 = (bf16[128,1024]{1,0:T(8,128)(2,1)}, bf16[128,1024]{1,0:T(8,128)(2,1)S(1)}, u32[]{:S(2)}, u32[]{:S(2)}) collective-permute-start(bf16[128,1024]{1,0:T(8,128)(2,1)} %get-tuple-element.54), channel_id=1, source_target_pairs={{0,1},{1,0},{2,3},{3,2},{4,5},{5,4},{6,7},{7,6},{8,9},{9,8},{10,11... | collective-permute-start | bytes 786440 | tf_op jit(solution)/shard_map/ppermute | solution.py:493
  26.2 19.3 %collective-permute-start.4 = (bf16[128,512]{1,0:T(8,128)(2,1)S(1)}, bf16[128,512]{1,0:T(8,128)(2,1)S(1)}, u32[]{:S(2)}, u32[]{:S(2)}) collective-permute-start(bf16[128,512]{1,0:T(8,128)(2,1)S(1)} %copy-done.33), channel_id=1, source_target_pairs={{0,4},{1,5},{2,6},{3,7},{4,0},{5,1},{6,2},{7,3},{8,12},{9,13},{10,... | collective-permute-start | bytes 393224 | tf_op jit(solution)/shard_map/ppermute | solution.py:493
  27.0 19.3 %collective-permute-start.5 = (bf16[128,512]{1,0:T(8,128)(2,1)S(1)}, bf16[128,512]{1,0:T(8,128)(2,1)S(1)}, u32[]{:S(2)}, u32[]{:S(2)}) collective-permute-start(bf16[128,512]{1,0:T(8,128)(2,1)S(1)} %copy-done.32), channel_id=1, source_target_pairs={{0,5},{1,4},{2,7},{3,6},{4,1},{5,0},{6,3},{7,2},{8,13},{9,12},{10,... | collective-permute-start | bytes 393224 | tf_op jit(solution)/shard_map/ppermute | solution.py:493
  29.0 24.3 %collective-permute-start.14 = (bf16[128,1024]{1,0:T(8,128)(2,1)S(1)}, bf16[128,1024]{1,0:T(8,128)(2,1)S(1)}, u32[]{:S(2)}, u32[]{:S(2)}) collective-permute-start(bf16[128,1024]{1,0:T(8,128)(2,1)S(1)} %copy-done.24), channel_id=1, source_target_pairs={{0,2},{1,3},{2,0},{3,1},{4,6},{5,7},{6,4},{7,5},{8,10},{9,11},{10,... | collective-permute-start | bytes 786440 | tf_op jit(solution)/shard_map/ppermute | solution.py:493
  37.0 19.4 %collective-permute-start.15 = (bf16[128,1024]{1,0:T(8,128)(2,1)S(1)}, bf16[128,1024]{1,0:T(8,128)(2,1)S(1)}, u32[]{:S(2)}, u32[]{:S(2)}) collective-permute-start(bf16[128,1024]{1,0:T(8,128)(2,1)S(1)} %copy-done.22), channel_id=1, source_target_pairs={{0,3},{1,2},{2,1},{3,0},{4,7},{5,6},{6,5},{7,4},{8,11},{9,10},{10,... | collective-permute-start | bytes 786440 | tf_op jit(solution)/shard_map/ppermute | solution.py:493
  45.5 23.3 %collective-permute-start.1 = (bf16[128,1024]{1,0:T(8,128)(2,1)}, bf16[128,1024]{1,0:T(8,128)(2,1)S(1)}, u32[]{:S(2)}, u32[]{:S(2)}) collective-permute-start(bf16[128,1024]{1,0:T(8,128)(2,1)} %get-tuple-element.41), channel_id=1, source_target_pairs={{0,1},{1,0},{2,3},{3,2},{4,5},{5,4},{6,7},{7,6},{8,9},{9,8},{10,11... | collective-permute-start | bytes 786440 | tf_op jit(solution)/shard_map/ppermute | solution.py:493
  46.3 22.5 %collective-permute-start.2 = (bf16[128,1024]{1,0:T(8,128)(2,1)}, bf16[128,1024]{1,0:T(8,128)(2,1)S(1)}, u32[]{:S(2)}, u32[]{:S(2)}) collective-permute-start(bf16[128,1024]{1,0:T(8,128)(2,1)} %get-tuple-element.42), channel_id=1, source_target_pairs={{0,2},{1,3},{2,0},{3,1},{4,6},{5,7},{6,4},{7,5},{8,10},{9,11},{10,... | collective-permute-start | bytes 786440 | tf_op jit(solution)/shard_map/ppermute | solution.py:493
  48.2 20.7 %collective-permute-start.3 = (bf16[128,1024]{1,0:T(8,128)(2,1)}, bf16[128,1024]{1,0:T(8,128)(2,1)S(1)}, u32[]{:S(2)}, u32[]{:S(2)}) collective-permute-start(bf16[128,1024]{1,0:T(8,128)(2,1)} %get-tuple-element.43), channel_id=1, source_target_pairs={{0,3},{1,2},{2,1},{3,0},{4,7},{5,6},{6,5},{7,4},{8,11},{9,10},{10,... | collective-permute-start | bytes 786440 | tf_op jit(solution)/shard_map/ppermute | solution.py:493
  53.3 14.7 %collective-permute-start.6 = (bf16[128,512]{1,0:T(8,128)(2,1)S(1)}, bf16[128,512]{1,0:T(8,128)(2,1)S(1)}, u32[]{:S(2)}, u32[]{:S(2)}) collective-permute-start(bf16[128,512]{1,0:T(8,128)(2,1)S(1)} %copy-done.29), channel_id=1, source_target_pairs={{0,6},{1,7},{2,4},{3,5},{4,2},{5,3},{6,0},{7,1},{8,14},{9,15},{10,... | collective-permute-start | bytes 393224 | tf_op jit(solution)/shard_map/ppermute | solution.py:493
  56.4 12.4 %collective-permute-start.7 = (bf16[128,512]{1,0:T(8,128)(2,1)S(1)}, bf16[128,512]{1,0:T(8,128)(2,1)S(1)}, u32[]{:S(2)}, u32[]{:S(2)}) collective-permute-start(bf16[128,512]{1,0:T(8,128)(2,1)S(1)} %copy-done.28), channel_id=1, source_target_pairs={{0,7},{1,6},{2,5},{3,4},{4,3},{5,2},{6,1},{7,0},{8,15},{9,14},{10,... | collective-permute-start | bytes 393224 | tf_op jit(solution)/shard_map/ppermute | solution.py:493
  68.0 15.1 %collective-permute-start.26 = (f32[256,512]{1,0:T(8,128)}, f32[256,512]{1,0:T(8,128)S(1)}, u32[]{:S(2)}, u32[]{:S(2)}) collective-permute-start(f32[256,512]{1,0:T(8,128)} %get-tuple-element.73), channel_id=1, source_target_pairs={{0,8},{8,0},{16,24},{24,16},{1,9},{9,1},{17,25},{25,17},{2,10},{10... | collective-permute-start | bytes 1572872 | tf_op jit(solution)/shard_map/ppermute | solution.py:540
  83.0 20.8 %collective-permute-start.24 = (f32[512,512]{1,0:T(8,128)}, f32[512,512]{1,0:T(8,128)S(1)}, u32[]{:S(2)}, u32[]{:S(2)}) collective-permute-start(f32[512,512]{1,0:T(8,128)} %get-tuple-element.71), channel_id=1, source_target_pairs={{0,8},{8,0},{16,24},{24,16},{1,9},{9,1},{17,25},{25,17},{2,10},{10... | collective-permute-start | bytes 3145736 | tf_op jit(solution)/shard_map/ppermute | solution.py:532
  83.9 19.9 %collective-permute-start.27 = (bf16[256,512]{1,0:T(8,128)(2,1)}, bf16[256,512]{1,0:T(8,128)(2,1)S(1)}, u32[]{:S(2)}, u32[]{:S(2)}) collective-permute-start(bf16[256,512]{1,0:T(8,128)(2,1)} %get-tuple-element.74), channel_id=1, source_target_pairs={{16,0},{24,8},{17,1},{25,9},{18,2},{26,10},{19,3},{27,11},{20,4},{... | collective-permute-start | bytes 786440 | tf_op jit(solution)/shard_map/ppermute | solution.py:541
  85.2 11.8 %collective-permute-start.19 = (bf16[128,512]{1,0:T(8,128)(2,1)}, bf16[128,512]{1,0:T(8,128)(2,1)S(1)}, u32[]{:S(2)}, u32[]{:S(2)}) collective-permute-start(bf16[128,512]{1,0:T(8,128)(2,1)} %get-tuple-element.61), channel_id=1, source_target_pairs={{0,4},{1,5},{2,6},{3,7},{4,0},{5,1},{6,2},{7,3},{8,12},{9,13},{10,... | collective-permute-start | bytes 393224 | tf_op jit(solution)/shard_map/ppermute | solution.py:493
  86.5 14.6 %collective-permute-start.20 = (bf16[128,512]{1,0:T(8,128)(2,1)}, bf16[128,512]{1,0:T(8,128)(2,1)S(1)}, u32[]{:S(2)}, u32[]{:S(2)}) collective-permute-start(bf16[128,512]{1,0:T(8,128)(2,1)} %get-tuple-element.62), channel_id=1, source_target_pairs={{0,5},{1,4},{2,7},{3,6},{4,1},{5,0},{6,3},{7,2},{8,13},{9,12},{10,... | collective-permute-start | bytes 393224 | tf_op jit(solution)/shard_map/ppermute | solution.py:493
  90.3 22.5 %collective-permute-start.8 = (bf16[128,1024]{1,0:T(8,128)(2,1)}, bf16[128,1024]{1,0:T(8,128)(2,1)S(1)}, u32[]{:S(2)}, u32[]{:S(2)}) collective-permute-start(bf16[128,1024]{1,0:T(8,128)(2,1)} %get-tuple-element.49), channel_id=1, source_target_pairs={{0,1},{1,0},{2,3},{3,2},{4,5},{5,4},{6,7},{7,6},{8,9},{9,8},{10,11... | collective-permute-start | bytes 786440 | tf_op jit(solution)/shard_map/ppermute | solution.py:493
  103.8 22.6 %collective-permute-start.10 = (bf16[128,1024]{1,0:T(8,128)(2,1)}, bf16[128,1024]{1,0:T(8,128)(2,1)S(1)}, u32[]{:S(2)}, u32[]{:S(2)}) collective-permute-start(bf16[128,1024]{1,0:T(8,128)(2,1)} %get-tuple-element.51), channel_id=1, source_target_pairs={{0,3},{1,2},{2,1},{3,0},{4,7},{5,6},{6,5},{7,4},{8,11},{9,10},{10,... | collective-permute-start | bytes 786440 | tf_op jit(solution)/shard_map/ppermute | solution.py:493
  107.9 26.8 %collective-permute-start.16 = (bf16[128,1024]{1,0:T(8,128)(2,1)S(1)}, bf16[128,1024]{1,0:T(8,128)(2,1)S(1)}, u32[]{:S(2)}, u32[]{:S(2)}) collective-permute-start(bf16[128,1024]{1,0:T(8,128)(2,1)S(1)} %copy-done.17), channel_id=1, source_target_pairs={{0,1},{1,0},{2,3},{3,2},{4,5},{5,4},{6,7},{7,6},{8,9},{9,8},{10,11... | collective-permute-start | bytes 786440 | tf_op jit(solution)/shard_map/ppermute | solution.py:493
  110.3 25.7 %collective-permute-start.17 = (bf16[128,1024]{1,0:T(8,128)(2,1)S(1)}, bf16[128,1024]{1,0:T(8,128)(2,1)S(1)}, u32[]{:S(2)}, u32[]{:S(2)}) collective-permute-start(bf16[128,1024]{1,0:T(8,128)(2,1)S(1)} %copy-done.16), channel_id=1, source_target_pairs={{0,2},{1,3},{2,0},{3,1},{4,6},{5,7},{6,4},{7,5},{8,10},{9,11},{10,... | collective-permute-start | bytes 786440 | tf_op jit(solution)/shard_map/ppermute | solution.py:493
  112.8 24.8 %collective-permute-start.18 = (bf16[128,1024]{1,0:T(8,128)(2,1)S(1)}, bf16[128,1024]{1,0:T(8,128)(2,1)S(1)}, u32[]{:S(2)}, u32[]{:S(2)}) collective-permute-start(bf16[128,1024]{1,0:T(8,128)(2,1)S(1)} %copy-done.15), channel_id=1, source_target_pairs={{0,3},{1,2},{2,1},{3,0},{4,7},{5,6},{6,5},{7,4},{8,11},{9,10},{10,... | collective-permute-start | bytes 786440 | tf_op jit(solution)/shard_map/ppermute | solution.py:493
  114.2 40.7 %collective-permute-start.28 = (bf16[256,512]{1,0:T(8,128)(2,1)}, bf16[256,512]{1,0:T(8,128)(2,1)S(1)}, u32[]{:S(2)}, u32[]{:S(2)}) collective-permute-start(bf16[256,512]{1,0:T(8,128)(2,1)} %add_convert_fusion), channel_id=1, source_target_pairs={{0,4},{1,5},{2,6},{3,7},{4,0},{5,1},{6,2},{7,3},{8,12},{9,13},{10,... | collective-permute-start | bytes 786440 | tf_op jit(solution)/shard_map/ppermute | solution.py:543
  126.4 28.4 %collective-permute-start.25 = (bf16[256,512]{1,0:T(8,128)(2,1)S(1)}, bf16[256,512]{1,0:T(8,128)(2,1)S(1)}, u32[]{:S(2)}, u32[]{:S(2)}) collective-permute-start(bf16[256,512]{1,0:T(8,128)(2,1)S(1)} %dynamic-slice_convert_fusion), channel_id=1, source_target_pairs={{0,16},{8,24},{16,0},{24,8},{1,17},{9,25},{17,1},{25,9},{2,18},{10... | collective-permute-start | bytes 786440 | tf_op jit(solution)/shard_map/ppermute | solution.py:535
  134.7 12.7 %collective-permute-start.11 = (bf16[4,3,2,512]{3,2,1,0:T(2,128)(2,1)}, bf16[4,3,2,512]{3,2,1,0:T(2,128)(2,1)S(1)}, u32[]{:S(2)}, u32[]{:S(2)}) collective-permute-start(bf16[4,3,2,512]{3,2,1,0:T(2,128)(2,1)} %get-tuple-element.52), channel_id=1, source_target_pairs={{1,0},{2,1},{3,2},{4,3},{5,4},{6,5},{7,6},{9,8},{10,9},{11,10},{12... | collective-permute-start | bytes 73736 | tf_op jit(solution)/shard_map/ppermute | solution.py:565
  (39 other events, 411.3 us)

commit v3 on v0

--- a/solution.py
+++ b/solution.py
@@ -1,9 +1,677 @@
+import functools
 import math
 
 import jax
 import jax.numpy as jnp
+import numpy as np
 from jax import lax
+from jax.experimental import pallas as pl
+from jax.experimental.pallas import tpu as pltpu
 from jax.sharding import PartitionSpec as P
+
+VMEM_LIMIT = 56 * 1024 * 1024
+STEP = 128
+STRIP = 128
+
+
+def params():
+    return pltpu.CompilerParams(vmem_limit_bytes=VMEM_LIMIT)
+
+
+def cost(flops, moved):
+    return pl.CostEstimate(flops=flops, bytes_accessed=moved, transcendentals=0)
+
+
+def odd_tables(size):
+    freq = 2 * np.arange(size, dtype=np.int64)[:, None] + 1
+    spot = np.arange(size, dtype=np.int64)[None, :]
+    theta = (freq * spot % (4 * size)).astype(np.float64) * (2.0 * math.pi / (4 * size))
+    full = np.concatenate([np.cos(theta), -np.sin(theta)], axis=0).astype(np.float32)
+    high = full.astype(jnp.bfloat16)
+    low = (full - high.astype(np.float32)).astype(jnp.bfloat16)
+    return high, low
+
+
+def dot(a, b):
+    return jnp.dot(a, b, preferred_element_type=jnp.float32)
+
+
+def run(copies):
+    for copy in copies:
+        copy.start()
+    return copies
+
+
+def finish(copies):
+    for copy in copies:
+        copy.wait()
+
+
+def behind(values, before):
+    spot = lax.broadcasted_iota(jnp.int32, (values.shape[0], 1), 0)
+    one = jnp.where(spot == 0, before[1:2], pltpu.roll(values, 1, 0))
+    two = jnp.where(spot == 0, before[0:1], jnp.where(spot == 1, before[1:2], pltpu.roll(values, 2, 0)))
+    return one, two
+
+
+def conv_rows(values, before, taps):
+    values = values.astype(jnp.float32)
+    one, two = behind(values, before.astype(jnp.float32))
+    return taps[0:1] * values + taps[1:2] * one + taps[2:3] * two
+
+
+def where(hc):
+    me = lax.axis_index("ctx")
+    return me, me // hc, lax.axis_index("dp") % 2
+
+
+def strips(cols):
+    return [slice(c, c + STRIP) for c in range(0, cols, STRIP)]
+
+
+def gate_kernel(hc, count, base, feats_ref, before, taps_ref, grad_ref, *refs):
+    outs, refs = refs[:hc], refs[hc:]
+    parts, taps, stage, in_sem, small_sem, out_sem = refs
+    rows, cols = parts.shape[2:]
+    me, half, core = where(hc)
+
+    def column(region, j):
+        return pl.ds(pl.multiple_of((region * count + (me ^ (base + j))) * cols, cols), cols)
+
+    small = run([pltpu.make_async_copy(taps_ref, taps, small_sem)])
+    loads = [
+        run(
+            [
+                pltpu.make_async_copy(feats_ref.at[:, column(r, j)], parts.at[j, r], in_sem.at[j, r])
+                for r in range(3)
+            ]
+            + [pltpu.make_async_copy(grad_ref.at[:, column(0, j)], parts.at[j, 3], in_sem.at[j, 3])]
+        )
+        for j in range(hc)
+    ]
+    finish(small)
+    stores = []
+    for j in range(hc):
+        finish(loads[j])
+        mine = [(before[:, column(r, j)], taps[:, column(r, j)]) for r in range(3)]
+        for strip in strips(cols):
+            query, key, value = (
+                conv_rows(parts[j, r, :, strip], mine[r][0][:, strip], mine[r][1][:, strip])
+                for r in range(3)
+            )
+            stage[j, :, strip] = (key * value).astype(jnp.bfloat16)
+            stage[j, :, cols + strip.start : cols + strip.stop] = (
+                parts[j, 3, :, strip].astype(jnp.float32) * query
+            ).astype(jnp.bfloat16)
+        stores += run([pltpu.make_async_copy(stage.at[j], outs[j], out_sem.at[j])])
+    finish(stores)
+
+
+def gate(feats, before, taps, grad_out, count, cols, base):
+    rows = feats.shape[0]
+    hc = count // 2
+    shapes = [jax.ShapeDtypeStruct((rows, 2 * cols), jnp.bfloat16)] * hc
+    hbm = pl.BlockSpec(memory_space=pl.ANY)
+    return pl.pallas_call(
+        functools.partial(gate_kernel, hc, count, base),
+        in_specs=[hbm, pl.BlockSpec(memory_space=pltpu.VMEM), hbm, hbm],
+        out_specs=[hbm] * len(shapes),
+        out_shape=shapes,
+        scratch_shapes=[
+            pltpu.VMEM((hc, 4, rows, cols), jnp.bfloat16),
+            pltpu.VMEM(taps.shape, taps.dtype),
+            pltpu.VMEM((hc, rows, 2 * cols), jnp.bfloat16),
+            pltpu.SemaphoreType.DMA((hc, 4)),
+            pltpu.SemaphoreType.DMA,
+            pltpu.SemaphoreType.DMA((len(shapes),)),
+        ],
+        compiler_params=params(),
+        cost_estimate=cost(20 * rows * cols * hc, 12 * rows * cols * hc),
+        name="gate_other",
+    )(feats, before, taps, grad_out)
+
+
+def signs(first, rows):
+    odd = (lax.broadcasted_iota(jnp.int32, (rows, 1), 0) + first) % 2
+    return 1.0 - 2.0 * odd.astype(jnp.float32)
+
+
+def filter_home_kernel(scale, filt_ref, high_ref, low_ref, near_ref, far_ref):
+    size = filt_ref.shape[0] // 2
+
+    def spectrum(part):
+        now = part * scale
+        high = now.astype(jnp.bfloat16)
+        low = (now - high.astype(jnp.float32)).astype(jnp.bfloat16)
+        return dot(high_ref[...], high) + dot(high_ref[...], low) + dot(low_ref[...], high)
+
+    near = spectrum(filt_ref[:size, :])
+    far = spectrum(filt_ref[size:, :])
+    near_ref[...] = near
+    sign = signs(0, size)
+    far_ref[:size, :] = far[:size] - sign * near[size:]
+    far_ref[size:, :] = far[size:] + sign * near[:size]
+
+
+def prepare_kernel(hc, count, scale, *refs):
+    filters, refs = refs[:3], refs[3:]
+    gate_in, refs = refs[:4], refs[4:]
+    gate_out, refs = refs[:hc], refs[hc:]
+    gate_kernel(hc, count, 0, *gate_in, *gate_out, *refs[2:])
+    filter_home_kernel(scale, *filters, *refs[:2])
+
+
+def prepare(filt, high, low, feats, before, taps, grad_out, scale, count):
+    rows = feats.shape[0]
+    length, cols = filt.shape
+    hc = count // 2
+    shapes = [jax.ShapeDtypeStruct((rows, 2 * cols), jnp.bfloat16)] * hc
+    spectra = [jax.ShapeDtypeStruct((length, cols), jnp.float32)] * 2
+    hbm = pl.BlockSpec(memory_space=pl.ANY)
+    vmem = pl.BlockSpec(memory_space=pltpu.VMEM)
+    return pl.pallas_call(
+        functools.partial(prepare_kernel, hc, count, scale),
+        in_specs=[vmem] * 3 + [hbm, vmem, hbm, hbm],
+        out_specs=[hbm] * hc + [vmem] * 2,
+        out_shape=shapes + spectra,
+        scratch_shapes=[
+            pltpu.VMEM((hc, 4, rows, cols), jnp.bfloat16),
+            pltpu.VMEM(taps.shape, taps.dtype),
+            pltpu.VMEM((hc, rows, 2 * cols), jnp.bfloat16),
+            pltpu.SemaphoreType.DMA((hc, 4)),
+            pltpu.SemaphoreType.DMA,
+            pltpu.SemaphoreType.DMA((len(shapes),)),
+        ],
+        compiler_params=params(),
+        cost_estimate=cost(8 * length * length * cols, 20 * length * cols),
+        name="prepare",
+    )(filt, high, low, feats, before, taps, grad_out)
+
+
+def assemble_kernel(hc, *refs):
+    pieces, out_ref, stage, in_sem, out_sem = refs[:hc], *refs[hc:]
+    rows = pieces[0].shape[0]
+    cols = pieces[0].shape[1] // 2
+    me, half, _ = where(hc)
+    side = pl.ds(pl.multiple_of(half * cols, cols), cols)
+    loads = run([pltpu.make_async_copy(pieces[j].at[:, side], stage.at[j], in_sem.at[j]) for j in range(hc)])
+    stores = []
+    for j in range(hc):
+        finish([loads[j]])
+        place = pl.ds(pl.multiple_of(((me % hc) ^ j) * rows, rows), rows)
+        stores += run([pltpu.make_async_copy(stage.at[j], out_ref.at[place], out_sem.at[j])])
+    finish(stores)
+
+
+def assemble(pieces):
+    hc = len(pieces)
+    rows, width = pieces[0].shape
+    hbm = pl.BlockSpec(memory_space=pl.ANY)
+    return pl.pallas_call(
+        functools.partial(assemble_kernel, hc),
+        in_specs=[hbm] * hc,
+        out_specs=hbm,
+        out_shape=jax.ShapeDtypeStruct((hc * rows, width // 2), jnp.bfloat16),
+        scratch_shapes=[
+            pltpu.VMEM((hc, rows, width // 2), jnp.bfloat16),
+            pltpu.SemaphoreType.DMA((hc,)),
+            pltpu.SemaphoreType.DMA((hc,)),
+        ],
+        compiler_params=params(),
+        cost_estimate=cost(0, 2 * hc * rows * width),
+        name="assemble",
+    )(*pieces)
+
+
+def times(a_re, a_im, b_re, b_im):
+    return a_re * b_re - a_im * b_im, a_re * b_im + a_im * b_re
+
+
+def conj_times(a_re, a_im, b_re, b_im):
+    return a_re * b_re + a_im * b_im, a_re * b_im - a_im * b_re
+
+
+def spectral_kernel(hc, rows, home, scale, *refs):
+    tables, refs = refs[: 4 if home else 5], refs[4 if home else 5 :]
+    pieces, refs = refs[:hc], refs[hc:]
+    cross_ref = None
+    if home:
+        cross_ref, refs = refs[0], refs[1:]
+    outs, refs = refs[:hc], refs[hc:]
+    cross_outs = ()
+    if home:
+        cross_outs, refs = refs[:hc], refs[hc:]
+    corr_send, corr_keep, refs = refs[0], refs[1], refs[2:]
+    held, refs = refs[: len(tables)], refs[len(tables) :]
+    data, spec, prod, res, corr, piece_sem, table_sem, out_sem, corr_sem = refs[:9]
+    forward_ref, inverse_ref = held[:2]
+    near_ref, far_ref = (held[2], held[3]) if home else (refs[-1], None)
+    me, half, core = where(hc)
+    spot = me % hc
+    size = data.shape[0]
+    cols = res.shape[1] // (3 if home else 2)
+
+    def place(j):
+        return pl.ds(pl.multiple_of((spot ^ j) * rows, rows), rows)
+
+    def load(i):
+        return run([pltpu.make_async_copy(tables[i], held[i], table_sem.at[i])])
+
+    forward_copy = load(0)
+    piece_copies = run(
+        [pltpu.make_async_copy(pieces[j], data.at[place(j), : 2 * cols], piece_sem.at[j]) for j in range(hc)]
+    )
+    cross_copies = []
+    if home:
+        cross_copies = run([pltpu.make_async_copy(cross_ref, data.at[:, 2 * cols :], piece_sem.at[hc])])
+    filter_copies = [copy for i in range(2, len(tables)) for copy in load(i)]
+    inverse_copy = load(1)
+    finish(forward_copy)
+    finish(piece_copies)
+    for part in range(data.shape[1] // cols):
+        if part == 2:
+            finish(cross_copies)
+        here = slice(part * cols, (part + 1) * cols)
+        spec[:, here] = dot(forward_ref[...], data[:, here])
+    finish(filter_copies)
+    if not home:
+        low_ref, mine_ref, theirs_ref = held[2:]
+        share = mine_ref.shape[0]
+        mine = pl.ds(pl.multiple_of(core * share, share), share)
+        theirs = pl.ds(pl.multiple_of((1 - core) * share, share), share)
+        near_ref[...] = (
+            dot(forward_ref[:, mine], mine_ref[...])
+            + dot(forward_ref[:, theirs], theirs_ref[...])
+            + dot(low_ref[:, mine], mine_ref[...])
+            + dot(low_ref[:, theirs], theirs_ref[...])
+        )
+
+    def products(side):
+        def body(i, carry):
+            low = pl.ds(pl.multiple_of(i * STEP, STEP), STEP)
+            high = pl.ds(pl.multiple_of(size + i * STEP, STEP), STEP)
+
+            def get(part):
+                here = slice(part * cols, (part + 1) * cols)
+                return spec[low, here], spec[high, here]
+
+            def put(part, value):
+                here = slice(part * cols, (part + 1) * cols)
+                prod[low, here] = value[0].astype(jnp.bfloat16)
+                prod[high, here] = value[1].astype(jnp.bfloat16)
+
+            g, d = get(0), get(1)
+            h = near_ref[low, :], near_ref[high, :]
+            conv = times(*h, *g)
+            grad = conj_times(*h, *d)
+            corr = conj_times(*g, *d)
+            if home:
+                f = far_ref[low, :], far_ref[high, :]
+                gx, dx = (g, get(2)) if side == 0 else (get(2), d)
+                far_conv = times(*f, *gx)
+                far_grad = conj_times(*f, *dx)
+                if side == 0:
+                    grad = (grad[0] + far_grad[0], grad[1] + far_grad[1])
+                else:
+                    conv = (conv[0] + far_conv[0], conv[1] + far_conv[1])
+                put(2, far_conv if side == 0 else far_grad)
+                far_corr = conj_times(*gx, *dx)
+                sign = signs(0, STEP)
+                corr = (corr[0] + sign * far_corr[1], corr[1] - sign * far_corr[0])
+                put(4, far_corr)
+                put(3, corr)
+            else:
+                put(2, corr)
+            put(0, conv)
+            put(1, grad)
+            return carry
+
+        lax.fori_loop(0, size // STEP, body, 0)
+
+    if home:
+
+        @pl.when(half == 0)
+        def _():
+            products(0)
+
+        @pl.when(half == 1)
+        def _():
+            products(1)
+
+    else:
+        products(0)
+
+    def back(part):
+        return dot(inverse_ref[...], prod[:, part * cols : (part + 1) * cols])
+
+    finish(inverse_copy)
+    res[:, :cols] = back(0).astype(jnp.bfloat16)
+    res[:, cols : 2 * cols] = back(1).astype(jnp.bfloat16)
+    stores = run(
+        [pltpu.make_async_copy(res.at[place(j), : 2 * cols], outs[j], out_sem.at[j]) for j in range(hc)]
+    )
+    if home:
+        res[:, 2 * cols :] = back(2).astype(jnp.bfloat16)
+        stores += run(
+            [
+                pltpu.make_async_copy(res.at[place(j), 2 * cols :], cross_outs[j], out_sem.at[hc + j])
+                for j in range(hc)
+            ]
+        )
+    quarter = size // 2
+    for x in range(2 if home else 1):
+        corr[x] = back((3 if home else 2) + x) * scale
+        for i, (ref, which) in enumerate(((corr_send, 1 - core), (corr_keep, core))):
+            lags = pl.ds(pl.multiple_of(which * quarter, quarter), quarter)
+            stores += run(
+                [
+                    pltpu.make_async_copy(
+                        corr.at[x, lags], ref.at[x * quarter : (x + 1) * quarter], corr_sem.at[x, i]
+                    )
+                ]
+            )
+    finish(stores)
+
+
+def spectral(forward, inverse, filters, pieces, cross, scale):
+    hc = len(pieces)
+    rows, width = pieces[0].shape
+    cols = width // 2
+    size = hc * rows
+    home = cross is not None
+    hbm = pl.BlockSpec(memory_space=pl.ANY)
+    tables = [forward, inverse, *filters]
+    arrived = [*pieces, cross] if home else pieces
+    ins = 3 if home else 2
+    parts = 5 if home else 3
+    shapes = [jax.ShapeDtypeStruct((rows, width), jnp.bfloat16)] * hc
+    if home:
+        shapes = shapes + [jax.ShapeDtypeStruct((rows, cols), jnp.bfloat16)] * hc
+    corr = jax.ShapeDtypeStruct((size if home else size // 2, cols), jnp.float32)
+    return pl.pallas_call(
+        functools.partial(spectral_kernel, hc, rows, home, scale),
+        in_specs=[hbm] * (len(tables) + len(arrived)),
+        out_specs=[hbm] * (len(shapes) + 2),
+        out_shape=shapes + [corr, corr],
+        scratch_shapes=[pltpu.VMEM(t.shape, t.dtype) for t in tables]
+        + [
+            pltpu.VMEM((size, ins * cols), jnp.bfloat16),
+            pltpu.VMEM((2 * size, ins * cols), jnp.float32),
+            pltpu.VMEM((2 * size, parts * cols), jnp.bfloat16),
+            pltpu.VMEM((size, ins * cols), jnp.bfloat16),
+            pltpu.VMEM((2 if home else 1, size, cols), jnp.float32),
+            pltpu.SemaphoreType.DMA((len(arrived),)),
+            pltpu.SemaphoreType.DMA((len(tables),)),
+            pltpu.SemaphoreType.DMA((len(shapes),)),
+            pltpu.SemaphoreType.DMA((2, 2)),
+        ]
+        + ([] if home else [pltpu.VMEM((2 * size, cols), jnp.float32)]),
+        compiler_params=params(),
+        cost_estimate=cost(4 * size * size * cols * (ins + parts), 8 * size * size + 30 * size * cols),
+        name="spectral_home" if home else "spectral_other",
+    )(*tables, *arrived)
+
+
+def final_kernel(hc, count, base, top, aliased, *refs):
+    feats_ref, before, grad_ref, taps_ref = refs[:4]
+    pieces, refs = refs[4 : 4 + hc], refs[4 + hc :]
+    crosses = ()
+    if base > 0:
+        crosses, refs = refs[:hc], refs[hc:]
+    if aliased:
+        refs = refs[1:]
+    out_ref = last_ref = stage = last = None
+    if top:
+        edge_ref, parts, taps, back, edge, in_sem, small_sem, back_sem, end_sem = refs
+    else:
+        out_ref, edge_ref, last_ref, parts, taps, back, edge, last, stage = refs[:9]
+        in_sem, small_sem, back_sem, end_sem, out_sem = refs[9:]
+    me, half, _ = where(hc)
+    rows, cols = parts.shape[2:]
+
+    def column(region, j):
+        return pl.ds(pl.multiple_of((region * count + (me ^ (base + j))) * cols, cols), cols)
+
+    small = run([pltpu.make_async_copy(taps_ref, taps, small_sem)])
+    loads = []
+    for j in range(hc):
+        copies = [
+            pltpu.make_async_copy(source.at[:rows, column(r, j)], parts.at[j, r], in_sem.at[j, r])
+            for r, source in enumerate((grad_ref, feats_ref, feats_ref))
+        ]
+        copies.append(
+            pltpu.make_async_copy(pieces[j].at[:rows], back.at[j, :, : 2 * cols], back_sem.at[j])
+        )
+        if base > 0:
+            copies.append(
+                pltpu.make_async_copy(crosses[j].at[:rows], back.at[j, :, 2 * cols :], back_sem.at[hc + j])
+            )
+        loads.append(run(copies))
+    finish(small)
+    stores = []
+    spot = lax.broadcasted_iota(jnp.int32, (rows, 1), 0)
+    for j in range(hc):
+        finish(loads[j])
+        near_taps = [taps[:, column(r, j)] for r in range(3)]
+        near_before = [before[:, column(r, j)] for r in range(3)]
+        slot = (me ^ (base + j)) % hc
+        for strip in strips(cols):
+
+            def unmixed(region, dz):
+                edge[slot, region, :, strip] = dz[:2].astype(jnp.bfloat16)
+                if top:
+                    return
+                weights = near_taps[region][:, strip]
+                one = jnp.where(spot < rows - 1, pltpu.roll(dz, rows - 1, 0), 0.0)
+                two = jnp.where(spot < rows - 2, pltpu.roll(dz, rows - 2, 0), 0.0)
+                out = weights[0:1] * dz + weights[1:2] * one + weights[2:3] * two
+                last[slot, region, :, strip] = out[rows - 16 :]
+                stage[j, region, :, strip] = out.astype(jnp.bfloat16)
+
+            key, value = (
+                conv_rows(parts[j, r, :, strip], near_before[r][:, strip], near_taps[r][:, strip])
+                for r in (1, 2)
+            )
+            conv = back[j, :, strip].astype(jnp.float32)
+            grad = back[j, :, cols + strip.start : cols + strip.stop].astype(jnp.float32)
+            if base > 0:
+                extra = back[j, :, 2 * cols + strip.start : 2 * cols + strip.stop].astype(jnp.float32)
+                conv = jnp.where(half == 1, conv + extra, conv)
+                grad = jnp.where(half == 0, grad + extra, grad)
+            unmixed(0, parts[j, 0, :, strip].astype(jnp.float32) * conv)
+            unmixed(1, grad * value)
+            unmixed(2, grad * key)
+        if not top:
+            stores += run(
+                [
+                    pltpu.make_async_copy(stage.at[j, r], out_ref.at[:, column(r, j)], out_sem.at[j, r])
+                    for r in range(3)
+                ]
+            )
+    stores += run([pltpu.make_async_copy(edge, edge_ref, end_sem.at[0])])
+    if not top:
+        stores += run([pltpu.make_async_copy(last, last_ref, end_sem.at[1])])
+    finish(stores)
+
+
+def final(feats, before, grad_out, taps, pieces, crosses, so_far, count, base, top=False):
+    hc = len(pieces)
+    rows = 16 if top else feats.shape[0]
+    cols = pieces[0].shape[1] // 2
+    hbm = pl.BlockSpec(memory_space=pl.ANY)
+    arrived = [*pieces, *crosses]
+    args = [feats, before, grad_out, taps, *arrived]
+    aliases = {}
+    if so_far is not None:
+        args.append(so_far)
+        aliases = {len(args) - 1: 0}
+    edge = jax.ShapeDtypeStruct((hc, 3, 2, cols), jnp.bfloat16)
+    last = jax.ShapeDtypeStruct((hc, 3, 16, cols), jnp.float32)
+    shapes = [edge] if top else [jax.ShapeDtypeStruct(feats.shape, jnp.bfloat16), edge, last]
+    scratch = [
+        pltpu.VMEM((hc, 3, rows, cols), jnp.bfloat16),
+        pltpu.VMEM(taps.shape, taps.dtype),
+        pltpu.VMEM((hc, rows, (3 if base > 0 else 2) * cols), jnp.bfloat16),
+        pltpu.VMEM(edge.shape, edge.dtype),
+    ]
+    if not top:
+        scratch += [
+            pltpu.VMEM(last.shape, last.dtype),
+            pltpu.VMEM((hc, 3, rows, cols), jnp.bfloat16),
+        ]
+    scratch += [
+        pltpu.SemaphoreType.DMA((hc, 3)),
+        pltpu.SemaphoreType.DMA,
+        pltpu.SemaphoreType.DMA((len(arrived),)),
+        pltpu.SemaphoreType.DMA((2,)),
+    ]
+    if not top:
+        scratch.append(pltpu.SemaphoreType.DMA((hc, 3)))
+    name = ("edge_" if top else "final_") + ("other" if base > 0 else "home")
+    return pl.pallas_call(
+        functools.partial(final_kernel, hc, count, base, top, so_far is not None),
+        in_specs=[hbm, pl.BlockSpec(memory_space=pltpu.VMEM)] + [hbm] * (len(args) - 2),
+        out_specs=[hbm] * len(shapes),
+        scratch_shapes=scratch,
+        out_shape=shapes,
+        input_output_aliases=aliases,
+        compiler_params=params(),
+        cost_estimate=cost(30 * rows * cols * hc, 16 * rows * cols * hc),
+        name=name,
+    )(*args)
+
+
+def fix_kernel(hc, taps_ref, eh_ref, eo_ref, lh_ref, lo_ref, _, out_ref, stage, sem):
+    me, half, _ = where(hc)
+    cols = eh_ref.shape[3]
+    width = out_ref.shape[1] // 3
+    turn = me == hc - 1
+    spot = lax.broadcasted_iota(jnp.int32, (16, 1), 0)
+    for slot, last in enumerate((lh_ref, lo_ref)):
+        mine, swapped = (eh_ref, eo_ref) if slot == 0 else (eo_ref, eh_ref)
+        first = jnp.where(half == slot, 0, hc)
+        for j in range(hc):
+            for region in range(3):
+                col = pl.ds(pl.multiple_of(region * width + (first + j) * cols, cols), cols)
+                ahead = jnp.where(
+                    turn, swapped[j, region].astype(jnp.float32), mine[j, region].astype(jnp.float32)
+                )
+                one, two = taps_ref[1:2, col], taps_ref[2:3, col]
+                add = jnp.where(
+                    spot == 14,
+                    two * ahead[0:1],
+                    jnp.where(spot == 15, one * ahead[0:1] + two * ahead[1:2], 0.0),
+                )
+                stage[:, col] = (last[j, region] + add).astype(jnp.bfloat16)
+    copy = pltpu.make_async_copy(stage, out_ref.at[pl.ds(out_ref.shape[0] - 16, 16)], sem)
+    copy.start()
+    copy.wait()
+
+
+def fix(taps, edge_home, edge_other, last_home, last_other, result):
+    hc = edge_home.shape[0]
+    vmem = pl.BlockSpec(memory_space=pltpu.VMEM)
+    hbm = pl.BlockSpec(memory_space=pl.ANY)
+    return pl.pallas_call(
+        functools.partial(fix_kernel, hc),
+        in_specs=[vmem] * 5 + [hbm],
+        out_specs=hbm,
+        out_shape=jax.ShapeDtypeStruct(result.shape, result.dtype),
+        scratch_shapes=[pltpu.VMEM((16, result.shape[1]), jnp.bfloat16), pltpu.SemaphoreType.DMA],
+        input_output_aliases={5: 0},
+        compiler_params=params(),
+        cost_estimate=cost(16 * 8 * result.shape[1], 128 * result.shape[1]),
+        name="fix",
+    )(taps, edge_home, edge_other, last_home, last_other, result)
+
+
+def exchange(pieces, base):
+    devices = range(lax.axis_size("ctx"))
+    return [
+        piece if base + j == 0 else lax.ppermute(piece, "ctx", [(i, i ^ (base + j)) for i in devices])
+        for j, piece in enumerate(pieces)
+    ]
+
+
+def half_shards(feats, short_weight, grad_out, filt):
+    length, block = filt.shape
+    count = lax.axis_size("ctx")
+    hc = count // 2
+    size = length // 2
+    quarter = length // 4
+    feats, grad_out = feats[0], grad_out[0]
+    rows = feats.shape[0]
+    high, low = odd_tables(size)
+    inverse = np.ascontiguousarray(high.T)
+    scale = 1.0 / (math.sqrt(length) * size)
+    me = lax.axis_index("ctx")
+    dp = lax.axis_index("dp")
+    core, x = dp % 2, dp // 2
+    tie = lax.optimization_barrier
+    cores = [(i, i ^ 1) for i in range(4)]
+
+    late, source = tie((feats[rows - 2 :], filt))
+    before = from_behind(late, "ctx", 1)
+    share = size // 2
+    part = (lax.dynamic_slice_in_dim(source, core * share, share, 0) * scale).astype(jnp.bfloat16)
+    part = lax.ppermute(part, "ctx", [(i, i ^ hc) for i in range(count)])
+    gated = gate(feats, before, short_weight, grad_out, count, block, hc)
+
+    ready, gated = tie((before, gated))
+    other_pieces = exchange(gated, 0)
+    outs = prepare(filt, high, low, feats, ready, short_weight, grad_out, scale, count)
+    outs, other_pieces, part = tie((outs, other_pieces, part))
+    near, far = outs[hc:]
+
+    home_pieces = exchange(outs[:hc], 0)
+    cross, part = tie((assemble(other_pieces), part))
+    cross = lax.ppermute(cross, "ctx", [(i, i ^ hc) for i in range(count)])
+    rest = lax.ppermute(part, "dp", cores)
+    outs = spectral(high, inverse, (low, part, rest), other_pieces, None, scale)
+    outs, home_pieces, cross = tie((outs, home_pieces, cross))
+
+    other_back = exchange(outs[:hc], 0)
+    send, keep = outs[hc:]
+    summed = keep + lax.ppermute(send, "dp", cores)
+    summed = summed + lax.ppermute(summed.astype(jnp.bfloat16), "dp", [(2, 0), (3, 1)]).astype(jnp.float32)
+    crossing = summed.astype(jnp.bfloat16)
+    outs = spectral(high, inverse, (near, far), home_pieces, cross, scale)
+    outs, other_back, crossing = tie((outs, other_back, crossing))
+
+    home_back = exchange(outs[:hc], 0)
+    cross_outs = outs[hc : 2 * hc]
+    early = exchange(cross_outs[: hc // 2], hc)
+    late, sums, home_back, early, crossing = tie(
+        (cross_outs[hc // 2 :], outs[2 * hc :], home_back, early, crossing)
+    )
+
+    cross_back = list(early) + exchange(late, hc + hc // 2)
+    owners = [(d * count + i, d * count + (i ^ hc)) for d in range(2) for i in range(count)]
+    filt_other = lax.ppermute(crossing, ("dp", "ctx"), owners)
+    send, keep = sums
+    came = lax.ppermute(send, "dp", cores)
+    result, edge_home, last_home = final(
+        feats, before, grad_out, short_weight, home_back, (), None, count, 0
+    )
+    keep, came, edge_home = tie((keep, came, edge_home))
+    summed = keep + came
+    there = lax.dynamic_slice_in_dim(summed, (1 - x) * quarter, quarter, 0).astype(jnp.bfloat16)
+    here = lax.dynamic_slice_in_dim(summed, x * quarter, quarter, 0)
+    cross_back, there, edge_home = tie((cross_back, there, edge_home))
+
+    there = lax.ppermute(there, "dp", [(i, i ^ 2) for i in range(4)])
+    filt_out = here + there.astype(jnp.float32) + filt_other.astype(jnp.float32)
+    edge_home = from_behind(edge_home, "ctx", -1)
+    (edge_other,) = final(
+        feats, before, grad_out, short_weight, other_back, cross_back, None, count, hc, True
+    )
+    edge_other = from_behind(edge_other, "ctx", -1)
+    result, _, last_other = final(
+        feats, before, grad_out, short_weight, other_back, cross_back, result, count, hc
+    )
+    result = fix(short_weight, edge_home, edge_other, last_home, last_other, result)
+    return (result[None], filt_out)
+
 
 full_precision = lax.Precision.HIGHEST
 split_precision = lax.Precision.HIGH
@@ -85,7 +753,7 @@
     return signal.reshape(length, signal.shape[2]) / (2.0 * length)
 
 
-def spectral(gated_sig, grad_sig, filter_cols, tables, length):
+def long_spectral(gated_sig, grad_sig, filter_cols, tables, length):
     g_spec = data_forward(gated_sig, tables, split_precision)
     d_spec = data_forward(grad_sig, tables, split_precision)
     h_spec = filter_forward(filter_cols, tables)
@@ -103,7 +771,7 @@
     return (conv_out, gated_grad, filt_grad)
 
 
-def shards(feats, short_weight, grad_out, filt):
+def long_shards(feats, short_weight, grad_out, filt):
     rows = feats.shape[1]
     width = feats.shape[2] // 3
     length = filt.shape[0]
@@ -150,7 +818,7 @@
     wide_grad = wide_grad.reshape(replicas, narrow, length)
     offset = lax.axis_index("dp") * narrow
     filt_cols = lax.dynamic_slice_in_dim(filt, offset, narrow, 1)
-    conv_out, gated_grad, filt_grad = spectral(
+    conv_out, gated_grad, filt_grad = long_spectral(
         wide_gated, wide_grad, filt_cols * scale_inv, tables, length
     )
     back_conv, back_grad = (
@@ -210,6 +878,22 @@
     return (grad_in.astype(jnp.bfloat16), filt_out)
 
 
+def shards(feats, short_weight, grad_out, filt):
+    count = lax.axis_size("ctx")
+    length, block = filt.shape
+    fits = (
+        length <= 1024
+        and length % (4 * STEP) == 0
+        and count > 1
+        and count & (count - 1) == 0
+        and feats.shape[1] % 128 == 0
+        and block % 128 == 0
+        and lax.axis_size("dp") == 4
+    )
+    plan = half_shards if fits else long_shards
+    return plan(feats, short_weight, grad_out, filt)
+
+
 def solution(mesh):
     return jax.shard_map(
         shards,

time: 356 us -> 143 us (0.40)
  the two profiles are of different devices: /device:TPU:0 before, /device:TPU:18 now
where the time goes in v3:
time: 143 us; the launch traced here: 142 us
  Pallas kernels  52.6 us (37%)
  starting transfers between devices  44.5 us (31%)
  waiting for transfers between devices  34.2 us (24%)
  other arithmetic  5.06 us (4%)
  local copies, waits for them, and re-layouts  4.3 us (3%)
    ppermute x16, waiting for transfers between devices, exchange(): lax.ppermute(piece, 'ctx', [(i, i ^ base + j) for i in devices])  32.2 us
    ppermute x16, starting transfers between devices, exchange(): lax.ppermute(piece, 'ctx', [(i, i ^ base + j) for i in devices])  22.8 us
    pallas_call x2, Pallas kernels, spectral(): pl.pallas_call(functools.partial(spectral_kernel, hc, rows, home, scale),...  18.6 us
    pallas_call x3, Pallas kernels, final(): pl.pallas_call(functools.partial(final_kernel, hc, count, base, top, so_f...  14.7 us
    pallas_call x1, Pallas kernels, prepare(): pl.pallas_call(functools.partial(prepare_kernel, hc, count, scale), in_sp...  10.7 us
    ppermute x3, starting transfers between devices, from_behind(): return lax.ppermute(block, axis, route)  9.79 us
    ppermute x1, starting transfers between devices, half_shards(): there = lax.ppermute(there, 'dp', [(i, i ^ 2) for i in range(4)])  5.31 us
    pallas_call x1, Pallas kernels, gate(): pl.pallas_call(functools.partial(gate_kernel, hc, count, base), in_specs=...  4.58 us
  transfers between devices with their start and end apart: 27, of which 8 were waited for; matrix products, arithmetic and copies ran while one was open for 2% of the time, Pallas kernels for 36%

profile of v3, /device:TPU:18, one launch (start us, length us, event | category | flops | bytes accessed | tf_op | source)
XLA Modules:
  0.0 141.8 jit_solution(7283286579205637578)
XLA Ops:
  1.6 3.4 %collective-permute-start = (bf16[2,12288]{1,0:T(2,128)(2,1)S(1)}, bf16[2,12288]{1,0:T(2,128)(2,1)S(1)}, u32[]{:S(2)}, u32[]{:S(2)}) collective-permute-start(bf16[2,12288]{1,0:T(2,128)(2,1)S(1)} %slice_bitcast_fusion), channel_id=1, source_target_pairs={{0,1},{1,2},{2,3},{3,4},{4,5},{5,6},{6,7},{8,9},{9,10},{10,11},{11... | collective-permute-start | bytes 147464 | tf_op jit(solution)/shard_map/ppermute | solution.py:683
  6.6 2.0 %collective-permute-done.before.refs_4_.refs_1_ = bf16[2,12288]{1,0:T(2,128)(2,1)S(1)} collective-permute-done((bf16[2,12288]{1,0:T(2,128)(2,1)S(1)}, bf16[2,12288]{1,0:T(2,128)(2,1)S(1)}, u32[]{:S(2)}, u32[]{:S(2)}) %collective-permute-start) | collective-permute-done | bytes 49184 | tf_op jit(solution)/shard_map/ppermute | solution.py:683
  9.2 4.6 %gate_other.1 = (bf16[128,1024]{1,0:T(8,128)(2,1)}, bf16[128,1024]{1,0:T(8,128)(2,1)}, bf16[128,1024]{1,0:T(8,128)(2,1)}, bf16[128,1024]{1,0:T(8,128)(2,1)}) custom-call(bf16[128,12288]{1,0:T(8,128)(2,1)} %bitcast.5, bf16[2,12288]{1,0:T(2,128)(2,1)} %copy-done.4, f32[3,12288]{1,0:T(4,128)} %taps_ref.3, bf16[128,4096]{1,0:T(8,128)(2,1)} %bitcast.10), custom_call_target="tpu_custom_call" | custom-call | flops 5242880 | bytes 3145728 | tf_op jit(solution)/shard_map/gate_other/pallas_call | solution.py:115
  14.4 2.8 %collective-permute-start.2 = (bf16[128,1024]{1,0:T(8,128)(2,1)}, bf16[128,1024]{1,0:T(8,128)(2,1)S(1)}, u32[]{:S(2)}, u32[]{:S(2)}) collective-permute-start(bf16[128,1024]{1,0:T(8,128)(2,1)} %get-tuple-element.113), channel_id=1, source_target_pairs={{0,2},{1,3},{2,0},{3,1},{4,6},{5,7},{6,4},{7,5},{8,10},{9,11},{10,... | collective-permute-start | bytes 786440 | tf_op jit(solution)/shard_map/ppermute | solution.py:591
  18.6 10.7 %prepare.1 = (bf16[128,1024]{1,0:T(8,128)(2,1)}, bf16[128,1024]{1,0:T(8,128)(2,1)}, bf16[128,1024]{1,0:T(8,128)(2,1)}, bf16[128,1024]{1,0:T(8,128)(2,1)}, f32[1024,512]{1,0:T(8,128)}, /*index=5*/f32[1024,512]{1,0:T(8,128)}) custom-call(f32[1024,512]{1,0:T(8,128)} %refs_0_.3, bf16[1024,512]{1,0:T(8,128)(2,1)} %constant.45.clone.refs_1_.refs_0_, ...), custom_call_target="tpu_custom_call" | custom-call | flops 4294967296 | bytes 10485760 | tf_op jit(solution)/shard_map/prepare/pallas_call | solution.py:172
  33.4 2.3 %collective-permute-start.9 = (bf16[512,512]{1,0:T(8,128)(2,1)}, bf16[512,512]{1,0:T(8,128)(2,1)S(1)}, u32[]{:S(2)}, u32[]{:S(2)}) collective-permute-start(bf16[512,512]{1,0:T(8,128)(2,1)} %assemble.1), channel_id=1, source_target_pairs={{0,4},{1,5},{2,6},{3,7},{4,0},{5,1},{6,2},{7,3},{8,12},{9,13},{10,... | collective-permute-start | bytes 1572872 | tf_op jit(solution)/shard_map/ppermute | solution.py:628
  39.8 8.3 %spectral_other.1 = (bf16[128,1024]{1,0:T(8,128)(2,1)}, bf16[128,1024]{1,0:T(8,128)(2,1)}, bf16[128,1024]{1,0:T(8,128)(2,1)}, bf16[128,1024]{1,0:T(8,128)(2,1)}, f32[256,512]{1,0:T(8,128)}, /*index=5*/f32[256,512]{1,0:T(8,128)}) custom-call(bf16[1024,512]{1,0:T(8,128)(2,1)} %constant.45.clone.refs_1_.refs_0_, bf16[512,1024]{1,0:T(8,128)(2,1)} %constant.47.clone.refs_1_, ...), custom_call_target="tpu_custom_call" | custom-call | flops 2684354560 | bytes 9961472 | tf_op jit(solution)/shard_map/spectral_other/pallas_call | solution.py:391
  48.1 5.6 %collective-permute-done.7.refs_6_ = bf16[128,1024]{1,0:T(8,128)(2,1)S(1)} collective-permute-done((bf16[128,1024]{1,0:T(8,128)(2,1)}, bf16[128,1024]{1,0:T(8,128)(2,1)S(1)}, u32[]{:S(2)}, u32[]{:S(2)}) %collective-permute-start.7) | collective-permute-done | bytes 262176 | tf_op jit(solution)/shard_map/ppermute | solution.py:591
  53.8 6.5 %collective-permute-done.8.refs_7_ = bf16[128,1024]{1,0:T(8,128)(2,1)S(1)} collective-permute-done((bf16[128,1024]{1,0:T(8,128)(2,1)}, bf16[128,1024]{1,0:T(8,128)(2,1)S(1)}, u32[]{:S(2)}, u32[]{:S(2)}) %collective-permute-start.8) | collective-permute-done | bytes 262176 | tf_op jit(solution)/shard_map/ppermute | solution.py:591
  61.2 2.3 %collective-permute-start.11 = (bf16[128,1024]{1,0:T(8,128)(2,1)}, bf16[128,1024]{1,0:T(8,128)(2,1)S(1)}, u32[]{:S(2)}, u32[]{:S(2)}) collective-permute-start(bf16[128,1024]{1,0:T(8,128)(2,1)} %get-tuple-element.152), channel_id=1, source_target_pairs={{0,2},{1,3},{2,0},{3,1},{4,6},{5,7},{6,4},{7,5},{8,10},{9,11},{10,... | collective-permute-start | bytes 786440 | tf_op jit(solution)/shard_map/ppermute | solution.py:591
  65.6 2.5 %collective-permute-start.14 = (bf16[256,512]{1,0:T(8,128)(2,1)S(1)}, bf16[256,512]{1,0:T(8,128)(2,1)S(1)}, u32[]{:S(2)}, u32[]{:S(2)}) collective-permute-start(bf16[256,512]{1,0:T(8,128)(2,1)S(1)} %get-tuple-element.196), channel_id=1, source_target_pairs={{16,0},{24,8},{17,1},{25,9},{18,2},{26,10},{19,3},{27,11},{20,4},{... | collective-permute-start | bytes 786440 | tf_op jit(solution)/shard_map/ppermute | solution.py:636
  68.1 10.4 %spectral_home.1 = (bf16[128,1024]{1,0:T(8,128)(2,1)}, bf16[128,1024]{1,0:T(8,128)(2,1)}, bf16[128,1024]{1,0:T(8,128)(2,1)}, bf16[128,1024]{1,0:T(8,128)(2,1)}, ...) custom-call(bf16[1024,512]{1,0:T(8,128)(2,1)} %constant.45.clone.ref, ...), custom_call_target="tpu_custom_call" | custom-call | flops 4294967296 | bytes 9961472 | tf_op jit(solution)/shard_map/spectral_home/pallas_call | solution.py:391
  82.9 2.5 %collective-permute-start.18 = (bf16[128,512]{1,0:T(8,128)(2,1)}, bf16[128,512]{1,0:T(8,128)(2,1)S(1)}, u32[]{:S(2)}, u32[]{:S(2)}) collective-permute-start(bf16[128,512]{1,0:T(8,128)(2,1)} %get-tuple-element.164), channel_id=1, source_target_pairs={{0,4},{1,5},{2,6},{3,7},{4,0},{5,1},{6,2},{7,3},{8,12},{9,13},{10,... | collective-permute-start | bytes 393224 | tf_op jit(solution)/shard_map/ppermute | solution.py:591
  86.8 12.6 %collective-permute-done.18.refs_8_ = bf16[128,512]{1,0:T(8,128)(2,1)S(1)} collective-permute-done((bf16[128,512]{1,0:T(8,128)(2,1)}, bf16[128,512]{1,0:T(8,128)(2,1)S(1)}, u32[]{:S(2)}, u32[]{:S(2)}) %collective-permute-start.18) | collective-permute-done | bytes 131104 | tf_op jit(solution)/shard_map/ppermute | solution.py:591
  102.0 2.4 %collective-permute-start.21 = (bf16[128,512]{1,0:T(8,128)(2,1)}, bf16[128,512]{1,0:T(8,128)(2,1)}, u32[]{:S(2)}, u32[]{:S(2)}) collective-permute-start(bf16[128,512]{1,0:T(8,128)(2,1)} %get-tuple-element.170), channel_id=1, source_target_pairs={{0,7},{1,6},{2,5},{3,4},{4,3},{5,2},{6,1},{7,0},{8,15},{9,14},{10,... | collective-permute-start | bytes 393224 | tf_op jit(solution)/shard_map/ppermute | solution.py:591
  105.8 5.7 %final_home.1 = (bf16[128,12288]{1,0:T(8,128)(2,1)}, bf16[4,3,2,512]{3,2,1,0:T(2,128)(2,1)}, f32[4,3,16,512]{3,2,1,0:T(8,128)}) custom-call(bf16[128,12288]{1,0:T(8,128)(2,1)} %bitcast.7, bf16[2,12288]{1,0:T(2,128)(2,1)} %copy-done.4, bf16[128,4096]{1,0:T(8,128)(2,1)} %bitcast.12, f32[3,12288]{1,0:T(4,128)} %taps_ref.3, ...), custom_call_target="tpu_custom_call" | custom-call | flops 7864320 | bytes 4194304 | tf_op jit(solution)/shard_map/final_home/pallas_call | solution.py:531
  111.8 1.9 %collective-permute-done.20.refs_10_ = bf16[128,512]{1,0:T(8,128)(2,1)} collective-permute-done((bf16[128,512]{1,0:T(8,128)(2,1)}, bf16[128,512]{1,0:T(8,128)(2,1)}, u32[]{:S(2)}, u32[]{:S(2)}) %collective-permute-start.20) | collective-permute-done | bytes 131104 | tf_op jit(solution)/shard_map/ppermute | solution.py:591
  113.8 2.7 %collective-permute-done.21.refs_11_ = bf16[128,512]{1,0:T(8,128)(2,1)} collective-permute-done((bf16[128,512]{1,0:T(8,128)(2,1)}, bf16[128,512]{1,0:T(8,128)(2,1)}, u32[]{:S(2)}, u32[]{:S(2)}) %collective-permute-start.21) | collective-permute-done | bytes 131104 | tf_op jit(solution)/shard_map/ppermute | solution.py:591
  116.4 5.3 %collective-permute-start.25 = (bf16[256,512]{1,0:T(8,128)(2,1)S(1)}, bf16[256,512]{1,0:T(8,128)(2,1)S(1)}, u32[]{:S(2)}, u32[]{:S(2)}) collective-permute-start(bf16[256,512]{1,0:T(8,128)(2,1)S(1)} %dynamic-slice_convert_fusion), channel_id=1, source_target_pairs={{0,16},{8,24},{16,0},{24,8},{1,17},{9,25},{17,1},{25,9},{2,18},{10... | collective-permute-start | bytes 786440 | tf_op jit(solution)/shard_map/ppermute | solution.py:662
  121.8 2.9 %edge_other.1 = bf16[4,3,2,512]{3,2,1,0:T(2,128)(2,1)} custom-call(bf16[128,12288]{1,0:T(8,128)(2,1)} %bitcast.8, bf16[2,12288]{1,0:T(2,128)(2,1)} %copy-done.4, bf16[128,4096]{1,0:T(8,128)(2,1)} %bitcast.13, f32[3,12288]{1,0:T(4,128)} %taps_ref.3, bf16[128,1024]{1,0:T(8,128)(2,1)} %get-tuple-element.182.refs_4_, bf16[128,1024]{1,0:T(8,128)(2,1)} %copy-done.1, ...), custom_call_target="tpu_custom_call" | custom-call | flops 983040 | bytes 524288 | tf_op jit(solution)/shard_map/edge_other/pallas_call | solution.py:531
  124.7 3.4 %collective-permute-start.24 = (bf16[4,3,2,512]{3,2,1,0:T(2,128)(2,1)}, bf16[4,3,2,512]{3,2,1,0:T(2,128)(2,1)S(1)}, u32[]{:S(2)}, u32[]{:S(2)}) collective-permute-start(bf16[4,3,2,512]{3,2,1,0:T(2,128)(2,1)} %edge_other.1), channel_id=1, source_target_pairs={{1,0},{2,1},{3,2},{4,3},{5,4},{6,5},{7,6},{9,8},{10,9},{11,10},{12... | collective-permute-start | bytes 73736 | tf_op jit(solution)/shard_map/ppermute | solution.py:683
  128.1 2.9 %collective-permute-start.23 = (bf16[4,3,2,512]{3,2,1,0:T(2,128)(2,1)S(1)}, bf16[4,3,2,512]{3,2,1,0:T(2,128)(2,1)S(1)}, u32[]{:S(2)}, u32[]{:S(2)}) collective-permute-start(bf16[4,3,2,512]{3,2,1,0:T(2,128)(2,1)S(1)} %copy-done.21), channel_id=1, source_target_pairs={{1,0},{2,1},{3,2},{4,3},{5,4},{6,5},{7,6},{9,8},{10,9},{11,10},{12... | collective-permute-start | bytes 73736 | tf_op jit(solution)/shard_map/ppermute | solution.py:683
  131.1 6.1 %final_other.1 = (bf16[128,12288]{1,0:T(8,128)(2,1)}, bf16[4,3,2,512]{3,2,1,0:T(2,128)(2,1)}, f32[4,3,16,512]{3,2,1,0:T(8,128)}) custom-call(bf16[128,12288]{1,0:T(8,128)(2,1)} %bitcast.9, bf16[2,12288]{1,0:T(2,128)(2,1)} %copy-done.4, bf16[128,4096]{1,0:T(8,128)(2,1)} %bitcast.14, f32[3,12288]{1,0:T(4,128)} %taps_ref.3, ...), custom_call_target="tpu_custom_call", output_to_operand_aliasing={{0}: (12, {})} | custom-call | flops 7864320 | bytes 4194304 | tf_op jit(solution)/shard_map/final_other/pallas_call | solution.py:531
  137.8 2.1 %fix.1 = bf16[128,12288]{1,0:T(8,128)(2,1)} custom-call(f32[3,12288]{1,0:T(4,128)} %taps_ref.3, bf16[4,3,2,512]{3,2,1,0:T(2,128)(2,1)} %copy-done.14, bf16[4,3,2,512]{3,2,1,0:T(2,128)(2,1)} %copy-done.13, f32[4,3,16,512]{3,2,1,0:T(8,128)} %get-tuple-element.190.lh_ref, f32[4,3,16,512]{3,2,1,0:T(8,128)} %get-tuple-element.192.lo_ref, ...), custom_call_target="tpu_custom_call", output_to_operand_aliasing={{}: (5, {})} | custom-call | flops 1572864 | bytes 1572864 | tf_op jit(solution)/shard_map/fix/pallas_call | solution.py:575
  (90 shorter events, 28.6 us)
Async XLA Ops:
  6.2 23.2 %collective-permute-start.4 = (bf16[256,512]{1,0:T(8,128)(2,1)S(1)}, bf16[256,512]{1,0:T(8,128)(2,1)S(1)}, u32[]{:S(2)}, u32[]{:S(2)}) collective-permute-start(bf16[256,512]{1,0:T(8,128)(2,1)S(1)} %multiply_convert_fusion), channel_id=1, source_target_pairs={{0,4},{1,5},{2,6},{3,7},{4,0},{5,1},{6,2},{7,3},{8,12},{9,13},{10,... | collective-permute-start | bytes 786440 | tf_op jit(solution)/shard_map/ppermute | solution.py:617
  13.8 15.6 %collective-permute-start.1 = (bf16[128,1024]{1,0:T(8,128)(2,1)}, bf16[128,1024]{1,0:T(8,128)(2,1)S(1)}, u32[]{:S(2)}, u32[]{:S(2)}) collective-permute-start(bf16[128,1024]{1,0:T(8,128)(2,1)} %get-tuple-element.112), channel_id=1, source_target_pairs={{0,1},{1,0},{2,3},{3,2},{4,5},{5,4},{6,7},{7,6},{8,9},{9,8},{10,11... | collective-permute-start | bytes 786440 | tf_op jit(solution)/shard_map/ppermute | solution.py:591
  14.4 15.0 %collective-permute-start.2 = (bf16[128,1024]{1,0:T(8,128)(2,1)}, bf16[128,1024]{1,0:T(8,128)(2,1)S(1)}, u32[]{:S(2)}, u32[]{:S(2)}) collective-permute-start(bf16[128,1024]{1,0:T(8,128)(2,1)} %get-tuple-element.113), channel_id=1, source_target_pairs={{0,2},{1,3},{2,0},{3,1},{4,6},{5,7},{6,4},{7,5},{8,10},{9,11},{10,... | collective-permute-start | bytes 786440 | tf_op jit(solution)/shard_map/ppermute | solution.py:591
  17.2 13.6 %collective-permute-start.3 = (bf16[128,1024]{1,0:T(8,128)(2,1)}, bf16[128,1024]{1,0:T(8,128)(2,1)S(1)}, u32[]{:S(2)}, u32[]{:S(2)}) collective-permute-start(bf16[128,1024]{1,0:T(8,128)(2,1)} %get-tuple-element.114), channel_id=1, source_target_pairs={{0,3},{1,2},{2,1},{3,0},{4,7},{5,6},{6,5},{7,4},{8,11},{9,10},{10,... | collective-permute-start | bytes 786440 | tf_op jit(solution)/shard_map/ppermute | solution.py:591
  33.4 26.9 %collective-permute-start.9 = (bf16[512,512]{1,0:T(8,128)(2,1)}, bf16[512,512]{1,0:T(8,128)(2,1)S(1)}, u32[]{:S(2)}, u32[]{:S(2)}) collective-permute-start(bf16[512,512]{1,0:T(8,128)(2,1)} %assemble.1), channel_id=1, source_target_pairs={{0,4},{1,5},{2,6},{3,7},{4,0},{5,1},{6,2},{7,3},{8,12},{9,13},{10,... | collective-permute-start | bytes 1572872 | tf_op jit(solution)/shard_map/ppermute | solution.py:628
  35.6 12.5 %collective-permute-start.6 = (bf16[128,1024]{1,0:T(8,128)(2,1)}, bf16[128,1024]{1,0:T(8,128)(2,1)S(1)}, u32[]{:S(2)}, u32[]{:S(2)}) collective-permute-start(bf16[128,1024]{1,0:T(8,128)(2,1)} %get-tuple-element.131), channel_id=1, source_target_pairs={{0,1},{1,0},{2,3},{3,2},{4,5},{5,4},{6,7},{7,6},{8,9},{9,8},{10,11... | collective-permute-start | bytes 786440 | tf_op jit(solution)/shard_map/ppermute | solution.py:591
  36.1 17.6 %collective-permute-start.7 = (bf16[128,1024]{1,0:T(8,128)(2,1)}, bf16[128,1024]{1,0:T(8,128)(2,1)S(1)}, u32[]{:S(2)}, u32[]{:S(2)}) collective-permute-start(bf16[128,1024]{1,0:T(8,128)(2,1)} %get-tuple-element.132), channel_id=1, source_target_pairs={{0,2},{1,3},{2,0},{3,1},{4,6},{5,7},{6,4},{7,5},{8,10},{9,11},{10,... | collective-permute-start | bytes 786440 | tf_op jit(solution)/shard_map/ppermute | solution.py:591
  37.4 22.9 %collective-permute-start.8 = (bf16[128,1024]{1,0:T(8,128)(2,1)}, bf16[128,1024]{1,0:T(8,128)(2,1)S(1)}, u32[]{:S(2)}, u32[]{:S(2)}) collective-permute-start(bf16[128,1024]{1,0:T(8,128)(2,1)} %get-tuple-element.133), channel_id=1, source_target_pairs={{0,3},{1,2},{2,1},{3,0},{4,7},{5,6},{6,5},{7,4},{8,11},{9,10},{10,... | collective-permute-start | bytes 786440 | tf_op jit(solution)/shard_map/ppermute | solution.py:591
  60.4 18.9 %collective-permute-start.10 = (bf16[128,1024]{1,0:T(8,128)(2,1)}, bf16[128,1024]{1,0:T(8,128)(2,1)S(1)}, u32[]{:S(2)}, u32[]{:S(2)}) collective-permute-start(bf16[128,1024]{1,0:T(8,128)(2,1)} %get-tuple-element.151), channel_id=1, source_target_pairs={{0,1},{1,0},{2,3},{3,2},{4,5},{5,4},{6,7},{7,6},{8,9},{9,8},{10,11... | collective-permute-start | bytes 786440 | tf_op jit(solution)/shard_map/ppermute | solution.py:591
  61.2 18.2 %collective-permute-start.11 = (bf16[128,1024]{1,0:T(8,128)(2,1)}, bf16[128,1024]{1,0:T(8,128)(2,1)S(1)}, u32[]{:S(2)}, u32[]{:S(2)}) collective-permute-start(bf16[128,1024]{1,0:T(8,128)(2,1)} %get-tuple-element.152), channel_id=1, source_target_pairs={{0,2},{1,3},{2,0},{3,1},{4,6},{5,7},{6,4},{7,5},{8,10},{9,11},{10,... | collective-permute-start | bytes 786440 | tf_op jit(solution)/shard_map/ppermute | solution.py:591
  63.4 15.9 %collective-permute-start.12 = (bf16[128,1024]{1,0:T(8,128)(2,1)}, bf16[128,1024]{1,0:T(8,128)(2,1)S(1)}, u32[]{:S(2)}, u32[]{:S(2)}) collective-permute-start(bf16[128,1024]{1,0:T(8,128)(2,1)} %get-tuple-element.153), channel_id=1, source_target_pairs={{0,3},{1,2},{2,1},{3,0},{4,7},{5,6},{6,5},{7,4},{8,11},{9,10},{10,... | collective-permute-start | bytes 786440 | tf_op jit(solution)/shard_map/ppermute | solution.py:591
  65.6 12.9 %collective-permute-start.14 = (bf16[256,512]{1,0:T(8,128)(2,1)S(1)}, bf16[256,512]{1,0:T(8,128)(2,1)S(1)}, u32[]{:S(2)}, u32[]{:S(2)}) collective-permute-start(bf16[256,512]{1,0:T(8,128)(2,1)S(1)} %get-tuple-element.196), channel_id=1, source_target_pairs={{16,0},{24,8},{17,1},{25,9},{18,2},{26,10},{19,3},{27,11},{20,4},{... | collective-permute-start | bytes 786440 | tf_op jit(solution)/shard_map/ppermute | solution.py:636
  79.3 21.5 %collective-permute-start.15 = (bf16[128,1024]{1,0:T(8,128)(2,1)}, bf16[128,1024]{1,0:T(8,128)(2,1)S(1)}, u32[]{:S(2)}, u32[]{:S(2)}) collective-permute-start(bf16[128,1024]{1,0:T(8,128)(2,1)} %get-tuple-element.161), channel_id=1, source_target_pairs={{0,1},{1,0},{2,3},{3,2},{4,5},{5,4},{6,7},{7,6},{8,9},{9,8},{10,11... | collective-permute-start | bytes 786440 | tf_op jit(solution)/shard_map/ppermute | solution.py:591
  80.0 20.9 %collective-permute-start.16 = (bf16[128,1024]{1,0:T(8,128)(2,1)}, bf16[128,1024]{1,0:T(8,128)(2,1)S(1)}, u32[]{:S(2)}, u32[]{:S(2)}) collective-permute-start(bf16[128,1024]{1,0:T(8,128)(2,1)} %get-tuple-element.162), channel_id=1, source_target_pairs={{0,2},{1,3},{2,0},{3,1},{4,6},{5,7},{6,4},{7,5},{8,10},{9,11},{10,... | collective-permute-start | bytes 786440 | tf_op jit(solution)/shard_map/ppermute | solution.py:591
  81.8 19.6 %collective-permute-start.17 = (bf16[128,1024]{1,0:T(8,128)(2,1)}, bf16[128,1024]{1,0:T(8,128)(2,1)S(1)}, u32[]{:S(2)}, u32[]{:S(2)}) collective-permute-start(bf16[128,1024]{1,0:T(8,128)(2,1)} %get-tuple-element.163), channel_id=1, source_target_pairs={{0,3},{1,2},{2,1},{3,0},{4,7},{5,6},{6,5},{7,4},{8,11},{9,10},{10,... | collective-permute-start | bytes 786440 | tf_op jit(solution)/shard_map/ppermute | solution.py:591
  82.9 16.5 %collective-permute-start.18 = (bf16[128,512]{1,0:T(8,128)(2,1)}, bf16[128,512]{1,0:T(8,128)(2,1)S(1)}, u32[]{:S(2)}, u32[]{:S(2)}) collective-permute-start(bf16[128,512]{1,0:T(8,128)(2,1)} %get-tuple-element.164), channel_id=1, source_target_pairs={{0,4},{1,5},{2,6},{3,7},{4,0},{5,1},{6,2},{7,3},{8,12},{9,13},{10,... | collective-permute-start | bytes 393224 | tf_op jit(solution)/shard_map/ppermute | solution.py:591
  85.4 15.4 %collective-permute-start.19 = (bf16[128,512]{1,0:T(8,128)(2,1)}, bf16[128,512]{1,0:T(8,128)(2,1)S(1)}, u32[]{:S(2)}, u32[]{:S(2)}) collective-permute-start(bf16[128,512]{1,0:T(8,128)(2,1)} %get-tuple-element.165), channel_id=1, source_target_pairs={{0,5},{1,4},{2,7},{3,6},{4,1},{5,0},{6,3},{7,2},{8,13},{9,12},{10,... | collective-permute-start | bytes 393224 | tf_op jit(solution)/shard_map/ppermute | solution.py:591
  101.5 10.1 %collective-permute-start.22 = (f32[512,512]{1,0:T(8,128)}, f32[512,512]{1,0:T(8,128)S(1)}, u32[]{:S(2)}, u32[]{:S(2)}) collective-permute-start(f32[512,512]{1,0:T(8,128)} %get-tuple-element.172), channel_id=1, source_target_pairs={{0,8},{8,0},{16,24},{24,16},{1,9},{9,1},{17,25},{25,17},{2,10},{10... | collective-permute-start | bytes 3145736 | tf_op jit(solution)/shard_map/ppermute | solution.py:652
  101.5 12.3 %collective-permute-start.20 = (bf16[128,512]{1,0:T(8,128)(2,1)}, bf16[128,512]{1,0:T(8,128)(2,1)}, u32[]{:S(2)}, u32[]{:S(2)}) collective-permute-start(bf16[128,512]{1,0:T(8,128)(2,1)} %get-tuple-element.169), channel_id=1, source_target_pairs={{0,6},{1,7},{2,4},{3,5},{4,2},{5,3},{6,0},{7,1},{8,14},{9,15},{10,... | collective-permute-start | bytes 393224 | tf_op jit(solution)/shard_map/ppermute | solution.py:591
  102.0 14.4 %collective-permute-start.21 = (bf16[128,512]{1,0:T(8,128)(2,1)}, bf16[128,512]{1,0:T(8,128)(2,1)}, u32[]{:S(2)}, u32[]{:S(2)}) collective-permute-start(bf16[128,512]{1,0:T(8,128)(2,1)} %get-tuple-element.170), channel_id=1, source_target_pairs={{0,7},{1,6},{2,5},{3,4},{4,3},{5,2},{6,1},{7,0},{8,15},{9,14},{10,... | collective-permute-start | bytes 393224 | tf_op jit(solution)/shard_map/ppermute | solution.py:591
  104.5 35.4 %collective-permute-start.26 = (bf16[256,512]{1,0:T(8,128)(2,1)}, bf16[256,512]{1,0:T(8,128)(2,1)}, u32[]{:S(2)}, u32[]{:S(2)}) collective-permute-start(bf16[256,512]{1,0:T(8,128)(2,1)} %add_convert_fusion), channel_id=1, source_target_pairs={{0,4},{1,5},{2,6},{3,7},{4,0},{5,1},{6,2},{7,3},{8,12},{9,13},{10,... | collective-permute-start | bytes 786440 | tf_op jit(solution)/shard_map/ppermute | solution.py:650
  116.4 23.5 %collective-permute-start.25 = (bf16[256,512]{1,0:T(8,128)(2,1)S(1)}, bf16[256,512]{1,0:T(8,128)(2,1)S(1)}, u32[]{:S(2)}, u32[]{:S(2)}) collective-permute-start(bf16[256,512]{1,0:T(8,128)(2,1)S(1)} %dynamic-slice_convert_fusion), channel_id=1, source_target_pairs={{0,16},{8,24},{16,0},{24,8},{1,17},{9,25},{17,1},{25,9},{2,18},{10... | collective-permute-start | bytes 786440 | tf_op jit(solution)/shard_map/ppermute | solution.py:662
  124.7 12.5 %collective-permute-start.24 = (bf16[4,3,2,512]{3,2,1,0:T(2,128)(2,1)}, bf16[4,3,2,512]{3,2,1,0:T(2,128)(2,1)S(1)}, u32[]{:S(2)}, u32[]{:S(2)}) collective-permute-start(bf16[4,3,2,512]{3,2,1,0:T(2,128)(2,1)} %edge_other.1), channel_id=1, source_target_pairs={{1,0},{2,1},{3,2},{4,3},{5,4},{6,5},{7,6},{9,8},{10,9},{11,10},{12... | collective-permute-start | bytes 73736 | tf_op jit(solution)/shard_map/ppermute | solution.py:683
  128.1 9.1 %collective-permute-start.23 = (bf16[4,3,2,512]{3,2,1,0:T(2,128)(2,1)S(1)}, bf16[4,3,2,512]{3,2,1,0:T(2,128)(2,1)S(1)}, u32[]{:S(2)}, u32[]{:S(2)}) collective-permute-start(bf16[4,3,2,512]{3,2,1,0:T(2,128)(2,1)S(1)} %copy-done.21), channel_id=1, source_target_pairs={{1,0},{2,1},{3,2},{4,3},{5,4},{6,5},{7,6},{9,8},{10,9},{11,10},{12... | collective-permute-start | bytes 73736 | tf_op jit(solution)/shard_map/ppermute | solution.py:683
  (25 other events, 231.9 us)

commit v4 on v3

--- a/solution.py
+++ b/solution.py
@@ -9,13 +9,12 @@
 from jax.experimental.pallas import tpu as pltpu
 from jax.sharding import PartitionSpec as P
 
-VMEM_LIMIT = 56 * 1024 * 1024
 STEP = 128
 STRIP = 128
 
 
-def params():
-    return pltpu.CompilerParams(vmem_limit_bytes=VMEM_LIMIT)
+def params(mebibytes):
+    return pltpu.CompilerParams(vmem_limit_bytes=mebibytes * 1024 * 1024)
 
 
 def cost(flops, moved):
@@ -70,7 +69,8 @@
 
 
 def gate_kernel(hc, count, base, feats_ref, before, taps_ref, grad_ref, *refs):
-    outs, refs = refs[:hc], refs[hc:]
+    crossing = base > 0
+    outs, refs = refs[: hc * (2 if crossing else 1)], refs[hc * (2 if crossing else 1) :]
     parts, taps, stage, in_sem, small_sem, out_sem = refs
     rows, cols = parts.shape[2:]
     me, half, core = where(hc)
@@ -104,6 +104,9 @@
                 parts[j, 3, :, strip].astype(jnp.float32) * query
             ).astype(jnp.bfloat16)
         stores += run([pltpu.make_async_copy(stage.at[j], outs[j], out_sem.at[j])])
+        if crossing:
+            crossed = stage.at[j, :, pl.ds(pl.multiple_of(half * cols, cols), cols)]
+            stores += run([pltpu.make_async_copy(crossed, outs[hc + j], out_sem.at[hc + j])])
     finish(stores)
 
 
@@ -111,6 +114,7 @@
     rows = feats.shape[0]
     hc = count // 2
     shapes = [jax.ShapeDtypeStruct((rows, 2 * cols), jnp.bfloat16)] * hc
+    shapes = shapes + [jax.ShapeDtypeStruct((rows, cols), jnp.bfloat16)] * hc
     hbm = pl.BlockSpec(memory_space=pl.ANY)
     return pl.pallas_call(
         functools.partial(gate_kernel, hc, count, base),
@@ -125,7 +129,7 @@
             pltpu.SemaphoreType.DMA,
             pltpu.SemaphoreType.DMA((len(shapes),)),
         ],
-        compiler_params=params(),
+        compiler_params=params(56),
         cost_estimate=cost(20 * rows * cols * hc, 12 * rows * cols * hc),
         name="gate_other",
     )(feats, before, taps, grad_out)
@@ -182,47 +186,12 @@
             pltpu.SemaphoreType.DMA,
             pltpu.SemaphoreType.DMA((len(shapes),)),
         ],
-        compiler_params=params(),
+        compiler_params=params(56),
         cost_estimate=cost(8 * length * length * cols, 20 * length * cols),
         name="prepare",
     )(filt, high, low, feats, before, taps, grad_out)
 
 
-def assemble_kernel(hc, *refs):
-    pieces, out_ref, stage, in_sem, out_sem = refs[:hc], *refs[hc:]
-    rows = pieces[0].shape[0]
-    cols = pieces[0].shape[1] // 2
-    me, half, _ = where(hc)
-    side = pl.ds(pl.multiple_of(half * cols, cols), cols)
-    loads = run([pltpu.make_async_copy(pieces[j].at[:, side], stage.at[j], in_sem.at[j]) for j in range(hc)])
-    stores = []
-    for j in range(hc):
-        finish([loads[j]])
-        place = pl.ds(pl.multiple_of(((me % hc) ^ j) * rows, rows), rows)
-        stores += run([pltpu.make_async_copy(stage.at[j], out_ref.at[place], out_sem.at[j])])
-    finish(stores)
-
-
-def assemble(pieces):
-    hc = len(pieces)
-    rows, width = pieces[0].shape
-    hbm = pl.BlockSpec(memory_space=pl.ANY)
-    return pl.pallas_call(
-        functools.partial(assemble_kernel, hc),
-        in_specs=[hbm] * hc,
-        out_specs=hbm,
-        out_shape=jax.ShapeDtypeStruct((hc * rows, width // 2), jnp.bfloat16),
-        scratch_shapes=[
-            pltpu.VMEM((hc, rows, width // 2), jnp.bfloat16),
-            pltpu.SemaphoreType.DMA((hc,)),
-            pltpu.SemaphoreType.DMA((hc,)),
-        ],
-        compiler_params=params(),
-        cost_estimate=cost(0, 2 * hc * rows * width),
-        name="assemble",
-    )(*pieces)
-
-
 def times(a_re, a_im, b_re, b_im):
     return a_re * b_re - a_im * b_im, a_re * b_im + a_im * b_re
 
@@ -234,14 +203,14 @@
 def spectral_kernel(hc, rows, home, scale, *refs):
     tables, refs = refs[: 4 if home else 5], refs[4 if home else 5 :]
     pieces, refs = refs[:hc], refs[hc:]
-    cross_ref = None
+    crosses = ()
     if home:
-        cross_ref, refs = refs[0], refs[1:]
-    outs, refs = refs[:hc], refs[hc:]
+        crosses, refs = refs[:hc], refs[hc:]
+    outs, refs = refs[: 1 if home else hc], refs[1 if home else hc :]
     cross_outs = ()
     if home:
         cross_outs, refs = refs[:hc], refs[hc:]
-    corr_send, corr_keep, refs = refs[0], refs[1], refs[2:]
+    sums, refs = refs[:2], refs[2:]
     held, refs = refs[: len(tables)], refs[len(tables) :]
     data, spec, prod, res, corr, piece_sem, table_sem, out_sem, corr_sem = refs[:9]
     forward_ref, inverse_ref = held[:2]
@@ -261,9 +230,12 @@
     piece_copies = run(
         [pltpu.make_async_copy(pieces[j], data.at[place(j), : 2 * cols], piece_sem.at[j]) for j in range(hc)]
     )
-    cross_copies = []
-    if home:
-        cross_copies = run([pltpu.make_async_copy(cross_ref, data.at[:, 2 * cols :], piece_sem.at[hc])])
+    cross_copies = run(
+        [
+            pltpu.make_async_copy(crosses[j], data.at[place(j), 2 * cols :], piece_sem.at[hc + j])
+            for j in range(len(crosses))
+        ]
+    )
     filter_copies = [copy for i in range(2, len(tables)) for copy in load(i)]
     inverse_copy = load(1)
     finish(forward_copy)
@@ -347,9 +319,12 @@
     finish(inverse_copy)
     res[:, :cols] = back(0).astype(jnp.bfloat16)
     res[:, cols : 2 * cols] = back(1).astype(jnp.bfloat16)
-    stores = run(
-        [pltpu.make_async_copy(res.at[place(j), : 2 * cols], outs[j], out_sem.at[j]) for j in range(hc)]
-    )
+    if home:
+        stores = run([pltpu.make_async_copy(res.at[:, : 2 * cols], outs[0], out_sem.at[0])])
+    else:
+        stores = run(
+            [pltpu.make_async_copy(res.at[place(j), : 2 * cols], outs[j], out_sem.at[j]) for j in range(hc)]
+        )
     if home:
         res[:, 2 * cols :] = back(2).astype(jnp.bfloat16)
         stores += run(
@@ -361,38 +336,41 @@
     quarter = size // 2
     for x in range(2 if home else 1):
         corr[x] = back((3 if home else 2) + x) * scale
-        for i, (ref, which) in enumerate(((corr_send, 1 - core), (corr_keep, core))):
+        for i, which in enumerate((1 - core, core)):
             lags = pl.ds(pl.multiple_of(which * quarter, quarter), quarter)
             stores += run(
                 [
                     pltpu.make_async_copy(
-                        corr.at[x, lags], ref.at[x * quarter : (x + 1) * quarter], corr_sem.at[x, i]
+                        corr.at[x, lags], sums[i].at[x * quarter : (x + 1) * quarter], corr_sem.at[x, i]
                     )
                 ]
             )
     finish(stores)
 
 
-def spectral(forward, inverse, filters, pieces, cross, scale):
+def spectral(forward, inverse, filters, pieces, crosses, scale):
     hc = len(pieces)
     rows, width = pieces[0].shape
     cols = width // 2
     size = hc * rows
-    home = cross is not None
+    home = len(crosses) > 0
     hbm = pl.BlockSpec(memory_space=pl.ANY)
     tables = [forward, inverse, *filters]
-    arrived = [*pieces, cross] if home else pieces
+    arrived = [*pieces, *crosses]
     ins = 3 if home else 2
     parts = 5 if home else 3
-    shapes = [jax.ShapeDtypeStruct((rows, width), jnp.bfloat16)] * hc
+    share = jax.ShapeDtypeStruct((size if home else size // 2, cols), jnp.float32)
+    sums = [share, share]
     if home:
+        shapes = [jax.ShapeDtypeStruct((size, width), jnp.bfloat16)]
         shapes = shapes + [jax.ShapeDtypeStruct((rows, cols), jnp.bfloat16)] * hc
-    corr = jax.ShapeDtypeStruct((size if home else size // 2, cols), jnp.float32)
+    else:
+        shapes = [jax.ShapeDtypeStruct((rows, width), jnp.bfloat16)] * hc
     return pl.pallas_call(
         functools.partial(spectral_kernel, hc, rows, home, scale),
         in_specs=[hbm] * (len(tables) + len(arrived)),
-        out_specs=[hbm] * (len(shapes) + 2),
-        out_shape=shapes + [corr, corr],
+        out_specs=[hbm] * (len(shapes) + len(sums)),
+        out_shape=shapes + sums,
         scratch_shapes=[pltpu.VMEM(t.shape, t.dtype) for t in tables]
         + [
             pltpu.VMEM((size, ins * cols), jnp.bfloat16),
@@ -402,11 +380,11 @@
             pltpu.VMEM((2 if home else 1, size, cols), jnp.float32),
             pltpu.SemaphoreType.DMA((len(arrived),)),
             pltpu.SemaphoreType.DMA((len(tables),)),
-            pltpu.SemaphoreType.DMA((len(shapes),)),
+            pltpu.SemaphoreType.DMA((2 * hc,)),
             pltpu.SemaphoreType.DMA((2, 2)),
         ]
         + ([] if home else [pltpu.VMEM((2 * size, cols), jnp.float32)]),
-        compiler_params=params(),
+        compiler_params=params(56 if home else 36),
         cost_estimate=cost(4 * size * size * cols * (ins + parts), 8 * size * size + 30 * size * cols),
         name="spectral_home" if home else "spectral_other",
     )(*tables, *arrived)
@@ -414,15 +392,18 @@
 
 def final_kernel(hc, count, base, top, aliased, *refs):
     feats_ref, before, grad_ref, taps_ref = refs[:4]
-    pieces, refs = refs[4 : 4 + hc], refs[4 + hc :]
     crosses = ()
     if base > 0:
-        crosses, refs = refs[:hc], refs[hc:]
+        pieces, crosses, refs = refs[4 : 4 + hc], refs[4 + hc : 4 + 2 * hc], refs[4 + 2 * hc :]
+    else:
+        slots = [(lax.axis_index("ctx") % hc) ^ j for j in range(hc)]
+        pieces, refs = [refs[4].at[slot] for slot in slots], refs[5:]
     if aliased:
         refs = refs[1:]
     out_ref = last_ref = stage = last = None
     if top:
-        edge_ref, parts, taps, back, edge, in_sem, small_sem, back_sem, end_sem = refs
+        first_ref, edge_ref, parts, taps, back, edges, in_sem, small_sem, back_sem, end_sem = refs
+        edge = edges.at[1]
     else:
         out_ref, edge_ref, last_ref, parts, taps, back, edge, last, stage = refs[:9]
         in_sem, small_sem, back_sem, end_sem, out_sem = refs[9:]
@@ -433,6 +414,8 @@
         return pl.ds(pl.multiple_of((region * count + (me ^ (base + j))) * cols, cols), cols)
 
     small = run([pltpu.make_async_copy(taps_ref, taps, small_sem)])
+    if top:
+        small += run([pltpu.make_async_copy(first_ref, edges.at[0], end_sem.at[1])])
     loads = []
     for j in range(hc):
         copies = [
@@ -488,31 +471,35 @@
                     for r in range(3)
                 ]
             )
-    stores += run([pltpu.make_async_copy(edge, edge_ref, end_sem.at[0])])
+    stores += run([pltpu.make_async_copy(edges if top else edge, edge_ref, end_sem.at[0])])
     if not top:
         stores += run([pltpu.make_async_copy(last, last_ref, end_sem.at[1])])
     finish(stores)
 
 
-def final(feats, before, grad_out, taps, pieces, crosses, so_far, count, base, top=False):
-    hc = len(pieces)
+def final(feats, before, grad_out, taps, pieces, crosses, so_far, count, base, first=None):
+    hc = count // 2
+    top = first is not None
     rows = 16 if top else feats.shape[0]
-    cols = pieces[0].shape[1] // 2
+    cols = pieces[0].shape[-1] // 2
     hbm = pl.BlockSpec(memory_space=pl.ANY)
     arrived = [*pieces, *crosses]
     args = [feats, before, grad_out, taps, *arrived]
     aliases = {}
+    if top:
+        args.append(first)
     if so_far is not None:
         args.append(so_far)
         aliases = {len(args) - 1: 0}
     edge = jax.ShapeDtypeStruct((hc, 3, 2, cols), jnp.bfloat16)
     last = jax.ShapeDtypeStruct((hc, 3, 16, cols), jnp.float32)
-    shapes = [edge] if top else [jax.ShapeDtypeStruct(feats.shape, jnp.bfloat16), edge, last]
+    edges = jax.ShapeDtypeStruct((2, *edge.shape), edge.dtype)
+    shapes = [edges] if top else [jax.ShapeDtypeStruct(feats.shape, jnp.bfloat16), edge, last]
     scratch = [
         pltpu.VMEM((hc, 3, rows, cols), jnp.bfloat16),
         pltpu.VMEM(taps.shape, taps.dtype),
         pltpu.VMEM((hc, rows, (3 if base > 0 else 2) * cols), jnp.bfloat16),
-        pltpu.VMEM(edge.shape, edge.dtype),
+        pltpu.VMEM(edges.shape if top else edge.shape, edge.dtype),
     ]
     if not top:
         scratch += [
@@ -522,7 +509,7 @@
     scratch += [
         pltpu.SemaphoreType.DMA((hc, 3)),
         pltpu.SemaphoreType.DMA,
-        pltpu.SemaphoreType.DMA((len(arrived),)),
+        pltpu.SemaphoreType.DMA((2 * hc,)),
         pltpu.SemaphoreType.DMA((2,)),
     ]
     if not top:
@@ -535,20 +522,21 @@
         scratch_shapes=scratch,
         out_shape=shapes,
         input_output_aliases=aliases,
-        compiler_params=params(),
+        compiler_params=params(16 if top or base > 0 else 56),
         cost_estimate=cost(30 * rows * cols * hc, 16 * rows * cols * hc),
         name=name,
     )(*args)
 
 
-def fix_kernel(hc, taps_ref, eh_ref, eo_ref, lh_ref, lo_ref, _, out_ref, stage, sem):
+def fix_kernel(hc, taps_ref, edge_ref, lh_ref, lo_ref, *refs):
+    own_ref, *sums, _, out_ref, filt_ref, stage, sem = refs
     me, half, _ = where(hc)
-    cols = eh_ref.shape[3]
+    cols = edge_ref.shape[4]
     width = out_ref.shape[1] // 3
     turn = me == hc - 1
     spot = lax.broadcasted_iota(jnp.int32, (16, 1), 0)
     for slot, last in enumerate((lh_ref, lo_ref)):
-        mine, swapped = (eh_ref, eo_ref) if slot == 0 else (eo_ref, eh_ref)
+        mine, swapped = edge_ref.at[slot], edge_ref.at[1 - slot]
         first = jnp.where(half == slot, 0, hc)
         for j in range(hc):
             for region in range(3):
@@ -565,24 +553,32 @@
                 stage[:, col] = (last[j, region] + add).astype(jnp.bfloat16)
     copy = pltpu.make_async_copy(stage, out_ref.at[pl.ds(out_ref.shape[0] - 16, 16)], sem)
     copy.start()
+    lags = filt_ref.shape[0]
+    total = own_ref[pl.ds(pl.multiple_of((lax.axis_index("dp") // 2) * lags, lags), lags), :]
+    for ref in sums:
+        total += ref[...].astype(jnp.float32)
+    filt_ref[...] = total
     copy.wait()
 
 
-def fix(taps, edge_home, edge_other, last_home, last_other, result):
-    hc = edge_home.shape[0]
+def fix(taps, edges, last_home, last_other, sums, result):
+    hc = edges.shape[1]
     vmem = pl.BlockSpec(memory_space=pltpu.VMEM)
     hbm = pl.BlockSpec(memory_space=pl.ANY)
     return pl.pallas_call(
         functools.partial(fix_kernel, hc),
-        in_specs=[vmem] * 5 + [hbm],
-        out_specs=hbm,
-        out_shape=jax.ShapeDtypeStruct(result.shape, result.dtype),
+        in_specs=[vmem] * (4 + len(sums)) + [hbm],
+        out_specs=[hbm, vmem],
+        out_shape=[
+            jax.ShapeDtypeStruct(result.shape, result.dtype),
+            jax.ShapeDtypeStruct(sums[-1].shape, jnp.float32),
+        ],
         scratch_shapes=[pltpu.VMEM((16, result.shape[1]), jnp.bfloat16), pltpu.SemaphoreType.DMA],
-        input_output_aliases={5: 0},
-        compiler_params=params(),
+        input_output_aliases={4 + len(sums): 0},
+        compiler_params=params(16),
         cost_estimate=cost(16 * 8 * result.shape[1], 128 * result.shape[1]),
         name="fix",
-    )(taps, edge_home, edge_other, last_home, last_other, result)
+    )(taps, edges, last_home, last_other, *sums, result)
 
 
 def exchange(pieces, base):
@@ -593,12 +589,17 @@
     ]
 
 
+def within(stacked):
+    count = lax.axis_size("ctx")
+    groups = [list(range(count // 2)), list(range(count // 2, count))]
+    return lax.all_to_all(stacked, "ctx", 0, 0, axis_index_groups=groups, tiled=True)
+
+
 def half_shards(feats, short_weight, grad_out, filt):
     length, block = filt.shape
     count = lax.axis_size("ctx")
     hc = count // 2
     size = length // 2
-    quarter = length // 4
     feats, grad_out = feats[0], grad_out[0]
     rows = feats.shape[0]
     high, low = odd_tables(size)
@@ -607,6 +608,7 @@
     me = lax.axis_index("ctx")
     dp = lax.axis_index("dp")
     core, x = dp % 2, dp // 2
+    quarter = length // 4
     tie = lax.optimization_barrier
     cores = [(i, i ^ 1) for i in range(4)]
 
@@ -618,58 +620,49 @@
     gated = gate(feats, before, short_weight, grad_out, count, block, hc)
 
     ready, gated = tie((before, gated))
-    other_pieces = exchange(gated, 0)
+    other_pieces, across = exchange(gated[:hc], 0), gated[hc:]
+    sent = exchange(across[:1], hc)
     outs = prepare(filt, high, low, feats, ready, short_weight, grad_out, scale, count)
-    outs, other_pieces, part = tie((outs, other_pieces, part))
+    outs, other_pieces, sent, across, part = tie((outs, other_pieces, sent, across, part))
     near, far = outs[hc:]
 
     home_pieces = exchange(outs[:hc], 0)
-    cross, part = tie((assemble(other_pieces), part))
-    cross = lax.ppermute(cross, "ctx", [(i, i ^ hc) for i in range(count)])
     rest = lax.ppermute(part, "dp", cores)
-    outs = spectral(high, inverse, (low, part, rest), other_pieces, None, scale)
-    outs, home_pieces, cross = tie((outs, home_pieces, cross))
+    sent = list(sent) + exchange(across[1:3], hc + 1)
+    outs = spectral(high, inverse, (low, part, rest), other_pieces, (), scale)
+    far, outs, home_pieces, sent, across = tie((far, outs, home_pieces, sent, across))
 
     other_back = exchange(outs[:hc], 0)
+    sent = list(sent) + exchange(across[3:], hc + 3)
     send, keep = outs[hc:]
     summed = keep + lax.ppermute(send, "dp", cores)
-    summed = summed + lax.ppermute(summed.astype(jnp.bfloat16), "dp", [(2, 0), (3, 1)]).astype(jnp.float32)
-    crossing = summed.astype(jnp.bfloat16)
-    outs = spectral(high, inverse, (near, far), home_pieces, cross, scale)
-    outs, other_back, crossing = tie((outs, other_back, crossing))
-
-    home_back = exchange(outs[:hc], 0)
-    cross_outs = outs[hc : 2 * hc]
-    early = exchange(cross_outs[: hc // 2], hc)
-    late, sums, home_back, early, crossing = tie(
-        (cross_outs[hc // 2 :], outs[2 * hc :], home_back, early, crossing)
-    )
-
-    cross_back = list(early) + exchange(late, hc + hc // 2)
-    owners = [(d * count + i, d * count + (i ^ hc)) for d in range(2) for i in range(count)]
-    filt_other = lax.ppermute(crossing, ("dp", "ctx"), owners)
-    send, keep = sums
+    crossed = lax.ppermute(summed.astype(jnp.bfloat16), "ctx", [(i, i ^ hc) for i in range(count)])
+    outs = spectral(high, inverse, (near, far), home_pieces, sent, scale)
+    outs, other_back, crossed = tie((outs, other_back, crossed))
+
+    home_back = within(outs[0].reshape(hc, rows, 2 * block))
+    cross_back = exchange(outs[1 : 1 + hc], hc)
+    send, keep = outs[1 + hc :]
     came = lax.ppermute(send, "dp", cores)
     result, edge_home, last_home = final(
-        feats, before, grad_out, short_weight, home_back, (), None, count, 0
-    )
-    keep, came, edge_home = tie((keep, came, edge_home))
-    summed = keep + came
-    there = lax.dynamic_slice_in_dim(summed, (1 - x) * quarter, quarter, 0).astype(jnp.bfloat16)
-    here = lax.dynamic_slice_in_dim(summed, x * quarter, quarter, 0)
-    cross_back, there, edge_home = tie((cross_back, there, edge_home))
-
+        feats, before, grad_out, short_weight, [home_back], (), None, count, 0
+    )
+    keep, came, crossed, edge_home = tie((keep, came, crossed, edge_home))
+    crossed = jnp.concatenate([crossed.astype(jnp.float32), jnp.zeros((quarter, block), jnp.float32)], axis=0)
+    home_sum = keep + came + crossed
+    there = lax.dynamic_slice_in_dim(home_sum, (1 - x) * quarter, quarter, 0).astype(jnp.bfloat16)
+    cross_back, edge_home, there = tie((cross_back, edge_home, there))
+
+    (edges,) = final(
+        feats, before, grad_out, short_weight, other_back, cross_back, None, count, hc, edge_home
+    )
+    edges, there = tie((edges, there))
+    edges = from_behind(edges, "ctx", -1)
     there = lax.ppermute(there, "dp", [(i, i ^ 2) for i in range(4)])
-    filt_out = here + there.astype(jnp.float32) + filt_other.astype(jnp.float32)
-    edge_home = from_behind(edge_home, "ctx", -1)
-    (edge_other,) = final(
-        feats, before, grad_out, short_weight, other_back, cross_back, None, count, hc, True
-    )
-    edge_other = from_behind(edge_other, "ctx", -1)
     result, _, last_other = final(
         feats, before, grad_out, short_weight, other_back, cross_back, result, count, hc
     )
-    result = fix(short_weight, edge_home, edge_other, last_home, last_other, result)
+    result, filt_out = fix(short_weight, edges, last_home, last_other, [home_sum, there], result)
     return (result[None], filt_out)
 
 

time: 143 us -> 129 us (0.902)
  the two profiles are of different devices: /device:TPU:18 before, /device:TPU:0 now
where the time goes in v4:
time: 129 us
  Pallas kernels  43.8 us (34%)
  starting transfers between devices  41.3 us (32%)
  waiting for transfers between devices  35.6 us (28%)
  local copies, waits for them, and re-layouts  3.77 us (3%)
  other arithmetic  2.8 us (2%)
    ppermute x17, starting transfers between devices, exchange(): lax.ppermute(piece, 'ctx', [(i, i ^ base + j) for i in devices])  26.9 us
    ppermute x17, waiting for transfers between devices, exchange(): lax.ppermute(piece, 'ctx', [(i, i ^ base + j) for i in devices])  21.9 us
    pallas_call x2, Pallas kernels, spectral(): pl.pallas_call(functools.partial(spectral_kernel, hc, rows, home, scale),...  15.9 us
    all_to_all x1, waiting for transfers between devices, within(): lax.all_to_all(stacked, 'ctx', 0, 0, axis_index_groups=groups, tiled=True)  12.9 us
    pallas_call x1, Pallas kernels, prepare(): pl.pallas_call(functools.partial(prepare_kernel, hc, count, scale), in_sp...  10.8 us
    pallas_call x3, Pallas kernels, final(): pl.pallas_call(functools.partial(final_kernel, hc, count, base, top, so_f...  10.8 us
    ppermute x2, starting transfers between devices, from_behind(): return lax.ppermute(block, axis, route)  6.15 us
    pallas_call x1, Pallas kernels, gate(): pl.pallas_call(functools.partial(gate_kernel, hc, count, base), in_specs=...  4.66 us
  transfers between devices with their start and end apart: 26, of which 7 were waited for; matrix products, arithmetic and copies ran while one was open for 2% of the time, Pallas kernels for 32%

profile of v4, /device:TPU:0, one launch (start us, length us, event | category | flops | bytes accessed | tf_op | source)
XLA Modules:
  0.0 128.5 jit_solution(276603823527863628)
XLA Ops:
  1.6 4.9 %collective-permute-start = (bf16[2,12288]{1,0:T(2,128)(2,1)S(1)}, bf16[2,12288]{1,0:T(2,128)(2,1)S(1)}, u32[]{:S(2)}, u32[]{:S(2)}) collective-permute-start(bf16[2,12288]{1,0:T(2,128)(2,1)S(1)} %slice_bitcast_fusion), channel_id=1, source_target_pairs={{0,1},{1,2},{2,3},{3,4},{4,5},{5,6},{6,7},{8,9},{9,10},{10,11},{11... | collective-permute-start | bytes 147464 | tf_op jit(solution)/shard_map/ppermute | solution.py:676
  7.6 2.7 %collective-permute-start.5 = (bf16[256,512]{1,0:T(8,128)(2,1)S(1)}, bf16[256,512]{1,0:T(8,128)(2,1)S(1)}, u32[]{:S(2)}, u32[]{:S(2)}) collective-permute-start(bf16[256,512]{1,0:T(8,128)(2,1)S(1)} %multiply_convert_fusion), channel_id=1, source_target_pairs={{0,4},{1,5},{2,6},{3,7},{4,0},{5,1},{6,2},{7,3},{8,12},{9,13},{10,... | collective-permute-start | bytes 786440 | tf_op jit(solution)/shard_map/ppermute | solution.py:619
  10.9 4.7 %gate_other.1 = (bf16[128,1024]{1,0:T(8,128)(2,1)}, bf16[128,1024]{1,0:T(8,128)(2,1)}, bf16[128,1024]{1,0:T(8,128)(2,1)}, bf16[128,1024]{1,0:T(8,128)(2,1)}, bf1...) custom-call(bf16[128,12288]{1,0:T(8,128)(2,1)} %bitcast.6, ...), custom_call_target="tpu_custom_call" | custom-call | flops 5242880 | bytes 3145728 | tf_op jit(solution)/shard_map/gate_other/pallas_call | solution.py:119
  15.6 2.4 %collective-permute-start.4 = (bf16[128,512]{1,0:T(8,128)(2,1)}, bf16[128,512]{1,0:T(8,128)(2,1)S(1)}, u32[]{:S(2)}, u32[]{:S(2)}) collective-permute-start(bf16[128,512]{1,0:T(8,128)(2,1)} %get-tuple-element.121), channel_id=1, source_target_pairs={{0,4},{1,5},{2,6},{3,7},{4,0},{5,1},{6,2},{7,3},{8,12},{9,13},{10,... | collective-permute-start | bytes 393224 | tf_op jit(solution)/shard_map/ppermute | solution.py:587
  18.6 2.8 %collective-permute-start.2 = (bf16[128,1024]{1,0:T(8,128)(2,1)}, bf16[128,1024]{1,0:T(8,128)(2,1)S(1)}, u32[]{:S(2)}, u32[]{:S(2)}) collective-permute-start(bf16[128,1024]{1,0:T(8,128)(2,1)} %get-tuple-element.119), channel_id=1, source_target_pairs={{0,2},{1,3},{2,0},{3,1},{4,6},{5,7},{6,4},{7,5},{8,10},{9,11},{10,... | collective-permute-start | bytes 786440 | tf_op jit(solution)/shard_map/ppermute | solution.py:587
  22.8 10.8 %prepare.1 = (bf16[128,1024]{1,0:T(8,128)(2,1)}, bf16[128,1024]{1,0:T(8,128)(2,1)}, bf16[128,1024]{1,0:T(8,128)(2,1)}, bf16[128,1024]{1,0:T(8,128)(2,1)}, f32[1024,512]{1,0:T(8,128)}, /*index=5*/f32[1024,512]{1,0:T(8,128)}) custom-call(f32[1024,512]{1,0:T(8,128)} %refs_0_.3, bf16[1024,512]{1,0:T(8,128)(2,1)} %constant.48.clone.refs_1_.refs_0_, ...), custom_call_target="tpu_custom_call" | custom-call | flops 4294967296 | bytes 10485760 | tf_op jit(solution)/shard_map/prepare/pallas_call | solution.py:176
  33.6 4.7 %collective-permute-done.3.refs_8_ = bf16[128,1024]{1,0:T(8,128)(2,1)S(1)} collective-permute-done((bf16[128,1024]{1,0:T(8,128)(2,1)}, bf16[128,1024]{1,0:T(8,128)(2,1)S(1)}, u32[]{:S(2)}, u32[]{:S(2)}) %collective-permute-start.3) | collective-permute-done | bytes 262176 | tf_op jit(solution)/shard_map/ppermute | solution.py:587
  38.6 3.3 %collective-permute-start.9 = (bf16[128,1024]{1,0:T(8,128)(2,1)}, bf16[128,1024]{1,0:T(8,128)(2,1)S(1)}, u32[]{:S(2)}, u32[]{:S(2)}) collective-permute-start(bf16[128,1024]{1,0:T(8,128)(2,1)} %get-tuple-element.142), channel_id=1, source_target_pairs={{0,3},{1,2},{2,1},{3,0},{4,7},{5,6},{6,5},{7,4},{8,11},{9,10},{10,... | collective-permute-start | bytes 786440 | tf_op jit(solution)/shard_map/ppermute | solution.py:587
  42.5 1.7 %collective-permute-start.11 = (bf16[128,512]{1,0:T(8,128)(2,1)S(1)}, bf16[128,512]{1,0:T(8,128)(2,1)S(1)}, u32[]{:S(2)}, u32[]{:S(2)}) collective-permute-start(bf16[128,512]{1,0:T(8,128)(2,1)S(1)} %copy-done.19), channel_id=1, source_target_pairs={{0,6},{1,7},{2,4},{3,5},{4,2},{5,3},{6,0},{7,1},{8,14},{9,15},{10,... | collective-permute-start | bytes 393224 | tf_op jit(solution)/shard_map/ppermute | solution.py:587
  44.2 6.1 %spectral_other.1 = (bf16[128,1024]{1,0:T(8,128)(2,1)S(1)}, bf16[128,1024]{1,0:T(8,128)(2,1)S(1)}, bf16[128,1024]{1,0:T(8,128)(2,1)S(1)}, bf16[128,1024]{1,0:T(8...) custom-call(bf16[1024,512]{1,0:T(8,128)(2,1)S(1)} %copy-done.8, bf16[512,1024]{1,0:T(8,128)(2,1)S(1)} %copy-done.9, ...), custom_call_target="tpu_custom_call" | custom-call | flops 2684354560 | bytes 9961472 | tf_op jit(solution)/shard_map/spectral_other/pallas_call | solution.py:369
  50.3 3.5 %collective-permute-done.10.refs_9_ = bf16[128,512]{1,0:T(8,128)(2,1)S(1)} collective-permute-done((bf16[128,512]{1,0:T(8,128)(2,1)S(1)}, bf16[128,512]{1,0:T(8,128)(2,1)S(1)}, u32[]{:S(2)}, u32[]{:S(2)}) %collective-permute-start.10) | collective-permute-done | bytes 131104 | tf_op jit(solution)/shard_map/ppermute | solution.py:587
  53.8 5.3 %collective-permute-done.11.refs_10_ = bf16[128,512]{1,0:T(8,128)(2,1)S(1)} collective-permute-done((bf16[128,512]{1,0:T(8,128)(2,1)S(1)}, bf16[128,512]{1,0:T(8,128)(2,1)S(1)}, u32[]{:S(2)}, u32[]{:S(2)}) %collective-permute-start.11) | collective-permute-done | bytes 131104 | tf_op jit(solution)/shard_map/ppermute | solution.py:587
  59.3 2.7 %collective-permute-start.12 = (bf16[128,512]{1,0:T(8,128)(2,1)S(1)}, bf16[128,512]{1,0:T(8,128)(2,1)S(1)}, u32[]{:S(2)}, u32[]{:S(2)}) collective-permute-start(bf16[128,512]{1,0:T(8,128)(2,1)S(1)} %copy-done.17), channel_id=1, source_target_pairs={{0,7},{1,6},{2,5},{3,4},{4,3},{5,2},{6,1},{7,0},{8,15},{9,14},{10,... | collective-permute-start | bytes 393224 | tf_op jit(solution)/shard_map/ppermute | solution.py:587
  62.4 3.1 %collective-permute-start.15 = (bf16[128,1024]{1,0:T(8,128)(2,1)S(1)}, bf16[128,1024]{1,0:T(8,128)(2,1)S(1)}, u32[]{:S(2)}, u32[]{:S(2)}) collective-permute-start(bf16[128,1024]{1,0:T(8,128)(2,1)S(1)} %get-tuple-element.166), channel_id=1, source_target_pairs={{0,3},{1,2},{2,1},{3,0},{4,7},{5,6},{6,5},{7,4},{8,11},{9,10},{10,... | collective-permute-start | bytes 786440 | tf_op jit(solution)/shard_map/ppermute | solution.py:587
  65.9 2.5 %collective-permute-done.12.refs_11_ = bf16[128,512]{1,0:T(8,128)(2,1)S(1)} collective-permute-done((bf16[128,512]{1,0:T(8,128)(2,1)S(1)}, bf16[128,512]{1,0:T(8,128)(2,1)S(1)}, u32[]{:S(2)}, u32[]{:S(2)}) %collective-permute-start.12) | collective-permute-done | bytes 131104 | tf_op jit(solution)/shard_map/ppermute | solution.py:587
  69.1 9.9 %spectral_home.1 = (bf16[512,1024]{1,0:T(8,128)(2,1)}, bf16[128,512]{1,0:T(8,128)(2,1)}, bf16[128,512]{1,0:T(8,128)(2,1)}, bf16[128,512]{1,0:T(8,128)(2,1)}, bf1...) custom-call(bf16[1024,512]{1,0:T(8,128)(2,1)} %constant.48.clone.refs_1_.refs_0_, ...), custom_call_target="tpu_custom_call" | custom-call | flops 4294967296 | bytes 9961472 | tf_op jit(solution)/shard_map/spectral_home/pallas_call | solution.py:369
  79.0 5.8 %collective-permute-done.15.refs_7_ = bf16[128,1024]{1,0:T(8,128)(2,1)S(1)} collective-permute-done((bf16[128,1024]{1,0:T(8,128)(2,1)S(1)}, bf16[128,1024]{1,0:T(8,128)(2,1)S(1)}, u32[]{:S(2)}, u32[]{:S(2)}) %collective-permute-start.15) | collective-permute-done | bytes 262176 | tf_op jit(solution)/shard_map/ppermute | solution.py:587
  84.8 3.5 %all-to-all-start = ((bf16[4,128,1024]{2,1,0:T(8,128)(2,1)}), bf16[4,128,1024]{2,1,0:T(8,128)(2,1)S(1)}, u32[]{:S(2)}, u32[]{:S(2)}) async-start(bf16[4,128,1024]{2,1,0:T(8,128)(2,1)} %bitcast.17), calls=%async_computation | async-start | bytes 2097152 | tf_op jit(solution)/shard_map/all_to_all | solution.py:595
  89.3 3.4 %collective-permute-start.19 = (bf16[128,512]{1,0:T(8,128)(2,1)}, bf16[128,512]{1,0:T(8,128)(2,1)S(1)}, u32[]{:S(2)}, u32[]{:S(2)}) collective-permute-start(bf16[128,512]{1,0:T(8,128)(2,1)} %get-tuple-element.174), channel_id=1, source_target_pairs={{0,5},{1,4},{2,7},{3,6},{4,1},{5,0},{6,3},{7,2},{8,13},{9,12},{10,... | collective-permute-start | bytes 393224 | tf_op jit(solution)/shard_map/ppermute | solution.py:587
  92.6 1.9 %collective-permute-start.20 = (bf16[128,512]{1,0:T(8,128)(2,1)}, bf16[128,512]{1,0:T(8,128)(2,1)S(1)}, u32[]{:S(2)}, u32[]{:S(2)}) collective-permute-start(bf16[128,512]{1,0:T(8,128)(2,1)} %get-tuple-element.175), channel_id=1, source_target_pairs={{0,6},{1,7},{2,4},{3,5},{4,2},{5,3},{6,0},{7,1},{8,14},{9,15},{10,... | collective-permute-start | bytes 393224 | tf_op jit(solution)/shard_map/ppermute | solution.py:587
  96.1 12.9 %all-to-all-done.refs_4_ = bf16[4,128,1024]{2,1,0:T(8,128)(2,1)S(1)} async-done(((bf16[4,128,1024]{2,1,0:T(8,128)(2,1)}), bf16[4,128,1024]{2,1,0:T(8,128)(2,1)S(1)}, u32[]{:S(2)}, u32[]{:S(2)}) %all-to-all-start) | async-done | bytes 1048608 | tf_op jit(solution)/shard_map/all_to_all | solution.py:595
  110.0 5.9 %final_home.1 = (bf16[128,12288]{1,0:T(8,128)(2,1)}, bf16[4,3,2,512]{3,2,1,0:T(2,128)(2,1)}, f32[4,3,16,512]{3,2,1,0:T(8,128)}) custom-call(bf16[128,12288]{1,0:T(8,128)(2,1)} %bitcast.8, bf16[2,12288]{1,0:T(2,128)(2,1)} %copy-done.3, bf16[128,4096]{1,0:T(8,128)(2,1)} %bitcast.13, f32[3,12288]{1,0:T(4,128)} %taps_ref.3, bf16[4,128,1024]{2,1,0:T(8,128)(2,1)} %copy-done.11), custom_call_target="tpu_custom_call" | custom-call | flops 7864320 | bytes 4194304 | tf_op jit(solution)/shard_map/final_home/pallas_call | solution.py:518
  122.0 3.9 %final_other.1 = (bf16[128,12288]{1,0:T(8,128)(2,1)}, bf16[4,3,2,512]{3,2,1,0:T(2,128)(2,1)}, f32[4,3,16,512]{3,2,1,0:T(8,128)S(1)}) custom-call(bf16[128,12288]{1,0:T(8,128)(2,1)S(1)} %bitcast.10, bf16[2,12288]{1,0:T(2,128)(2,1)S(1)} %copy-done.4, bf16[128,4096]{1,0:T(8,128)(2,1)S(1)} %bitcast.15, ...), custom_call_target="tpu_custom_call", output_to_operand_aliasing={{0}: (12, {})} | custom-call | flops 7864320 | bytes 4194304 | tf_op jit(solution)/shard_map/final_other/pallas_call | solution.py:518
  126.7 1.7 %fix.1 = (bf16[128,12288]{1,0:T(8,128)(2,1)}, f32[256,512]{1,0:T(8,128)}) custom-call(f32[3,12288]{1,0:T(4,128)S(1)} %copy-done.2, bf16[2,4,3,2,512]{4,3,2,1,0:T(2,128)(2,1)S(1)} %collective-permute-done.23.edge_ref, f32[4,3,16,512]{3,2,1,0:T(8,128)S(1)} %copy-done.5, ...), custom_call_target="tpu_custom_call", output_to_operand_aliasing={{0}: (6, {})} | custom-call | flops 1572864 | bytes 1572864 | tf_op jit(solution)/shard_map/fix/pallas_call | solution.py:568
  (87 shorter events, 17.5 us)
Async XLA Ops:
  1.6 8.6 %collective-permute-start = (bf16[2,12288]{1,0:T(2,128)(2,1)S(1)}, bf16[2,12288]{1,0:T(2,128)(2,1)S(1)}, u32[]{:S(2)}, u32[]{:S(2)}) collective-permute-start(bf16[2,12288]{1,0:T(2,128)(2,1)S(1)} %slice_bitcast_fusion), channel_id=1, source_target_pairs={{0,1},{1,2},{2,3},{3,4},{4,5},{5,6},{6,7},{8,9},{9,10},{10,11},{11... | collective-permute-start | bytes 147464 | tf_op jit(solution)/shard_map/ppermute | solution.py:676
  7.6 26.0 %collective-permute-start.5 = (bf16[256,512]{1,0:T(8,128)(2,1)S(1)}, bf16[256,512]{1,0:T(8,128)(2,1)S(1)}, u32[]{:S(2)}, u32[]{:S(2)}) collective-permute-start(bf16[256,512]{1,0:T(8,128)(2,1)S(1)} %multiply_convert_fusion), channel_id=1, source_target_pairs={{0,4},{1,5},{2,6},{3,7},{4,0},{5,1},{6,2},{7,3},{8,12},{9,13},{10,... | collective-permute-start | bytes 786440 | tf_op jit(solution)/shard_map/ppermute | solution.py:619
  15.6 18.0 %collective-permute-start.4 = (bf16[128,512]{1,0:T(8,128)(2,1)}, bf16[128,512]{1,0:T(8,128)(2,1)S(1)}, u32[]{:S(2)}, u32[]{:S(2)}) collective-permute-start(bf16[128,512]{1,0:T(8,128)(2,1)} %get-tuple-element.121), channel_id=1, source_target_pairs={{0,4},{1,5},{2,6},{3,7},{4,0},{5,1},{6,2},{7,3},{8,12},{9,13},{10,... | collective-permute-start | bytes 393224 | tf_op jit(solution)/shard_map/ppermute | solution.py:587
  18.0 15.6 %collective-permute-start.1 = (bf16[128,1024]{1,0:T(8,128)(2,1)}, bf16[128,1024]{1,0:T(8,128)(2,1)S(1)}, u32[]{:S(2)}, u32[]{:S(2)}) collective-permute-start(bf16[128,1024]{1,0:T(8,128)(2,1)} %get-tuple-element.118), channel_id=1, source_target_pairs={{0,1},{1,0},{2,3},{3,2},{4,5},{5,4},{6,7},{7,6},{8,9},{9,8},{10,11... | collective-permute-start | bytes 786440 | tf_op jit(solution)/shard_map/ppermute | solution.py:587
  18.6 15.0 %collective-permute-start.2 = (bf16[128,1024]{1,0:T(8,128)(2,1)}, bf16[128,1024]{1,0:T(8,128)(2,1)S(1)}, u32[]{:S(2)}, u32[]{:S(2)}) collective-permute-start(bf16[128,1024]{1,0:T(8,128)(2,1)} %get-tuple-element.119), channel_id=1, source_target_pairs={{0,2},{1,3},{2,0},{3,1},{4,6},{5,7},{6,4},{7,5},{8,10},{9,11},{10,... | collective-permute-start | bytes 786440 | tf_op jit(solution)/shard_map/ppermute | solution.py:587
  21.3 17.0 %collective-permute-start.3 = (bf16[128,1024]{1,0:T(8,128)(2,1)}, bf16[128,1024]{1,0:T(8,128)(2,1)S(1)}, u32[]{:S(2)}, u32[]{:S(2)}) collective-permute-start(bf16[128,1024]{1,0:T(8,128)(2,1)} %get-tuple-element.120), channel_id=1, source_target_pairs={{0,3},{1,2},{2,1},{3,0},{4,7},{5,6},{6,5},{7,4},{8,11},{9,10},{10,... | collective-permute-start | bytes 786440 | tf_op jit(solution)/shard_map/ppermute | solution.py:587
  38.4 20.8 %collective-permute-start.7 = (bf16[128,1024]{1,0:T(8,128)(2,1)}, bf16[128,1024]{1,0:T(8,128)(2,1)S(1)}, u32[]{:S(2)}, u32[]{:S(2)}) collective-permute-start(bf16[128,1024]{1,0:T(8,128)(2,1)} %get-tuple-element.140), channel_id=1, source_target_pairs={{0,1},{1,0},{2,3},{3,2},{4,5},{5,4},{6,7},{7,6},{8,9},{9,8},{10,11... | collective-permute-start | bytes 786440 | tf_op jit(solution)/shard_map/ppermute | solution.py:587
  38.4 20.8 %collective-permute-start.8 = (bf16[128,1024]{1,0:T(8,128)(2,1)}, bf16[128,1024]{1,0:T(8,128)(2,1)S(1)}, u32[]{:S(2)}, u32[]{:S(2)}) collective-permute-start(bf16[128,1024]{1,0:T(8,128)(2,1)} %get-tuple-element.141), channel_id=1, source_target_pairs={{0,2},{1,3},{2,0},{3,1},{4,6},{5,7},{6,4},{7,5},{8,10},{9,11},{10,... | collective-permute-start | bytes 786440 | tf_op jit(solution)/shard_map/ppermute | solution.py:587
  38.6 20.6 %collective-permute-start.9 = (bf16[128,1024]{1,0:T(8,128)(2,1)}, bf16[128,1024]{1,0:T(8,128)(2,1)S(1)}, u32[]{:S(2)}, u32[]{:S(2)}) collective-permute-start(bf16[128,1024]{1,0:T(8,128)(2,1)} %get-tuple-element.142), channel_id=1, source_target_pairs={{0,3},{1,2},{2,1},{3,0},{4,7},{5,6},{6,5},{7,4},{8,11},{9,10},{10,... | collective-permute-start | bytes 786440 | tf_op jit(solution)/shard_map/ppermute | solution.py:587
  41.9 12.0 %collective-permute-start.10 = (bf16[128,512]{1,0:T(8,128)(2,1)S(1)}, bf16[128,512]{1,0:T(8,128)(2,1)S(1)}, u32[]{:S(2)}, u32[]{:S(2)}) collective-permute-start(bf16[128,512]{1,0:T(8,128)(2,1)S(1)} %copy-done.20), channel_id=1, source_target_pairs={{0,5},{1,4},{2,7},{3,6},{4,1},{5,0},{6,3},{7,2},{8,13},{9,12},{10,... | collective-permute-start | bytes 393224 | tf_op jit(solution)/shard_map/ppermute | solution.py:587
  42.5 16.7 %collective-permute-start.11 = (bf16[128,512]{1,0:T(8,128)(2,1)S(1)}, bf16[128,512]{1,0:T(8,128)(2,1)S(1)}, u32[]{:S(2)}, u32[]{:S(2)}) collective-permute-start(bf16[128,512]{1,0:T(8,128)(2,1)S(1)} %copy-done.19), channel_id=1, source_target_pairs={{0,6},{1,7},{2,4},{3,5},{4,2},{5,3},{6,0},{7,1},{8,14},{9,15},{10,... | collective-permute-start | bytes 393224 | tf_op jit(solution)/shard_map/ppermute | solution.py:587
  59.2 6.3 %collective-permute-start.16 = (f32[256,512]{1,0:T(8,128)S(1)}, f32[256,512]{1,0:T(8,128)S(1)}, u32[]{:S(2)}, u32[]{:S(2)}) collective-permute-start(f32[256,512]{1,0:T(8,128)S(1)} %get-tuple-element.168), channel_id=1, source_target_pairs={{0,8},{8,0},{16,24},{24,16},{1,9},{9,1},{17,25},{25,17},{2,10},{10... | collective-permute-start | bytes 1572872 | tf_op jit(solution)/shard_map/ppermute | solution.py:638
  59.3 9.1 %collective-permute-start.12 = (bf16[128,512]{1,0:T(8,128)(2,1)S(1)}, bf16[128,512]{1,0:T(8,128)(2,1)S(1)}, u32[]{:S(2)}, u32[]{:S(2)}) collective-permute-start(bf16[128,512]{1,0:T(8,128)(2,1)S(1)} %copy-done.17), channel_id=1, source_target_pairs={{0,7},{1,6},{2,5},{3,4},{4,3},{5,2},{6,1},{7,0},{8,15},{9,14},{10,... | collective-permute-start | bytes 393224 | tf_op jit(solution)/shard_map/ppermute | solution.py:587
  62.0 16.9 %collective-permute-start.13 = (bf16[128,1024]{1,0:T(8,128)(2,1)S(1)}, bf16[128,1024]{1,0:T(8,128)(2,1)S(1)}, u32[]{:S(2)}, u32[]{:S(2)}) collective-permute-start(bf16[128,1024]{1,0:T(8,128)(2,1)S(1)} %get-tuple-element.164), channel_id=1, source_target_pairs={{0,1},{1,0},{2,3},{3,2},{4,5},{5,4},{6,7},{7,6},{8,9},{9,8},{10,11... | collective-permute-start | bytes 786440 | tf_op jit(solution)/shard_map/ppermute | solution.py:587
  62.4 16.6 %collective-permute-start.14 = (bf16[128,1024]{1,0:T(8,128)(2,1)S(1)}, bf16[128,1024]{1,0:T(8,128)(2,1)S(1)}, u32[]{:S(2)}, u32[]{:S(2)}) collective-permute-start(bf16[128,1024]{1,0:T(8,128)(2,1)S(1)} %get-tuple-element.165), channel_id=1, source_target_pairs={{0,2},{1,3},{2,0},{3,1},{4,6},{5,7},{6,4},{7,5},{8,10},{9,11},{10,... | collective-permute-start | bytes 786440 | tf_op jit(solution)/shard_map/ppermute | solution.py:587
  62.4 22.4 %collective-permute-start.15 = (bf16[128,1024]{1,0:T(8,128)(2,1)S(1)}, bf16[128,1024]{1,0:T(8,128)(2,1)S(1)}, u32[]{:S(2)}, u32[]{:S(2)}) collective-permute-start(bf16[128,1024]{1,0:T(8,128)(2,1)S(1)} %get-tuple-element.166), channel_id=1, source_target_pairs={{0,3},{1,2},{2,1},{3,0},{4,7},{5,6},{6,5},{7,4},{8,11},{9,10},{10,... | collective-permute-start | bytes 786440 | tf_op jit(solution)/shard_map/ppermute | solution.py:587
  65.6 19.2 %collective-permute-start.17 = (bf16[256,512]{1,0:T(8,128)(2,1)S(1)}, bf16[256,512]{1,0:T(8,128)(2,1)S(1)}, u32[]{:S(2)}, u32[]{:S(2)}) collective-permute-start(bf16[256,512]{1,0:T(8,128)(2,1)S(1)} %add_convert_fusion), channel_id=1, source_target_pairs={{0,4},{1,5},{2,6},{3,7},{4,0},{5,1},{6,2},{7,3},{8,12},{9,13},{10,... | collective-permute-start | bytes 786440 | tf_op jit(solution)/shard_map/ppermute | solution.py:639
  84.8 24.3 %all-to-all-start = ((bf16[4,128,1024]{2,1,0:T(8,128)(2,1)}), bf16[4,128,1024]{2,1,0:T(8,128)(2,1)S(1)}, u32[]{:S(2)}, u32[]{:S(2)}) async-start(bf16[4,128,1024]{2,1,0:T(8,128)(2,1)} %bitcast.17), calls=%async_computation | async-start | bytes 2097152 | tf_op jit(solution)/shard_map/all_to_all | solution.py:595
  88.3 27.7 %collective-permute-start.22 = (f32[512,512]{1,0:T(8,128)}, f32[512,512]{1,0:T(8,128)}, u32[]{:S(2)}, u32[]{:S(2)}) collective-permute-start(f32[512,512]{1,0:T(8,128)} %get-tuple-element.178), channel_id=1, source_target_pairs={{0,8},{8,0},{16,24},{24,16},{1,9},{9,1},{17,25},{25,17},{2,10},{10... | collective-permute-start | bytes 3145736 | tf_op jit(solution)/shard_map/ppermute | solution.py:646
  88.4 29.3 %collective-permute-start.18 = (bf16[128,512]{1,0:T(8,128)(2,1)}, bf16[128,512]{1,0:T(8,128)(2,1)S(1)}, u32[]{:S(2)}, u32[]{:S(2)}) collective-permute-start(bf16[128,512]{1,0:T(8,128)(2,1)} %get-tuple-element.173), channel_id=1, source_target_pairs={{0,4},{1,5},{2,6},{3,7},{4,0},{5,1},{6,2},{7,3},{8,12},{9,13},{10,... | collective-permute-start | bytes 393224 | tf_op jit(solution)/shard_map/ppermute | solution.py:587
  89.3 28.4 %collective-permute-start.19 = (bf16[128,512]{1,0:T(8,128)(2,1)}, bf16[128,512]{1,0:T(8,128)(2,1)S(1)}, u32[]{:S(2)}, u32[]{:S(2)}) collective-permute-start(bf16[128,512]{1,0:T(8,128)(2,1)} %get-tuple-element.174), channel_id=1, source_target_pairs={{0,5},{1,4},{2,7},{3,6},{4,1},{5,0},{6,3},{7,2},{8,13},{9,12},{10,... | collective-permute-start | bytes 393224 | tf_op jit(solution)/shard_map/ppermute | solution.py:587
  92.6 25.0 %collective-permute-start.20 = (bf16[128,512]{1,0:T(8,128)(2,1)}, bf16[128,512]{1,0:T(8,128)(2,1)S(1)}, u32[]{:S(2)}, u32[]{:S(2)}) collective-permute-start(bf16[128,512]{1,0:T(8,128)(2,1)} %get-tuple-element.175), channel_id=1, source_target_pairs={{0,6},{1,7},{2,4},{3,5},{4,2},{5,3},{6,0},{7,1},{8,14},{9,15},{10,... | collective-permute-start | bytes 393224 | tf_op jit(solution)/shard_map/ppermute | solution.py:587
  94.5 23.2 %collective-permute-start.21 = (bf16[128,512]{1,0:T(8,128)(2,1)}, bf16[128,512]{1,0:T(8,128)(2,1)S(1)}, u32[]{:S(2)}, u32[]{:S(2)}) collective-permute-start(bf16[128,512]{1,0:T(8,128)(2,1)} %get-tuple-element.176), channel_id=1, source_target_pairs={{0,7},{1,6},{2,5},{3,4},{4,3},{5,2},{6,1},{7,0},{8,15},{9,14},{10,... | collective-permute-start | bytes 393224 | tf_op jit(solution)/shard_map/ppermute | solution.py:587
  119.2 7.5 %collective-permute-start.24 = (bf16[256,512]{1,0:T(8,128)(2,1)S(1)}, bf16[256,512]{1,0:T(8,128)(2,1)S(1)}, u32[]{:S(2)}, u32[]{:S(2)}) collective-permute-start(bf16[256,512]{1,0:T(8,128)(2,1)S(1)} %dynamic-slice_convert_fusion), channel_id=1, source_target_pairs={{0,16},{8,24},{16,0},{24,8},{1,17},{9,25},{17,1},{25,9},{2,18},{10... | collective-permute-start | bytes 786440 | tf_op jit(solution)/shard_map/ppermute | solution.py:661
  (25 other events, 296.3 us)

commit v5 on v4

--- a/solution.py
+++ b/solution.py
@@ -636,6 +636,10 @@
     sent = list(sent) + exchange(across[3:], hc + 3)
     send, keep = outs[hc:]
     summed = keep + lax.ppermute(send, "dp", cores)
+    eighth = quarter // 2
+    other = lax.dynamic_slice_in_dim(summed, (1 - x) * eighth, eighth, 0).astype(jnp.bfloat16)
+    other = lax.ppermute(other, "dp", [(i, i ^ 2) for i in range(4)]).astype(jnp.float32)
+    summed = lax.dynamic_slice_in_dim(summed, x * eighth, eighth, 0) + other
     crossed = lax.ppermute(summed.astype(jnp.bfloat16), "ctx", [(i, i ^ hc) for i in range(count)])
     outs = spectral(high, inverse, (near, far), home_pieces, sent, scale)
     outs, other_back, crossed = tie((outs, other_back, crossed))
@@ -648,7 +652,9 @@
         feats, before, grad_out, short_weight, [home_back], (), None, count, 0
     )
     keep, came, crossed, edge_home = tie((keep, came, crossed, edge_home))
-    crossed = jnp.concatenate([crossed.astype(jnp.float32), jnp.zeros((quarter, block), jnp.float32)], axis=0)
+    crossed = crossed.astype(jnp.float32)
+    spots = [jnp.where(x == i, crossed, 0.0) for i in range(2)]
+    crossed = jnp.concatenate([*spots, jnp.zeros((quarter, block), jnp.float32)], axis=0)
     home_sum = keep + came + crossed
     there = lax.dynamic_slice_in_dim(home_sum, (1 - x) * quarter, quarter, 0).astype(jnp.bfloat16)
     cross_back, edge_home, there = tie((cross_back, edge_home, there))

time: 129 us -> 128 us (level)
  waiting for transfers between devices: 35.6 us -> 33.6 us
    ppermute x17, waiting for transfers between devices: 21.9 us -> 18.6 us  [exchange(): lax.ppermute(piece, 'ctx', [(i, i ^ base + j) for i in devices])]
    ppermute x1, waiting for transfers between devices: 0.01 us -> 1.91 us  [half_shards(): summed = keep + lax.ppermute(send, 'dp', cores)]
    ppermute x0 -> x1, starting transfers between devices: none -> 1.56 us  [half_shards(): lax.ppermute(other, 'dp', [(i, i ^ 2) for i in range(4)])]
  transfers between devices with their start and end apart: 26 -> 27, of which waited for: 7 -> 8; matrix products, arithmetic and copies ran while one was open for 2% -> 2% of each run, Pallas kernels for 32% -> 32%
where the time goes in v5:
time: 128 us
  Pallas kernels  43.7 us (34%)
  starting transfers between devices  41.7 us (33%)
  waiting for transfers between devices  33.6 us (26%)
  local copies, waits for them, and re-layouts  4.88 us (4%)
  other arithmetic  2.79 us (2%)
    ppermute x17, starting transfers between devices, exchange(): lax.ppermute(piece, 'ctx', [(i, i ^ base + j) for i in devices])  26.8 us
    ppermute x17, waiting for transfers between devices, exchange(): lax.ppermute(piece, 'ctx', [(i, i ^ base + j) for i in devices])  18.6 us
    pallas_call x2, Pallas kernels, spectral(): pl.pallas_call(functools.partial(spectral_kernel, hc, rows, home, scale),...  15.9 us
    all_to_all x1, waiting for transfers between devices, within(): lax.all_to_all(stacked, 'ctx', 0, 0, axis_index_groups=groups, tiled=True)  12.3 us
    pallas_call x1, Pallas kernels, prepare(): pl.pallas_call(functools.partial(prepare_kernel, hc, count, scale), in_sp...  10.8 us
    pallas_call x3, Pallas kernels, final(): pl.pallas_call(functools.partial(final_kernel, hc, count, base, top, so_f...  10.7 us
    ppermute x2, starting transfers between devices, from_behind(): return lax.ppermute(block, axis, route)  6.15 us
    pallas_call x1, Pallas kernels, gate(): pl.pallas_call(functools.partial(gate_kernel, hc, count, base), in_specs=...  4.67 us
  transfers between devices with their start and end apart: 27, of which 8 were waited for; matrix products, arithmetic and copies ran while one was open for 2% of the time, Pallas kernels for 32%

profile of v5, /device:TPU:0, one launch (start us, length us, event | category | flops | bytes accessed | tf_op | source)
XLA Modules:
  0.0 128.0 jit_solution(16012417524435644936)
XLA Ops:
  1.6 4.9 %collective-permute-start = (bf16[2,12288]{1,0:T(2,128)(2,1)S(1)}, bf16[2,12288]{1,0:T(2,128)(2,1)S(1)}, u32[]{:S(2)}, u32[]{:S(2)}) collective-permute-start(bf16[2,12288]{1,0:T(2,128)(2,1)S(1)} %slice_bitcast_fusion), channel_id=1, source_target_pairs={{0,1},{1,2},{2,3},{3,4},{4,5},{5,6},{6,7},{8,9},{9,10},{10,11},{11... | collective-permute-start | bytes 147464 | tf_op jit(solution)/shard_map/ppermute | solution.py:682
  7.6 2.7 %collective-permute-start.5 = (bf16[256,512]{1,0:T(8,128)(2,1)S(1)}, bf16[256,512]{1,0:T(8,128)(2,1)S(1)}, u32[]{:S(2)}, u32[]{:S(2)}) collective-permute-start(bf16[256,512]{1,0:T(8,128)(2,1)S(1)} %multiply_convert_fusion), channel_id=1, source_target_pairs={{0,4},{1,5},{2,6},{3,7},{4,0},{5,1},{6,2},{7,3},{8,12},{9,13},{10,... | collective-permute-start | bytes 786440 | tf_op jit(solution)/shard_map/ppermute | solution.py:619
  10.9 4.7 %gate_other.1 = (bf16[128,1024]{1,0:T(8,128)(2,1)}, bf16[128,1024]{1,0:T(8,128)(2,1)}, bf16[128,1024]{1,0:T(8,128)(2,1)}, bf16[128,1024]{1,0:T(8,128)(2,1)}, bf1...) custom-call(bf16[128,12288]{1,0:T(8,128)(2,1)} %bitcast.6, ...), custom_call_target="tpu_custom_call" | custom-call | flops 5242880 | bytes 3145728 | tf_op jit(solution)/shard_map/gate_other/pallas_call | solution.py:119
  15.6 2.4 %collective-permute-start.4 = (bf16[128,512]{1,0:T(8,128)(2,1)}, bf16[128,512]{1,0:T(8,128)(2,1)S(1)}, u32[]{:S(2)}, u32[]{:S(2)}) collective-permute-start(bf16[128,512]{1,0:T(8,128)(2,1)} %get-tuple-element.121), channel_id=1, source_target_pairs={{0,4},{1,5},{2,6},{3,7},{4,0},{5,1},{6,2},{7,3},{8,12},{9,13},{10,... | collective-permute-start | bytes 393224 | tf_op jit(solution)/shard_map/ppermute | solution.py:587
  18.6 2.8 %collective-permute-start.2 = (bf16[128,1024]{1,0:T(8,128)(2,1)}, bf16[128,1024]{1,0:T(8,128)(2,1)S(1)}, u32[]{:S(2)}, u32[]{:S(2)}) collective-permute-start(bf16[128,1024]{1,0:T(8,128)(2,1)} %get-tuple-element.119), channel_id=1, source_target_pairs={{0,2},{1,3},{2,0},{3,1},{4,6},{5,7},{6,4},{7,5},{8,10},{9,11},{10,... | collective-permute-start | bytes 786440 | tf_op jit(solution)/shard_map/ppermute | solution.py:587
  22.8 10.8 %prepare.1 = (bf16[128,1024]{1,0:T(8,128)(2,1)}, bf16[128,1024]{1,0:T(8,128)(2,1)}, bf16[128,1024]{1,0:T(8,128)(2,1)}, bf16[128,1024]{1,0:T(8,128)(2,1)}, f32[1024,512]{1,0:T(8,128)}, /*index=5*/f32[1024,512]{1,0:T(8,128)}) custom-call(f32[1024,512]{1,0:T(8,128)} %refs_0_.3, bf16[1024,512]{1,0:T(8,128)(2,1)} %constant.50.clone.refs_1_.refs_0_, ...), custom_call_target="tpu_custom_call" | custom-call | flops 4294967296 | bytes 10485760 | tf_op jit(solution)/shard_map/prepare/pallas_call | solution.py:176
  33.6 4.7 %collective-permute-done.3.refs_8_ = bf16[128,1024]{1,0:T(8,128)(2,1)S(1)} collective-permute-done((bf16[128,1024]{1,0:T(8,128)(2,1)}, bf16[128,1024]{1,0:T(8,128)(2,1)S(1)}, u32[]{:S(2)}, u32[]{:S(2)}) %collective-permute-start.3) | collective-permute-done | bytes 262176 | tf_op jit(solution)/shard_map/ppermute | solution.py:587
  38.6 3.3 %collective-permute-start.9 = (bf16[128,1024]{1,0:T(8,128)(2,1)}, bf16[128,1024]{1,0:T(8,128)(2,1)S(1)}, u32[]{:S(2)}, u32[]{:S(2)}) collective-permute-start(bf16[128,1024]{1,0:T(8,128)(2,1)} %get-tuple-element.142), channel_id=1, source_target_pairs={{0,3},{1,2},{2,1},{3,0},{4,7},{5,6},{6,5},{7,4},{8,11},{9,10},{10,... | collective-permute-start | bytes 786440 | tf_op jit(solution)/shard_map/ppermute | solution.py:587
  42.5 1.7 %collective-permute-start.11 = (bf16[128,512]{1,0:T(8,128)(2,1)S(1)}, bf16[128,512]{1,0:T(8,128)(2,1)S(1)}, u32[]{:S(2)}, u32[]{:S(2)}) collective-permute-start(bf16[128,512]{1,0:T(8,128)(2,1)S(1)} %copy-done.20), channel_id=1, source_target_pairs={{0,6},{1,7},{2,4},{3,5},{4,2},{5,3},{6,0},{7,1},{8,14},{9,15},{10,... | collective-permute-start | bytes 393224 | tf_op jit(solution)/shard_map/ppermute | solution.py:587
  44.2 6.1 %spectral_other.1 = (bf16[128,1024]{1,0:T(8,128)(2,1)S(1)}, bf16[128,1024]{1,0:T(8,128)(2,1)S(1)}, bf16[128,1024]{1,0:T(8,128)(2,1)S(1)}, bf16[128,1024]{1,0:T(8...) custom-call(bf16[1024,512]{1,0:T(8,128)(2,1)S(1)} %copy-done.8, bf16[512,1024]{1,0:T(8,128)(2,1)S(1)} %copy-done.9, ...), custom_call_target="tpu_custom_call" | custom-call | flops 2684354560 | bytes 9961472 | tf_op jit(solution)/shard_map/spectral_other/pallas_call | solution.py:369
  50.3 3.5 %collective-permute-done.10.refs_9_ = bf16[128,512]{1,0:T(8,128)(2,1)S(1)} collective-permute-done((bf16[128,512]{1,0:T(8,128)(2,1)S(1)}, bf16[128,512]{1,0:T(8,128)(2,1)S(1)}, u32[]{:S(2)}, u32[]{:S(2)}) %collective-permute-start.10) | collective-permute-done | bytes 131104 | tf_op jit(solution)/shard_map/ppermute | solution.py:587
  53.8 5.3 %collective-permute-done.11.refs_10_ = bf16[128,512]{1,0:T(8,128)(2,1)S(1)} collective-permute-done((bf16[128,512]{1,0:T(8,128)(2,1)S(1)}, bf16[128,512]{1,0:T(8,128)(2,1)S(1)}, u32[]{:S(2)}, u32[]{:S(2)}) %collective-permute-start.11) | collective-permute-done | bytes 131104 | tf_op jit(solution)/shard_map/ppermute | solution.py:587
  60.0 1.9 %collective-permute-done.16 = f32[256,512]{1,0:T(8,128)S(1)} collective-permute-done((f32[256,512]{1,0:T(8,128)S(1)}, f32[256,512]{1,0:T(8,128)S(1)}, u32[]{:S(2)}, u32[]{:S(2)}) %collective-permute-start.16) | collective-permute-done | bytes 524320 | tf_op jit(solution)/shard_map/ppermute | solution.py:638
  63.6 2.6 %collective-permute-start.12 = (bf16[128,512]{1,0:T(8,128)(2,1)S(1)}, bf16[128,512]{1,0:T(8,128)(2,1)S(1)}, u32[]{:S(2)}, u32[]{:S(2)}) collective-permute-start(bf16[128,512]{1,0:T(8,128)(2,1)S(1)} %copy-done.17), channel_id=1, source_target_pairs={{0,7},{1,6},{2,5},{3,4},{4,3},{5,2},{6,1},{7,0},{8,15},{9,14},{10,... | collective-permute-start | bytes 393224 | tf_op jit(solution)/shard_map/ppermute | solution.py:587
  66.6 3.1 %collective-permute-start.15 = (bf16[128,1024]{1,0:T(8,128)(2,1)S(1)}, bf16[128,1024]{1,0:T(8,128)(2,1)S(1)}, u32[]{:S(2)}, u32[]{:S(2)}) collective-permute-start(bf16[128,1024]{1,0:T(8,128)(2,1)S(1)} %get-tuple-element.166), channel_id=1, source_target_pairs={{0,3},{1,2},{2,1},{3,0},{4,7},{5,6},{6,5},{7,4},{8,11},{9,10},{10,... | collective-permute-start | bytes 786440 | tf_op jit(solution)/shard_map/ppermute | solution.py:587
  70.1 2.6 %collective-permute-done.12.refs_11_ = bf16[128,512]{1,0:T(8,128)(2,1)S(1)} collective-permute-done((bf16[128,512]{1,0:T(8,128)(2,1)S(1)}, bf16[128,512]{1,0:T(8,128)(2,1)S(1)}, u32[]{:S(2)}, u32[]{:S(2)}) %collective-permute-start.12) | collective-permute-done | bytes 131104 | tf_op jit(solution)/shard_map/ppermute | solution.py:587
  73.4 9.9 %spectral_home.1 = (bf16[512,1024]{1,0:T(8,128)(2,1)}, bf16[128,512]{1,0:T(8,128)(2,1)}, bf16[128,512]{1,0:T(8,128)(2,1)}, bf16[128,512]{1,0:T(8,128)(2,1)}, bf1...) custom-call(bf16[1024,512]{1,0:T(8,128)(2,1)} %constant.50.clone.refs_1_.refs_0_, ...), custom_call_target="tpu_custom_call" | custom-call | flops 4294967296 | bytes 9961472 | tf_op jit(solution)/shard_map/spectral_home/pallas_call | solution.py:369
  83.3 2.3 %collective-permute-done.15.refs_7_ = bf16[128,1024]{1,0:T(8,128)(2,1)S(1)} collective-permute-done((bf16[128,1024]{1,0:T(8,128)(2,1)S(1)}, bf16[128,1024]{1,0:T(8,128)(2,1)S(1)}, u32[]{:S(2)}, u32[]{:S(2)}) %collective-permute-start.15) | collective-permute-done | bytes 262176 | tf_op jit(solution)/shard_map/ppermute | solution.py:587
  85.6 3.5 %all-to-all-start = ((bf16[4,128,1024]{2,1,0:T(8,128)(2,1)}), bf16[4,128,1024]{2,1,0:T(8,128)(2,1)S(1)}, u32[]{:S(2)}, u32[]{:S(2)}) async-start(bf16[4,128,1024]{2,1,0:T(8,128)(2,1)} %bitcast.17), calls=%async_computation | async-start | bytes 2097152 | tf_op jit(solution)/shard_map/all_to_all | solution.py:595
  90.1 3.4 %collective-permute-start.20 = (bf16[128,512]{1,0:T(8,128)(2,1)}, bf16[128,512]{1,0:T(8,128)(2,1)S(1)}, u32[]{:S(2)}, u32[]{:S(2)}) collective-permute-start(bf16[128,512]{1,0:T(8,128)(2,1)} %get-tuple-element.174), channel_id=1, source_target_pairs={{0,5},{1,4},{2,7},{3,6},{4,1},{5,0},{6,3},{7,2},{8,13},{9,12},{10,... | collective-permute-start | bytes 393224 | tf_op jit(solution)/shard_map/ppermute | solution.py:587
  93.5 1.9 %collective-permute-start.21 = (bf16[128,512]{1,0:T(8,128)(2,1)}, bf16[128,512]{1,0:T(8,128)(2,1)S(1)}, u32[]{:S(2)}, u32[]{:S(2)}) collective-permute-start(bf16[128,512]{1,0:T(8,128)(2,1)} %get-tuple-element.175), channel_id=1, source_target_pairs={{0,6},{1,7},{2,4},{3,5},{4,2},{5,3},{6,0},{7,1},{8,14},{9,15},{10,... | collective-permute-start | bytes 393224 | tf_op jit(solution)/shard_map/ppermute | solution.py:587
  96.9 12.3 %all-to-all-done.refs_4_ = bf16[4,128,1024]{2,1,0:T(8,128)(2,1)S(1)} async-done(((bf16[4,128,1024]{2,1,0:T(8,128)(2,1)}), bf16[4,128,1024]{2,1,0:T(8,128)(2,1)S(1)}, u32[]{:S(2)}, u32[]{:S(2)}) %all-to-all-start) | async-done | bytes 1048608 | tf_op jit(solution)/shard_map/all_to_all | solution.py:595
  110.2 5.8 %final_home.1 = (bf16[128,12288]{1,0:T(8,128)(2,1)}, bf16[4,3,2,512]{3,2,1,0:T(2,128)(2,1)}, f32[4,3,16,512]{3,2,1,0:T(8,128)}) custom-call(bf16[128,12288]{1,0:T(8,128)(2,1)} %bitcast.8, bf16[2,12288]{1,0:T(2,128)(2,1)} %copy-done.3, bf16[128,4096]{1,0:T(8,128)(2,1)} %bitcast.13, f32[3,12288]{1,0:T(4,128)} %taps_ref.3, bf16[4,128,1024]{2,1,0:T(8,128)(2,1)} %copy-done.11), custom_call_target="tpu_custom_call" | custom-call | flops 7864320 | bytes 4194304 | tf_op jit(solution)/shard_map/final_home/pallas_call | solution.py:518
  121.4 3.9 %final_other.1 = (bf16[128,12288]{1,0:T(8,128)(2,1)}, bf16[4,3,2,512]{3,2,1,0:T(2,128)(2,1)}, f32[4,3,16,512]{3,2,1,0:T(8,128)S(1)}) custom-call(bf16[128,12288]{1,0:T(8,128)(2,1)S(1)} %bitcast.10, bf16[2,12288]{1,0:T(2,128)(2,1)S(1)} %copy-done.4, bf16[128,4096]{1,0:T(8,128)(2,1)S(1)} %bitcast.15, ...), custom_call_target="tpu_custom_call", output_to_operand_aliasing={{0}: (12, {})} | custom-call | flops 7864320 | bytes 4194304 | tf_op jit(solution)/shard_map/final_other/pallas_call | solution.py:518
  (94 shorter events, 20.7 us)
Async XLA Ops:
  1.6 8.6 %collective-permute-start = (bf16[2,12288]{1,0:T(2,128)(2,1)S(1)}, bf16[2,12288]{1,0:T(2,128)(2,1)S(1)}, u32[]{:S(2)}, u32[]{:S(2)}) collective-permute-start(bf16[2,12288]{1,0:T(2,128)(2,1)S(1)} %slice_bitcast_fusion), channel_id=1, source_target_pairs={{0,1},{1,2},{2,3},{3,4},{4,5},{5,6},{6,7},{8,9},{9,10},{10,11},{11... | collective-permute-start | bytes 147464 | tf_op jit(solution)/shard_map/ppermute | solution.py:682
  7.6 26.0 %collective-permute-start.5 = (bf16[256,512]{1,0:T(8,128)(2,1)S(1)}, bf16[256,512]{1,0:T(8,128)(2,1)S(1)}, u32[]{:S(2)}, u32[]{:S(2)}) collective-permute-start(bf16[256,512]{1,0:T(8,128)(2,1)S(1)} %multiply_convert_fusion), channel_id=1, source_target_pairs={{0,4},{1,5},{2,6},{3,7},{4,0},{5,1},{6,2},{7,3},{8,12},{9,13},{10,... | collective-permute-start | bytes 786440 | tf_op jit(solution)/shard_map/ppermute | solution.py:619
  15.6 17.9 %collective-permute-start.4 = (bf16[128,512]{1,0:T(8,128)(2,1)}, bf16[128,512]{1,0:T(8,128)(2,1)S(1)}, u32[]{:S(2)}, u32[]{:S(2)}) collective-permute-start(bf16[128,512]{1,0:T(8,128)(2,1)} %get-tuple-element.121), channel_id=1, source_target_pairs={{0,4},{1,5},{2,6},{3,7},{4,0},{5,1},{6,2},{7,3},{8,12},{9,13},{10,... | collective-permute-start | bytes 393224 | tf_op jit(solution)/shard_map/ppermute | solution.py:587
  18.0 15.6 %collective-permute-start.1 = (bf16[128,1024]{1,0:T(8,128)(2,1)}, bf16[128,1024]{1,0:T(8,128)(2,1)S(1)}, u32[]{:S(2)}, u32[]{:S(2)}) collective-permute-start(bf16[128,1024]{1,0:T(8,128)(2,1)} %get-tuple-element.118), channel_id=1, source_target_pairs={{0,1},{1,0},{2,3},{3,2},{4,5},{5,4},{6,7},{7,6},{8,9},{9,8},{10,11... | collective-permute-start | bytes 786440 | tf_op jit(solution)/shard_map/ppermute | solution.py:587
  18.6 15.0 %collective-permute-start.2 = (bf16[128,1024]{1,0:T(8,128)(2,1)}, bf16[128,1024]{1,0:T(8,128)(2,1)S(1)}, u32[]{:S(2)}, u32[]{:S(2)}) collective-permute-start(bf16[128,1024]{1,0:T(8,128)(2,1)} %get-tuple-element.119), channel_id=1, source_target_pairs={{0,2},{1,3},{2,0},{3,1},{4,6},{5,7},{6,4},{7,5},{8,10},{9,11},{10,... | collective-permute-start | bytes 786440 | tf_op jit(solution)/shard_map/ppermute | solution.py:587
  21.3 17.0 %collective-permute-start.3 = (bf16[128,1024]{1,0:T(8,128)(2,1)}, bf16[128,1024]{1,0:T(8,128)(2,1)S(1)}, u32[]{:S(2)}, u32[]{:S(2)}) collective-permute-start(bf16[128,1024]{1,0:T(8,128)(2,1)} %get-tuple-element.120), channel_id=1, source_target_pairs={{0,3},{1,2},{2,1},{3,0},{4,7},{5,6},{6,5},{7,4},{8,11},{9,10},{10,... | collective-permute-start | bytes 786440 | tf_op jit(solution)/shard_map/ppermute | solution.py:587
  38.4 20.8 %collective-permute-start.7 = (bf16[128,1024]{1,0:T(8,128)(2,1)}, bf16[128,1024]{1,0:T(8,128)(2,1)S(1)}, u32[]{:S(2)}, u32[]{:S(2)}) collective-permute-start(bf16[128,1024]{1,0:T(8,128)(2,1)} %get-tuple-element.140), channel_id=1, source_target_pairs={{0,1},{1,0},{2,3},{3,2},{4,5},{5,4},{6,7},{7,6},{8,9},{9,8},{10,11... | collective-permute-start | bytes 786440 | tf_op jit(solution)/shard_map/ppermute | solution.py:587
  38.4 20.8 %collective-permute-start.8 = (bf16[128,1024]{1,0:T(8,128)(2,1)}, bf16[128,1024]{1,0:T(8,128)(2,1)S(1)}, u32[]{:S(2)}, u32[]{:S(2)}) collective-permute-start(bf16[128,1024]{1,0:T(8,128)(2,1)} %get-tuple-element.141), channel_id=1, source_target_pairs={{0,2},{1,3},{2,0},{3,1},{4,6},{5,7},{6,4},{7,5},{8,10},{9,11},{10,... | collective-permute-start | bytes 786440 | tf_op jit(solution)/shard_map/ppermute | solution.py:587
  38.6 20.6 %collective-permute-start.9 = (bf16[128,1024]{1,0:T(8,128)(2,1)}, bf16[128,1024]{1,0:T(8,128)(2,1)S(1)}, u32[]{:S(2)}, u32[]{:S(2)}) collective-permute-start(bf16[128,1024]{1,0:T(8,128)(2,1)} %get-tuple-element.142), channel_id=1, source_target_pairs={{0,3},{1,2},{2,1},{3,0},{4,7},{5,6},{6,5},{7,4},{8,11},{9,10},{10,... | collective-permute-start | bytes 786440 | tf_op jit(solution)/shard_map/ppermute | solution.py:587
  41.9 12.0 %collective-permute-start.10 = (bf16[128,512]{1,0:T(8,128)(2,1)S(1)}, bf16[128,512]{1,0:T(8,128)(2,1)S(1)}, u32[]{:S(2)}, u32[]{:S(2)}) collective-permute-start(bf16[128,512]{1,0:T(8,128)(2,1)S(1)} %copy-done.21), channel_id=1, source_target_pairs={{0,5},{1,4},{2,7},{3,6},{4,1},{5,0},{6,3},{7,2},{8,13},{9,12},{10,... | collective-permute-start | bytes 393224 | tf_op jit(solution)/shard_map/ppermute | solution.py:587
  42.5 16.7 %collective-permute-start.11 = (bf16[128,512]{1,0:T(8,128)(2,1)S(1)}, bf16[128,512]{1,0:T(8,128)(2,1)S(1)}, u32[]{:S(2)}, u32[]{:S(2)}) collective-permute-start(bf16[128,512]{1,0:T(8,128)(2,1)S(1)} %copy-done.20), channel_id=1, source_target_pairs={{0,6},{1,7},{2,4},{3,5},{4,2},{5,3},{6,0},{7,1},{8,14},{9,15},{10,... | collective-permute-start | bytes 393224 | tf_op jit(solution)/shard_map/ppermute | solution.py:587
  62.0 7.7 %collective-permute-start.17 = (bf16[128,512]{1,0:T(8,128)(2,1)S(1)}, bf16[128,512]{1,0:T(8,128)(2,1)S(1)}, u32[]{:S(2)}, u32[]{:S(2)}) collective-permute-start(bf16[128,512]{1,0:T(8,128)(2,1)S(1)} %dynamic-slice_convert_fusion.1), channel_id=1, source_target_pairs={{0,16},{8,24},{16,0},{24,8},{1,17},{9,25},{17,1},{25,9},{2,18},{10... | collective-permute-start | bytes 393224 | tf_op jit(solution)/shard_map/ppermute | solution.py:641
  63.6 9.1 %collective-permute-start.12 = (bf16[128,512]{1,0:T(8,128)(2,1)S(1)}, bf16[128,512]{1,0:T(8,128)(2,1)S(1)}, u32[]{:S(2)}, u32[]{:S(2)}) collective-permute-start(bf16[128,512]{1,0:T(8,128)(2,1)S(1)} %copy-done.17), channel_id=1, source_target_pairs={{0,7},{1,6},{2,5},{3,4},{4,3},{5,2},{6,1},{7,0},{8,15},{9,14},{10,... | collective-permute-start | bytes 393224 | tf_op jit(solution)/shard_map/ppermute | solution.py:587
  66.2 17.1 %collective-permute-start.13 = (bf16[128,1024]{1,0:T(8,128)(2,1)S(1)}, bf16[128,1024]{1,0:T(8,128)(2,1)S(1)}, u32[]{:S(2)}, u32[]{:S(2)}) collective-permute-start(bf16[128,1024]{1,0:T(8,128)(2,1)S(1)} %get-tuple-element.164), channel_id=1, source_target_pairs={{0,1},{1,0},{2,3},{3,2},{4,5},{5,4},{6,7},{7,6},{8,9},{9,8},{10,11... | collective-permute-start | bytes 786440 | tf_op jit(solution)/shard_map/ppermute | solution.py:587
  66.6 16.7 %collective-permute-start.14 = (bf16[128,1024]{1,0:T(8,128)(2,1)S(1)}, bf16[128,1024]{1,0:T(8,128)(2,1)S(1)}, u32[]{:S(2)}, u32[]{:S(2)}) collective-permute-start(bf16[128,1024]{1,0:T(8,128)(2,1)S(1)} %get-tuple-element.165), channel_id=1, source_target_pairs={{0,2},{1,3},{2,0},{3,1},{4,6},{5,7},{6,4},{7,5},{8,10},{9,11},{10,... | collective-permute-start | bytes 786440 | tf_op jit(solution)/shard_map/ppermute | solution.py:587
  66.6 19.0 %collective-permute-start.15 = (bf16[128,1024]{1,0:T(8,128)(2,1)S(1)}, bf16[128,1024]{1,0:T(8,128)(2,1)S(1)}, u32[]{:S(2)}, u32[]{:S(2)}) collective-permute-start(bf16[128,1024]{1,0:T(8,128)(2,1)S(1)} %get-tuple-element.166), channel_id=1, source_target_pairs={{0,3},{1,2},{2,1},{3,0},{4,7},{5,6},{6,5},{7,4},{8,11},{9,10},{10,... | collective-permute-start | bytes 786440 | tf_op jit(solution)/shard_map/ppermute | solution.py:587
  69.7 15.9 %collective-permute-start.18 = (bf16[128,512]{1,0:T(8,128)(2,1)S(1)}, bf16[128,512]{1,0:T(8,128)(2,1)S(1)}, u32[]{:S(2)}, u32[]{:S(2)}) collective-permute-start(bf16[128,512]{1,0:T(8,128)(2,1)S(1)} %add_convert_fusion), channel_id=1, source_target_pairs={{0,4},{1,5},{2,6},{3,7},{4,0},{5,1},{6,2},{7,3},{8,12},{9,13},{10,... | collective-permute-start | bytes 393224 | tf_op jit(solution)/shard_map/ppermute | solution.py:643
  85.6 23.7 %all-to-all-start = ((bf16[4,128,1024]{2,1,0:T(8,128)(2,1)}), bf16[4,128,1024]{2,1,0:T(8,128)(2,1)S(1)}, u32[]{:S(2)}, u32[]{:S(2)}) async-start(bf16[4,128,1024]{2,1,0:T(8,128)(2,1)} %bitcast.17), calls=%async_computation | async-start | bytes 2097152 | tf_op jit(solution)/shard_map/all_to_all | solution.py:595
  89.1 27.0 %collective-permute-start.23 = (f32[512,512]{1,0:T(8,128)}, f32[512,512]{1,0:T(8,128)}, u32[]{:S(2)}, u32[]{:S(2)}) collective-permute-start(f32[512,512]{1,0:T(8,128)} %get-tuple-element.178), channel_id=1, source_target_pairs={{0,8},{8,0},{16,24},{24,16},{1,9},{9,1},{17,25},{25,17},{2,10},{10... | collective-permute-start | bytes 3145736 | tf_op jit(solution)/shard_map/ppermute | solution.py:650
  89.2 28.5 %collective-permute-start.19 = (bf16[128,512]{1,0:T(8,128)(2,1)}, bf16[128,512]{1,0:T(8,128)(2,1)S(1)}, u32[]{:S(2)}, u32[]{:S(2)}) collective-permute-start(bf16[128,512]{1,0:T(8,128)(2,1)} %get-tuple-element.173), channel_id=1, source_target_pairs={{0,4},{1,5},{2,6},{3,7},{4,0},{5,1},{6,2},{7,3},{8,12},{9,13},{10,... | collective-permute-start | bytes 393224 | tf_op jit(solution)/shard_map/ppermute | solution.py:587
  90.1 27.7 %collective-permute-start.20 = (bf16[128,512]{1,0:T(8,128)(2,1)}, bf16[128,512]{1,0:T(8,128)(2,1)S(1)}, u32[]{:S(2)}, u32[]{:S(2)}) collective-permute-start(bf16[128,512]{1,0:T(8,128)(2,1)} %get-tuple-element.174), channel_id=1, source_target_pairs={{0,5},{1,4},{2,7},{3,6},{4,1},{5,0},{6,3},{7,2},{8,13},{9,12},{10,... | collective-permute-start | bytes 393224 | tf_op jit(solution)/shard_map/ppermute | solution.py:587
  93.5 24.3 %collective-permute-start.21 = (bf16[128,512]{1,0:T(8,128)(2,1)}, bf16[128,512]{1,0:T(8,128)(2,1)S(1)}, u32[]{:S(2)}, u32[]{:S(2)}) collective-permute-start(bf16[128,512]{1,0:T(8,128)(2,1)} %get-tuple-element.175), channel_id=1, source_target_pairs={{0,6},{1,7},{2,4},{3,5},{4,2},{5,3},{6,0},{7,1},{8,14},{9,15},{10,... | collective-permute-start | bytes 393224 | tf_op jit(solution)/shard_map/ppermute | solution.py:587
  95.4 22.4 %collective-permute-start.22 = (bf16[128,512]{1,0:T(8,128)(2,1)}, bf16[128,512]{1,0:T(8,128)(2,1)S(1)}, u32[]{:S(2)}, u32[]{:S(2)}) collective-permute-start(bf16[128,512]{1,0:T(8,128)(2,1)} %get-tuple-element.176), channel_id=1, source_target_pairs={{0,7},{1,6},{2,5},{3,4},{4,3},{5,2},{6,1},{7,0},{8,15},{9,14},{10,... | collective-permute-start | bytes 393224 | tf_op jit(solution)/shard_map/ppermute | solution.py:587
  119.5 6.6 %collective-permute-start.25 = (bf16[256,512]{1,0:T(8,128)(2,1)S(1)}, bf16[256,512]{1,0:T(8,128)(2,1)S(1)}, u32[]{:S(2)}, u32[]{:S(2)}) collective-permute-start(bf16[256,512]{1,0:T(8,128)(2,1)S(1)} %dynamic-slice_convert_fusion), channel_id=1, source_target_pairs={{0,16},{8,24},{16,0},{24,8},{1,17},{9,25},{17,1},{25,9},{2,18},{10... | collective-permute-start | bytes 786440 | tf_op jit(solution)/shard_map/ppermute | solution.py:667
  (26 other events, 281.4 us)

commit v6 on v4

--- a/solution.py
+++ b/solution.py
@@ -621,19 +621,18 @@
 
     ready, gated = tie((before, gated))
     other_pieces, across = exchange(gated[:hc], 0), gated[hc:]
-    sent = exchange(across[:1], hc)
     outs = prepare(filt, high, low, feats, ready, short_weight, grad_out, scale, count)
-    outs, other_pieces, sent, across, part = tie((outs, other_pieces, sent, across, part))
+    outs, other_pieces, across, part = tie((outs, other_pieces, across, part))
     near, far = outs[hc:]
 
     home_pieces = exchange(outs[:hc], 0)
     rest = lax.ppermute(part, "dp", cores)
-    sent = list(sent) + exchange(across[1:3], hc + 1)
+    sent = exchange(across[:2], hc)
     outs = spectral(high, inverse, (low, part, rest), other_pieces, (), scale)
     far, outs, home_pieces, sent, across = tie((far, outs, home_pieces, sent, across))
 
     other_back = exchange(outs[:hc], 0)
-    sent = list(sent) + exchange(across[3:], hc + 3)
+    sent = list(sent) + exchange(across[2:], hc + 2)
     send, keep = outs[hc:]
     summed = keep + lax.ppermute(send, "dp", cores)
     crossed = lax.ppermute(summed.astype(jnp.bfloat16), "ctx", [(i, i ^ hc) for i in range(count)])

time: 129 us -> 126 us (0.977)
  waiting for transfers between devices: 35.6 us -> 29.5 us
  starting transfers between devices: 41.3 us -> 44.5 us
    ppermute x1, starting transfers between devices: 0.35 us -> 5.57 us  [half_shards(): lax.ppermute(summed.astype(jnp.bfloat16), 'ctx', [(i, i ^ hc) for i in ra...]
    ppermute x17, waiting for transfers between devices: 21.9 us -> 16.8 us  [exchange(): lax.ppermute(piece, 'ctx', [(i, i ^ base + j) for i in devices])]
    ppermute x17, starting transfers between devices: 26.9 us -> 25 us  [exchange(): lax.ppermute(piece, 'ctx', [(i, i ^ base + j) for i in devices])]
    unnamed x46 -> x48, local copies, waits for them, and re-layouts: 2.74 us -> 2.74 us
  transfers between devices with their start and end apart: 26 -> 26, of which waited for: 7 -> 8; matrix products, arithmetic and copies ran while one was open for 2% -> 2% of each run, Pallas kernels for 32% -> 33%
where the time goes in v6:
time: 126 us
  starting transfers between devices  44.5 us (35%)
  Pallas kernels  43.8 us (35%)
  waiting for transfers between devices  29.5 us (23%)
  local copies, waits for them, and re-layouts  3.76 us (3%)
  other arithmetic  2.8 us (2%)
    ppermute x17, starting transfers between devices, exchange(): lax.ppermute(piece, 'ctx', [(i, i ^ base + j) for i in devices])  25 us
    ppermute x17, waiting for transfers between devices, exchange(): lax.ppermute(piece, 'ctx', [(i, i ^ base + j) for i in devices])  16.8 us
    pallas_call x2, Pallas kernels, spectral(): pl.pallas_call(functools.partial(spectral_kernel, hc, rows, home, scale),...  15.9 us
    all_to_all x1, waiting for transfers between devices, within(): lax.all_to_all(stacked, 'ctx', 0, 0, axis_index_groups=groups, tiled=True)  11.9 us
    pallas_call x1, Pallas kernels, prepare(): pl.pallas_call(functools.partial(prepare_kernel, hc, count, scale), in_sp...  10.8 us
    pallas_call x3, Pallas kernels, final(): pl.pallas_call(functools.partial(final_kernel, hc, count, base, top, so_f...  10.8 us
    ppermute x2, starting transfers between devices, from_behind(): return lax.ppermute(block, axis, route)  6.15 us
    ppermute x1, starting transfers between devices, half_shards(): lax.ppermute(summed.astype(jnp.bfloat16), 'ctx', [(i, i ^ hc) for i in ra...  5.57 us
  transfers between devices with their start and end apart: 26, of which 8 were waited for; matrix products, arithmetic and copies ran while one was open for 2% of the time, Pallas kernels for 33%

profile of v6, /device:TPU:0, one launch (start us, length us, event | category | flops | bytes accessed | tf_op | source)
XLA Modules:
  0.0 125.6 jit_solution(3801508300984481109)
XLA Ops:
  1.6 4.9 %collective-permute-start = (bf16[2,12288]{1,0:T(2,128)(2,1)S(1)}, bf16[2,12288]{1,0:T(2,128)(2,1)S(1)}, u32[]{:S(2)}, u32[]{:S(2)}) collective-permute-start(bf16[2,12288]{1,0:T(2,128)(2,1)S(1)} %slice_bitcast_fusion), channel_id=1, source_target_pairs={{0,1},{1,2},{2,3},{3,4},{4,5},{5,6},{6,7},{8,9},{9,10},{10,11},{11... | collective-permute-start | bytes 147464 | tf_op jit(solution)/shard_map/ppermute | solution.py:675
  7.6 2.7 %collective-permute-start.4 = (bf16[256,512]{1,0:T(8,128)(2,1)S(1)}, bf16[256,512]{1,0:T(8,128)(2,1)S(1)}, u32[]{:S(2)}, u32[]{:S(2)}) collective-permute-start(bf16[256,512]{1,0:T(8,128)(2,1)S(1)} %multiply_convert_fusion), channel_id=1, source_target_pairs={{0,4},{1,5},{2,6},{3,7},{4,0},{5,1},{6,2},{7,3},{8,12},{9,13},{10,... | collective-permute-start | bytes 786440 | tf_op jit(solution)/shard_map/ppermute | solution.py:619
  10.9 4.7 %gate_other.1 = (bf16[128,1024]{1,0:T(8,128)(2,1)}, bf16[128,1024]{1,0:T(8,128)(2,1)}, bf16[128,1024]{1,0:T(8,128)(2,1)}, bf16[128,1024]{1,0:T(8,128)(2,1)}, bf1...) custom-call(bf16[128,12288]{1,0:T(8,128)(2,1)} %bitcast.6, ...), custom_call_target="tpu_custom_call" | custom-call | flops 5242880 | bytes 3145728 | tf_op jit(solution)/shard_map/gate_other/pallas_call | solution.py:119
  19.2 10.8 %prepare.1 = (bf16[128,1024]{1,0:T(8,128)(2,1)}, bf16[128,1024]{1,0:T(8,128)(2,1)}, bf16[128,1024]{1,0:T(8,128)(2,1)}, bf16[128,1024]{1,0:T(8,128)(2,1)}, f32[1024,512]{1,0:T(8,128)}, /*index=5*/f32[1024,512]{1,0:T(8,128)}) custom-call(f32[1024,512]{1,0:T(8,128)} %refs_0_.3, bf16[1024,512]{1,0:T(8,128)(2,1)} %constant.48.clone.refs_1_.refs_0_, ...), custom_call_target="tpu_custom_call" | custom-call | flops 4294967296 | bytes 10485760 | tf_op jit(solution)/shard_map/prepare/pallas_call | solution.py:176
  30.0 4.2 %collective-permute-done.3.refs_8_ = bf16[128,1024]{1,0:T(8,128)(2,1)S(1)} collective-permute-done((bf16[128,1024]{1,0:T(8,128)(2,1)}, bf16[128,1024]{1,0:T(8,128)(2,1)S(1)}, u32[]{:S(2)}, u32[]{:S(2)}) %collective-permute-start.3) | collective-permute-done | bytes 262176 | tf_op jit(solution)/shard_map/ppermute | solution.py:587
  34.7 3.0 %collective-permute-start.8 = (bf16[128,1024]{1,0:T(8,128)(2,1)}, bf16[128,1024]{1,0:T(8,128)(2,1)S(1)}, u32[]{:S(2)}, u32[]{:S(2)}) collective-permute-start(bf16[128,1024]{1,0:T(8,128)(2,1)} %get-tuple-element.142), channel_id=1, source_target_pairs={{0,3},{1,2},{2,1},{3,0},{4,7},{5,6},{6,5},{7,4},{8,11},{9,10},{10,... | collective-permute-start | bytes 786440 | tf_op jit(solution)/shard_map/ppermute | solution.py:587
  37.7 2.0 %collective-permute-start.10 = (bf16[128,512]{1,0:T(8,128)(2,1)S(1)}, bf16[128,512]{1,0:T(8,128)(2,1)S(1)}, u32[]{:S(2)}, u32[]{:S(2)}) collective-permute-start(bf16[128,512]{1,0:T(8,128)(2,1)S(1)} %copy-done.21), channel_id=1, source_target_pairs={{0,5},{1,4},{2,7},{3,6},{4,1},{5,0},{6,3},{7,2},{8,13},{9,12},{10,... | collective-permute-start | bytes 393224 | tf_op jit(solution)/shard_map/ppermute | solution.py:587
  40.6 6.1 %spectral_other.1 = (bf16[128,1024]{1,0:T(8,128)(2,1)S(1)}, bf16[128,1024]{1,0:T(8,128)(2,1)S(1)}, bf16[128,1024]{1,0:T(8,128)(2,1)S(1)}, bf16[128,1024]{1,0:T(8...) custom-call(bf16[1024,512]{1,0:T(8,128)(2,1)S(1)} %copy-done.8, bf16[512,1024]{1,0:T(8,128)(2,1)S(1)} %copy-done.9, ...), custom_call_target="tpu_custom_call" | custom-call | flops 2684354560 | bytes 9961472 | tf_op jit(solution)/shard_map/spectral_other/pallas_call | solution.py:369
  46.7 4.3 %collective-permute-done.10.refs_9_ = bf16[128,512]{1,0:T(8,128)(2,1)S(1)} collective-permute-done((bf16[128,512]{1,0:T(8,128)(2,1)S(1)}, bf16[128,512]{1,0:T(8,128)(2,1)S(1)}, u32[]{:S(2)}, u32[]{:S(2)}) %collective-permute-start.10) | collective-permute-done | bytes 131104 | tf_op jit(solution)/shard_map/ppermute | solution.py:587
  50.9 2.4 %collective-permute-done.9.refs_8_ = bf16[128,512]{1,0:T(8,128)(2,1)S(1)} collective-permute-done((bf16[128,512]{1,0:T(8,128)(2,1)S(1)}, bf16[128,512]{1,0:T(8,128)(2,1)S(1)}, u32[]{:S(2)}, u32[]{:S(2)}) %collective-permute-start.9) | collective-permute-done | bytes 131104 | tf_op jit(solution)/shard_map/ppermute | solution.py:587
  53.4 2.1 %collective-permute-done.8.refs_7_ = bf16[128,1024]{1,0:T(8,128)(2,1)S(1)} collective-permute-done((bf16[128,1024]{1,0:T(8,128)(2,1)}, bf16[128,1024]{1,0:T(8,128)(2,1)S(1)}, u32[]{:S(2)}, u32[]{:S(2)}) %collective-permute-start.8) | collective-permute-done | bytes 262176 | tf_op jit(solution)/shard_map/ppermute | solution.py:587
  55.5 2.3 %collective-permute-start.11 = (bf16[128,512]{1,0:T(8,128)(2,1)S(1)}, bf16[128,512]{1,0:T(8,128)(2,1)S(1)}, u32[]{:S(2)}, u32[]{:S(2)}) collective-permute-start(bf16[128,512]{1,0:T(8,128)(2,1)S(1)} %copy-done.17), channel_id=1, source_target_pairs={{0,6},{1,7},{2,4},{3,5},{4,2},{5,3},{6,0},{7,1},{8,14},{9,15},{10,... | collective-permute-start | bytes 393224 | tf_op jit(solution)/shard_map/ppermute | solution.py:587
  60.9 2.0 %collective-permute-start.15 = (bf16[128,1024]{1,0:T(8,128)(2,1)S(1)}, bf16[128,1024]{1,0:T(8,128)(2,1)S(1)}, u32[]{:S(2)}, u32[]{:S(2)}) collective-permute-start(bf16[128,1024]{1,0:T(8,128)(2,1)S(1)} %get-tuple-element.166), channel_id=1, source_target_pairs={{0,3},{1,2},{2,1},{3,0},{4,7},{5,6},{6,5},{7,4},{8,11},{9,10},{10,... | collective-permute-start | bytes 786440 | tf_op jit(solution)/shard_map/ppermute | solution.py:587
  63.3 5.6 %collective-permute-start.17 = (bf16[256,512]{1,0:T(8,128)(2,1)S(1)}, bf16[256,512]{1,0:T(8,128)(2,1)S(1)}, u32[]{:S(2)}, u32[]{:S(2)}) collective-permute-start(bf16[256,512]{1,0:T(8,128)(2,1)S(1)} %add_convert_fusion), channel_id=1, source_target_pairs={{0,4},{1,5},{2,6},{3,7},{4,0},{5,1},{6,2},{7,3},{8,12},{9,13},{10,... | collective-permute-start | bytes 786440 | tf_op jit(solution)/shard_map/ppermute | solution.py:638
  69.6 9.9 %spectral_home.1 = (bf16[512,1024]{1,0:T(8,128)(2,1)}, bf16[128,512]{1,0:T(8,128)(2,1)}, bf16[128,512]{1,0:T(8,128)(2,1)}, bf16[128,512]{1,0:T(8,128)(2,1)}, bf1...) custom-call(bf16[1024,512]{1,0:T(8,128)(2,1)} %constant.48.clone.refs_1_.refs_0_, ...), custom_call_target="tpu_custom_call" | custom-call | flops 4294967296 | bytes 9961472 | tf_op jit(solution)/shard_map/spectral_home/pallas_call | solution.py:369
  79.5 3.4 %collective-permute-done.15.refs_7_ = bf16[128,1024]{1,0:T(8,128)(2,1)S(1)} collective-permute-done((bf16[128,1024]{1,0:T(8,128)(2,1)S(1)}, bf16[128,1024]{1,0:T(8,128)(2,1)S(1)}, u32[]{:S(2)}, u32[]{:S(2)}) %collective-permute-start.15) | collective-permute-done | bytes 262176 | tf_op jit(solution)/shard_map/ppermute | solution.py:587
  82.9 3.5 %all-to-all-start = ((bf16[4,128,1024]{2,1,0:T(8,128)(2,1)}), bf16[4,128,1024]{2,1,0:T(8,128)(2,1)S(1)}, u32[]{:S(2)}, u32[]{:S(2)}) async-start(bf16[4,128,1024]{2,1,0:T(8,128)(2,1)} %bitcast.17), calls=%async_computation | async-start | bytes 2097152 | tf_op jit(solution)/shard_map/all_to_all | solution.py:595
  86.5 1.7 %collective-permute-start.18 = (bf16[128,512]{1,0:T(8,128)(2,1)}, bf16[128,512]{1,0:T(8,128)(2,1)S(1)}, u32[]{:S(2)}, u32[]{:S(2)}) collective-permute-start(bf16[128,512]{1,0:T(8,128)(2,1)} %get-tuple-element.173), channel_id=1, source_target_pairs={{0,4},{1,5},{2,6},{3,7},{4,0},{5,1},{6,2},{7,3},{8,12},{9,13},{10,... | collective-permute-start | bytes 393224 | tf_op jit(solution)/shard_map/ppermute | solution.py:587
  88.2 2.5 %collective-permute-start.19 = (bf16[128,512]{1,0:T(8,128)(2,1)}, bf16[128,512]{1,0:T(8,128)(2,1)S(1)}, u32[]{:S(2)}, u32[]{:S(2)}) collective-permute-start(bf16[128,512]{1,0:T(8,128)(2,1)} %get-tuple-element.174), channel_id=1, source_target_pairs={{0,5},{1,4},{2,7},{3,6},{4,1},{5,0},{6,3},{7,2},{8,13},{9,12},{10,... | collective-permute-start | bytes 393224 | tf_op jit(solution)/shard_map/ppermute | solution.py:587
  90.8 2.7 %collective-permute-start.20 = (bf16[128,512]{1,0:T(8,128)(2,1)}, bf16[128,512]{1,0:T(8,128)(2,1)S(1)}, u32[]{:S(2)}, u32[]{:S(2)}) collective-permute-start(bf16[128,512]{1,0:T(8,128)(2,1)} %get-tuple-element.175), channel_id=1, source_target_pairs={{0,6},{1,7},{2,4},{3,5},{4,2},{5,3},{6,0},{7,1},{8,14},{9,15},{10,... | collective-permute-start | bytes 393224 | tf_op jit(solution)/shard_map/ppermute | solution.py:587
  94.3 11.9 %all-to-all-done.refs_4_ = bf16[4,128,1024]{2,1,0:T(8,128)(2,1)S(1)} async-done(((bf16[4,128,1024]{2,1,0:T(8,128)(2,1)}), bf16[4,128,1024]{2,1,0:T(8,128)(2,1)S(1)}, u32[]{:S(2)}, u32[]{:S(2)}) %all-to-all-start) | async-done | bytes 1048608 | tf_op jit(solution)/shard_map/all_to_all | solution.py:595
  107.1 5.9 %final_home.1 = (bf16[128,12288]{1,0:T(8,128)(2,1)}, bf16[4,3,2,512]{3,2,1,0:T(2,128)(2,1)}, f32[4,3,16,512]{3,2,1,0:T(8,128)}) custom-call(bf16[128,12288]{1,0:T(8,128)(2,1)} %bitcast.8, bf16[2,12288]{1,0:T(2,128)(2,1)} %copy-done.3, bf16[128,4096]{1,0:T(8,128)(2,1)} %bitcast.13, f32[3,12288]{1,0:T(4,128)} %taps_ref.3, bf16[4,128,1024]{2,1,0:T(8,128)(2,1)} %copy-done.11), custom_call_target="tpu_custom_call" | custom-call | flops 7864320 | bytes 4194304 | tf_op jit(solution)/shard_map/final_home/pallas_call | solution.py:518
  119.1 3.9 %final_other.1 = (bf16[128,12288]{1,0:T(8,128)(2,1)}, bf16[4,3,2,512]{3,2,1,0:T(2,128)(2,1)}, f32[4,3,16,512]{3,2,1,0:T(8,128)S(1)}) custom-call(bf16[128,12288]{1,0:T(8,128)(2,1)S(1)} %bitcast.10, bf16[2,12288]{1,0:T(2,128)(2,1)S(1)} %copy-done.4, bf16[128,4096]{1,0:T(8,128)(2,1)S(1)} %bitcast.15, ...), custom_call_target="tpu_custom_call", output_to_operand_aliasing={{0}: (12, {})} | custom-call | flops 7864320 | bytes 4194304 | tf_op jit(solution)/shard_map/final_other/pallas_call | solution.py:518
  123.8 1.7 %fix.1 = (bf16[128,12288]{1,0:T(8,128)(2,1)}, f32[256,512]{1,0:T(8,128)}) custom-call(f32[3,12288]{1,0:T(4,128)S(1)} %copy-done.2, bf16[2,4,3,2,512]{4,3,2,1,0:T(2,128)(2,1)S(1)} %collective-permute-done.23.edge_ref, f32[4,3,16,512]{3,2,1,0:T(8,128)S(1)} %copy-done.5, ...), custom_call_target="tpu_custom_call", output_to_operand_aliasing={{0}: (6, {})} | custom-call | flops 1572864 | bytes 1572864 | tf_op jit(solution)/shard_map/fix/pallas_call | solution.py:568
  (89 shorter events, 20.5 us)
Async XLA Ops:
  1.6 8.6 %collective-permute-start = (bf16[2,12288]{1,0:T(2,128)(2,1)S(1)}, bf16[2,12288]{1,0:T(2,128)(2,1)S(1)}, u32[]{:S(2)}, u32[]{:S(2)}) collective-permute-start(bf16[2,12288]{1,0:T(2,128)(2,1)S(1)} %slice_bitcast_fusion), channel_id=1, source_target_pairs={{0,1},{1,2},{2,3},{3,4},{4,5},{5,6},{6,7},{8,9},{9,10},{10,11},{11... | collective-permute-start | bytes 147464 | tf_op jit(solution)/shard_map/ppermute | solution.py:675
  7.6 22.4 %collective-permute-start.4 = (bf16[256,512]{1,0:T(8,128)(2,1)S(1)}, bf16[256,512]{1,0:T(8,128)(2,1)S(1)}, u32[]{:S(2)}, u32[]{:S(2)}) collective-permute-start(bf16[256,512]{1,0:T(8,128)(2,1)S(1)} %multiply_convert_fusion), channel_id=1, source_target_pairs={{0,4},{1,5},{2,6},{3,7},{4,0},{5,1},{6,2},{7,3},{8,12},{9,13},{10,... | collective-permute-start | bytes 786440 | tf_op jit(solution)/shard_map/ppermute | solution.py:619
  15.6 14.4 %collective-permute-start.1 = (bf16[128,1024]{1,0:T(8,128)(2,1)}, bf16[128,1024]{1,0:T(8,128)(2,1)S(1)}, u32[]{:S(2)}, u32[]{:S(2)}) collective-permute-start(bf16[128,1024]{1,0:T(8,128)(2,1)} %get-tuple-element.118), channel_id=1, source_target_pairs={{0,1},{1,0},{2,3},{3,2},{4,5},{5,4},{6,7},{7,6},{8,9},{9,8},{10,11... | collective-permute-start | bytes 786440 | tf_op jit(solution)/shard_map/ppermute | solution.py:587
  17.2 12.8 %collective-permute-start.2 = (bf16[128,1024]{1,0:T(8,128)(2,1)}, bf16[128,1024]{1,0:T(8,128)(2,1)S(1)}, u32[]{:S(2)}, u32[]{:S(2)}) collective-permute-start(bf16[128,1024]{1,0:T(8,128)(2,1)} %get-tuple-element.119), channel_id=1, source_target_pairs={{0,2},{1,3},{2,0},{3,1},{4,6},{5,7},{6,4},{7,5},{8,10},{9,11},{10,... | collective-permute-start | bytes 786440 | tf_op jit(solution)/shard_map/ppermute | solution.py:587
  17.6 16.6 %collective-permute-start.3 = (bf16[128,1024]{1,0:T(8,128)(2,1)}, bf16[128,1024]{1,0:T(8,128)(2,1)S(1)}, u32[]{:S(2)}, u32[]{:S(2)}) collective-permute-start(bf16[128,1024]{1,0:T(8,128)(2,1)} %get-tuple-element.120), channel_id=1, source_target_pairs={{0,3},{1,2},{2,1},{3,0},{4,7},{5,6},{6,5},{7,4},{8,11},{9,10},{10,... | collective-permute-start | bytes 786440 | tf_op jit(solution)/shard_map/ppermute | solution.py:587
  34.2 19.2 %collective-permute-start.6 = (bf16[128,1024]{1,0:T(8,128)(2,1)}, bf16[128,1024]{1,0:T(8,128)(2,1)S(1)}, u32[]{:S(2)}, u32[]{:S(2)}) collective-permute-start(bf16[128,1024]{1,0:T(8,128)(2,1)} %get-tuple-element.140), channel_id=1, source_target_pairs={{0,1},{1,0},{2,3},{3,2},{4,5},{5,4},{6,7},{7,6},{8,9},{9,8},{10,11... | collective-permute-start | bytes 786440 | tf_op jit(solution)/shard_map/ppermute | solution.py:587
  34.7 18.6 %collective-permute-start.7 = (bf16[128,1024]{1,0:T(8,128)(2,1)}, bf16[128,1024]{1,0:T(8,128)(2,1)S(1)}, u32[]{:S(2)}, u32[]{:S(2)}) collective-permute-start(bf16[128,1024]{1,0:T(8,128)(2,1)} %get-tuple-element.141), channel_id=1, source_target_pairs={{0,2},{1,3},{2,0},{3,1},{4,6},{5,7},{6,4},{7,5},{8,10},{9,11},{10,... | collective-permute-start | bytes 786440 | tf_op jit(solution)/shard_map/ppermute | solution.py:587
  34.7 20.8 %collective-permute-start.8 = (bf16[128,1024]{1,0:T(8,128)(2,1)}, bf16[128,1024]{1,0:T(8,128)(2,1)S(1)}, u32[]{:S(2)}, u32[]{:S(2)}) collective-permute-start(bf16[128,1024]{1,0:T(8,128)(2,1)} %get-tuple-element.142), channel_id=1, source_target_pairs={{0,3},{1,2},{2,1},{3,0},{4,7},{5,6},{6,5},{7,4},{8,11},{9,10},{10,... | collective-permute-start | bytes 786440 | tf_op jit(solution)/shard_map/ppermute | solution.py:587
  37.7 13.2 %collective-permute-start.10 = (bf16[128,512]{1,0:T(8,128)(2,1)S(1)}, bf16[128,512]{1,0:T(8,128)(2,1)S(1)}, u32[]{:S(2)}, u32[]{:S(2)}) collective-permute-start(bf16[128,512]{1,0:T(8,128)(2,1)S(1)} %copy-done.21), channel_id=1, source_target_pairs={{0,5},{1,4},{2,7},{3,6},{4,1},{5,0},{6,3},{7,2},{8,13},{9,12},{10,... | collective-permute-start | bytes 393224 | tf_op jit(solution)/shard_map/ppermute | solution.py:587
  39.7 13.7 %collective-permute-start.9 = (bf16[128,512]{1,0:T(8,128)(2,1)S(1)}, bf16[128,512]{1,0:T(8,128)(2,1)S(1)}, u32[]{:S(2)}, u32[]{:S(2)}) collective-permute-start(bf16[128,512]{1,0:T(8,128)(2,1)S(1)} %copy-done.20), channel_id=1, source_target_pairs={{0,4},{1,5},{2,6},{3,7},{4,0},{5,1},{6,2},{7,3},{8,12},{9,13},{10,... | collective-permute-start | bytes 393224 | tf_op jit(solution)/shard_map/ppermute | solution.py:587
  55.5 7.8 %collective-permute-start.11 = (bf16[128,512]{1,0:T(8,128)(2,1)S(1)}, bf16[128,512]{1,0:T(8,128)(2,1)S(1)}, u32[]{:S(2)}, u32[]{:S(2)}) collective-permute-start(bf16[128,512]{1,0:T(8,128)(2,1)S(1)} %copy-done.17), channel_id=1, source_target_pairs={{0,6},{1,7},{2,4},{3,5},{4,2},{5,3},{6,0},{7,1},{8,14},{9,15},{10,... | collective-permute-start | bytes 393224 | tf_op jit(solution)/shard_map/ppermute | solution.py:587
  57.8 11.1 %collective-permute-start.12 = (bf16[128,512]{1,0:T(8,128)(2,1)S(1)}, bf16[128,512]{1,0:T(8,128)(2,1)S(1)}, u32[]{:S(2)}, u32[]{:S(2)}) collective-permute-start(bf16[128,512]{1,0:T(8,128)(2,1)S(1)} %copy-done.16), channel_id=1, source_target_pairs={{0,7},{1,6},{2,5},{3,4},{4,3},{5,2},{6,1},{7,0},{8,15},{9,14},{10,... | collective-permute-start | bytes 393224 | tf_op jit(solution)/shard_map/ppermute | solution.py:587
  59.3 20.1 %collective-permute-start.13 = (bf16[128,1024]{1,0:T(8,128)(2,1)S(1)}, bf16[128,1024]{1,0:T(8,128)(2,1)S(1)}, u32[]{:S(2)}, u32[]{:S(2)}) collective-permute-start(bf16[128,1024]{1,0:T(8,128)(2,1)S(1)} %get-tuple-element.164), channel_id=1, source_target_pairs={{0,1},{1,0},{2,3},{3,2},{4,5},{5,4},{6,7},{7,6},{8,9},{9,8},{10,11... | collective-permute-start | bytes 786440 | tf_op jit(solution)/shard_map/ppermute | solution.py:587
  60.9 18.6 %collective-permute-start.14 = (bf16[128,1024]{1,0:T(8,128)(2,1)S(1)}, bf16[128,1024]{1,0:T(8,128)(2,1)S(1)}, u32[]{:S(2)}, u32[]{:S(2)}) collective-permute-start(bf16[128,1024]{1,0:T(8,128)(2,1)S(1)} %get-tuple-element.165), channel_id=1, source_target_pairs={{0,2},{1,3},{2,0},{3,1},{4,6},{5,7},{6,4},{7,5},{8,10},{9,11},{10,... | collective-permute-start | bytes 786440 | tf_op jit(solution)/shard_map/ppermute | solution.py:587
  60.9 22.1 %collective-permute-start.15 = (bf16[128,1024]{1,0:T(8,128)(2,1)S(1)}, bf16[128,1024]{1,0:T(8,128)(2,1)S(1)}, u32[]{:S(2)}, u32[]{:S(2)}) collective-permute-start(bf16[128,1024]{1,0:T(8,128)(2,1)S(1)} %get-tuple-element.166), channel_id=1, source_target_pairs={{0,3},{1,2},{2,1},{3,0},{4,7},{5,6},{6,5},{7,4},{8,11},{9,10},{10,... | collective-permute-start | bytes 786440 | tf_op jit(solution)/shard_map/ppermute | solution.py:587
  63.3 19.6 %collective-permute-start.17 = (bf16[256,512]{1,0:T(8,128)(2,1)S(1)}, bf16[256,512]{1,0:T(8,128)(2,1)S(1)}, u32[]{:S(2)}, u32[]{:S(2)}) collective-permute-start(bf16[256,512]{1,0:T(8,128)(2,1)S(1)} %add_convert_fusion), channel_id=1, source_target_pairs={{0,4},{1,5},{2,6},{3,7},{4,0},{5,1},{6,2},{7,3},{8,12},{9,13},{10,... | collective-permute-start | bytes 786440 | tf_op jit(solution)/shard_map/ppermute | solution.py:638
  82.9 23.2 %all-to-all-start = ((bf16[4,128,1024]{2,1,0:T(8,128)(2,1)}), bf16[4,128,1024]{2,1,0:T(8,128)(2,1)S(1)}, u32[]{:S(2)}, u32[]{:S(2)}) async-start(bf16[4,128,1024]{2,1,0:T(8,128)(2,1)} %bitcast.17), calls=%async_computation | async-start | bytes 2097152 | tf_op jit(solution)/shard_map/all_to_all | solution.py:595
  86.4 26.6 %collective-permute-start.22 = (f32[512,512]{1,0:T(8,128)}, f32[512,512]{1,0:T(8,128)}, u32[]{:S(2)}, u32[]{:S(2)}) collective-permute-start(f32[512,512]{1,0:T(8,128)} %get-tuple-element.178), channel_id=1, source_target_pairs={{0,8},{8,0},{16,24},{24,16},{1,9},{9,1},{17,25},{25,17},{2,10},{10... | collective-permute-start | bytes 3145736 | tf_op jit(solution)/shard_map/ppermute | solution.py:645
  86.5 28.2 %collective-permute-start.18 = (bf16[128,512]{1,0:T(8,128)(2,1)}, bf16[128,512]{1,0:T(8,128)(2,1)S(1)}, u32[]{:S(2)}, u32[]{:S(2)}) collective-permute-start(bf16[128,512]{1,0:T(8,128)(2,1)} %get-tuple-element.173), channel_id=1, source_target_pairs={{0,4},{1,5},{2,6},{3,7},{4,0},{5,1},{6,2},{7,3},{8,12},{9,13},{10,... | collective-permute-start | bytes 393224 | tf_op jit(solution)/shard_map/ppermute | solution.py:587
  88.2 26.5 %collective-permute-start.19 = (bf16[128,512]{1,0:T(8,128)(2,1)}, bf16[128,512]{1,0:T(8,128)(2,1)S(1)}, u32[]{:S(2)}, u32[]{:S(2)}) collective-permute-start(bf16[128,512]{1,0:T(8,128)(2,1)} %get-tuple-element.174), channel_id=1, source_target_pairs={{0,5},{1,4},{2,7},{3,6},{4,1},{5,0},{6,3},{7,2},{8,13},{9,12},{10,... | collective-permute-start | bytes 393224 | tf_op jit(solution)/shard_map/ppermute | solution.py:587
  90.8 24.0 %collective-permute-start.20 = (bf16[128,512]{1,0:T(8,128)(2,1)}, bf16[128,512]{1,0:T(8,128)(2,1)S(1)}, u32[]{:S(2)}, u32[]{:S(2)}) collective-permute-start(bf16[128,512]{1,0:T(8,128)(2,1)} %get-tuple-element.175), channel_id=1, source_target_pairs={{0,6},{1,7},{2,4},{3,5},{4,2},{5,3},{6,0},{7,1},{8,14},{9,15},{10,... | collective-permute-start | bytes 393224 | tf_op jit(solution)/shard_map/ppermute | solution.py:587
  93.5 21.3 %collective-permute-start.21 = (bf16[128,512]{1,0:T(8,128)(2,1)}, bf16[128,512]{1,0:T(8,128)(2,1)S(1)}, u32[]{:S(2)}, u32[]{:S(2)}) collective-permute-start(bf16[128,512]{1,0:T(8,128)(2,1)} %get-tuple-element.176), channel_id=1, source_target_pairs={{0,7},{1,6},{2,5},{3,4},{4,3},{5,2},{6,1},{7,0},{8,15},{9,14},{10,... | collective-permute-start | bytes 393224 | tf_op jit(solution)/shard_map/ppermute | solution.py:587
  116.2 7.5 %collective-permute-start.24 = (bf16[256,512]{1,0:T(8,128)(2,1)S(1)}, bf16[256,512]{1,0:T(8,128)(2,1)S(1)}, u32[]{:S(2)}, u32[]{:S(2)}) collective-permute-start(bf16[256,512]{1,0:T(8,128)(2,1)S(1)} %dynamic-slice_convert_fusion), channel_id=1, source_target_pairs={{0,16},{8,24},{16,0},{24,8},{1,17},{9,25},{17,1},{25,9},{2,18},{10... | collective-permute-start | bytes 786440 | tf_op jit(solution)/shard_map/ppermute | solution.py:660
  117.8 6.0 %collective-permute-start.23 = (bf16[2,4,3,2,512]{4,3,2,1,0:T(2,128)(2,1)S(1)}, bf16[2,4,3,2,512]{4,3,2,1,0:T(2,128)(2,1)S(1)}, u32[]{:S(2)}, u32[]{:S(2)}) collective-permute-start(bf16[2,4,3,2,512]{4,3,2,1,0:T(2,128)(2,1)S(1)} %edge_other.1), channel_id=1, source_target_pairs={{1,0},{2,1},{3,2},{4,3},{5,4},{6,5},{7,6},{9,8},{10,9},{11,10},{12... | collective-permute-start | bytes 147464 | tf_op jit(solution)/shard_map/ppermute | solution.py:675
  (26 other events, 315.2 us)

commit v7 on v6

--- a/solution.py
+++ b/solution.py
@@ -627,12 +627,12 @@
 
     home_pieces = exchange(outs[:hc], 0)
     rest = lax.ppermute(part, "dp", cores)
-    sent = exchange(across[:2], hc)
+    far_sent = exchange(across[2:], hc + 2)
     outs = spectral(high, inverse, (low, part, rest), other_pieces, (), scale)
-    far, outs, home_pieces, sent, across = tie((far, outs, home_pieces, sent, across))
+    far, outs, home_pieces, far_sent, across = tie((far, outs, home_pieces, far_sent, across))
 
     other_back = exchange(outs[:hc], 0)
-    sent = list(sent) + exchange(across[2:], hc + 2)
+    sent = exchange(across[:2], hc) + list(far_sent)
     send, keep = outs[hc:]
     summed = keep + lax.ppermute(send, "dp", cores)
     crossed = lax.ppermute(summed.astype(jnp.bfloat16), "ctx", [(i, i ^ hc) for i in range(count)])

time: 126 us -> 133 us (1.056)
  waiting for transfers between devices: 29.5 us -> 41.2 us
  starting transfers between devices: 44.5 us -> 39 us
    ppermute x17, waiting for transfers between devices: 16.8 us -> 24.8 us  [exchange(): lax.ppermute(piece, 'ctx', [(i, i ^ base + j) for i in devices])]
    ppermute x1, starting transfers between devices: 5.57 us -> 0.01 us  [half_shards(): lax.ppermute(summed.astype(jnp.bfloat16), 'ctx', [(i, i ^ hc) for i in ra...]
    ppermute x2, waiting for transfers between devices: 0.78 us -> 4.14 us  [from_behind(): return lax.ppermute(block, axis, route)]
  transfers between devices with their start and end apart: 26 -> 26, of which waited for: 8 -> 8; matrix products, arithmetic and copies ran while one was open for 2% -> 2% of each run, Pallas kernels for 33% -> 31%
where the time goes in v7:
time: 133 us; the launch traced here: 132 us
  Pallas kernels  43.8 us (33%)
  waiting for transfers between devices  41.2 us (31%)
  starting transfers between devices  39 us (29%)
  local copies, waits for them, and re-layouts  3.76 us (3%)
  other arithmetic  2.8 us (2%)
    ppermute x17, starting transfers between devices, exchange(): lax.ppermute(piece, 'ctx', [(i, i ^ base + j) for i in devices])  24.9 us
    ppermute x17, waiting for transfers between devices, exchange(): lax.ppermute(piece, 'ctx', [(i, i ^ base + j) for i in devices])  24.8 us
    pallas_call x2, Pallas kernels, spectral(): pl.pallas_call(functools.partial(spectral_kernel, hc, rows, home, scale),...  15.9 us
    all_to_all x1, waiting for transfers between devices, within(): lax.all_to_all(stacked, 'ctx', 0, 0, axis_index_groups=groups, tiled=True)  12.3 us
    pallas_call x1, Pallas kernels, prepare(): pl.pallas_call(functools.partial(prepare_kernel, hc, count, scale), in_sp...  10.8 us
    pallas_call x3, Pallas kernels, final(): pl.pallas_call(functools.partial(final_kernel, hc, count, base, top, so_f...  10.8 us
    ppermute x2, starting transfers between devices, from_behind(): return lax.ppermute(block, axis, route)  6.15 us
    pallas_call x1, Pallas kernels, gate(): pl.pallas_call(functools.partial(gate_kernel, hc, count, base), in_specs=...  4.66 us
  transfers between devices with their start and end apart: 26, of which 8 were waited for; matrix products, arithmetic and copies ran while one was open for 2% of the time, Pallas kernels for 31%

profile of v7, /device:TPU:0, one launch (start us, length us, event | category | flops | bytes accessed | tf_op | source)
XLA Modules:
  0.0 131.8 jit_solution(13942025513101400540)
XLA Ops:
  1.6 4.9 %collective-permute-start = (bf16[2,12288]{1,0:T(2,128)(2,1)S(1)}, bf16[2,12288]{1,0:T(2,128)(2,1)S(1)}, u32[]{:S(2)}, u32[]{:S(2)}) collective-permute-start(bf16[2,12288]{1,0:T(2,128)(2,1)S(1)} %slice_bitcast_fusion), channel_id=1, source_target_pairs={{0,1},{1,2},{2,3},{3,4},{4,5},{5,6},{6,7},{8,9},{9,10},{10,11},{11... | collective-permute-start | bytes 147464 | tf_op jit(solution)/shard_map/ppermute | solution.py:675
  7.6 2.7 %collective-permute-start.4 = (bf16[256,512]{1,0:T(8,128)(2,1)S(1)}, bf16[256,512]{1,0:T(8,128)(2,1)S(1)}, u32[]{:S(2)}, u32[]{:S(2)}) collective-permute-start(bf16[256,512]{1,0:T(8,128)(2,1)S(1)} %multiply_convert_fusion), channel_id=1, source_target_pairs={{0,4},{1,5},{2,6},{3,7},{4,0},{5,1},{6,2},{7,3},{8,12},{9,13},{10,... | collective-permute-start | bytes 786440 | tf_op jit(solution)/shard_map/ppermute | solution.py:619
  10.9 4.7 %gate_other.1 = (bf16[128,1024]{1,0:T(8,128)(2,1)}, bf16[128,1024]{1,0:T(8,128)(2,1)}, bf16[128,1024]{1,0:T(8,128)(2,1)}, bf16[128,1024]{1,0:T(8,128)(2,1)}, bf1...) custom-call(bf16[128,12288]{1,0:T(8,128)(2,1)} %bitcast.6, ...), custom_call_target="tpu_custom_call" | custom-call | flops 5242880 | bytes 3145728 | tf_op jit(solution)/shard_map/gate_other/pallas_call | solution.py:119
  19.2 10.8 %prepare.1 = (bf16[128,1024]{1,0:T(8,128)(2,1)}, bf16[128,1024]{1,0:T(8,128)(2,1)}, bf16[128,1024]{1,0:T(8,128)(2,1)}, bf16[128,1024]{1,0:T(8,128)(2,1)}, f32[1024,512]{1,0:T(8,128)}, /*index=5*/f32[1024,512]{1,0:T(8,128)}) custom-call(f32[1024,512]{1,0:T(8,128)} %refs_0_.3, bf16[1024,512]{1,0:T(8,128)(2,1)} %constant.48.clone.refs_1_.refs_0_, ...), custom_call_target="tpu_custom_call" | custom-call | flops 4294967296 | bytes 10485760 | tf_op jit(solution)/shard_map/prepare/pallas_call | solution.py:176
  30.0 4.2 %collective-permute-done.3.refs_8_ = bf16[128,1024]{1,0:T(8,128)(2,1)S(1)} collective-permute-done((bf16[128,1024]{1,0:T(8,128)(2,1)}, bf16[128,1024]{1,0:T(8,128)(2,1)S(1)}, u32[]{:S(2)}, u32[]{:S(2)}) %collective-permute-start.3) | collective-permute-done | bytes 262176 | tf_op jit(solution)/shard_map/ppermute | solution.py:587
  34.7 3.0 %collective-permute-start.8 = (bf16[128,1024]{1,0:T(8,128)(2,1)}, bf16[128,1024]{1,0:T(8,128)(2,1)S(1)}, u32[]{:S(2)}, u32[]{:S(2)}) collective-permute-start(bf16[128,1024]{1,0:T(8,128)(2,1)} %get-tuple-element.142), channel_id=1, source_target_pairs={{0,3},{1,2},{2,1},{3,0},{4,7},{5,6},{6,5},{7,4},{8,11},{9,10},{10,... | collective-permute-start | bytes 786440 | tf_op jit(solution)/shard_map/ppermute | solution.py:587
  37.7 3.4 %collective-permute-start.10 = (bf16[128,512]{1,0:T(8,128)(2,1)S(1)}, bf16[128,512]{1,0:T(8,128)(2,1)S(1)}, u32[]{:S(2)}, u32[]{:S(2)}) collective-permute-start(bf16[128,512]{1,0:T(8,128)(2,1)S(1)} %copy-done.21), channel_id=1, source_target_pairs={{0,7},{1,6},{2,5},{3,4},{4,3},{5,2},{6,1},{7,0},{8,15},{9,14},{10,... | collective-permute-start | bytes 393224 | tf_op jit(solution)/shard_map/ppermute | solution.py:587
  41.5 6.1 %spectral_other.1 = (bf16[128,1024]{1,0:T(8,128)(2,1)S(1)}, bf16[128,1024]{1,0:T(8,128)(2,1)S(1)}, bf16[128,1024]{1,0:T(8,128)(2,1)S(1)}, bf16[128,1024]{1,0:T(8...) custom-call(bf16[1024,512]{1,0:T(8,128)(2,1)S(1)} %copy-done.8, bf16[512,1024]{1,0:T(8,128)(2,1)S(1)} %copy-done.9, ...), custom_call_target="tpu_custom_call" | custom-call | flops 2684354560 | bytes 9961472 | tf_op jit(solution)/shard_map/spectral_other/pallas_call | solution.py:369
  47.6 6.1 %collective-permute-done.10.refs_11_ = bf16[128,512]{1,0:T(8,128)(2,1)S(1)} collective-permute-done((bf16[128,512]{1,0:T(8,128)(2,1)S(1)}, bf16[128,512]{1,0:T(8,128)(2,1)S(1)}, u32[]{:S(2)}, u32[]{:S(2)}) %collective-permute-start.10) | collective-permute-done | bytes 131104 | tf_op jit(solution)/shard_map/ppermute | solution.py:587
  53.7 2.6 %collective-permute-done.9.refs_10_ = bf16[128,512]{1,0:T(8,128)(2,1)S(1)} collective-permute-done((bf16[128,512]{1,0:T(8,128)(2,1)S(1)}, bf16[128,512]{1,0:T(8,128)(2,1)S(1)}, u32[]{:S(2)}, u32[]{:S(2)}) %collective-permute-start.9) | collective-permute-done | bytes 131104 | tf_op jit(solution)/shard_map/ppermute | solution.py:587
  56.5 2.8 %collective-permute-start.12 = (bf16[128,512]{1,0:T(8,128)(2,1)S(1)}, bf16[128,512]{1,0:T(8,128)(2,1)S(1)}, u32[]{:S(2)}, u32[]{:S(2)}) collective-permute-start(bf16[128,512]{1,0:T(8,128)(2,1)S(1)} %copy-done.16), channel_id=1, source_target_pairs={{0,5},{1,4},{2,7},{3,6},{4,1},{5,0},{6,3},{7,2},{8,13},{9,12},{10,... | collective-permute-start | bytes 393224 | tf_op jit(solution)/shard_map/ppermute | solution.py:587
  60.9 1.9 %collective-permute-start.15 = (bf16[128,1024]{1,0:T(8,128)(2,1)S(1)}, bf16[128,1024]{1,0:T(8,128)(2,1)S(1)}, u32[]{:S(2)}, u32[]{:S(2)}) collective-permute-start(bf16[128,1024]{1,0:T(8,128)(2,1)S(1)} %get-tuple-element.166), channel_id=1, source_target_pairs={{0,3},{1,2},{2,1},{3,0},{4,7},{5,6},{6,5},{7,4},{8,11},{9,10},{10,... | collective-permute-start | bytes 786440 | tf_op jit(solution)/shard_map/ppermute | solution.py:587
  62.9 4.8 %collective-permute-done.11.refs_8_ = bf16[128,512]{1,0:T(8,128)(2,1)S(1)} collective-permute-done((bf16[128,512]{1,0:T(8,128)(2,1)S(1)}, bf16[128,512]{1,0:T(8,128)(2,1)S(1)}, u32[]{:S(2)}, u32[]{:S(2)}) %collective-permute-start.11) | collective-permute-done | bytes 131104 | tf_op jit(solution)/shard_map/ppermute | solution.py:587
  67.7 3.9 %collective-permute-done.12.refs_9_ = bf16[128,512]{1,0:T(8,128)(2,1)S(1)} collective-permute-done((bf16[128,512]{1,0:T(8,128)(2,1)S(1)}, bf16[128,512]{1,0:T(8,128)(2,1)S(1)}, u32[]{:S(2)}, u32[]{:S(2)}) %collective-permute-start.12) | collective-permute-done | bytes 131104 | tf_op jit(solution)/shard_map/ppermute | solution.py:587
  72.3 9.9 %spectral_home.1 = (bf16[512,1024]{1,0:T(8,128)(2,1)}, bf16[128,512]{1,0:T(8,128)(2,1)}, bf16[128,512]{1,0:T(8,128)(2,1)}, bf16[128,512]{1,0:T(8,128)(2,1)}, bf1...) custom-call(bf16[1024,512]{1,0:T(8,128)(2,1)} %constant.48.clone.refs_1_.refs_0_, ...), custom_call_target="tpu_custom_call" | custom-call | flops 4294967296 | bytes 9961472 | tf_op jit(solution)/shard_map/spectral_home/pallas_call | solution.py:369
  82.2 3.1 %collective-permute-done.15.refs_7_ = bf16[128,1024]{1,0:T(8,128)(2,1)S(1)} collective-permute-done((bf16[128,1024]{1,0:T(8,128)(2,1)S(1)}, bf16[128,1024]{1,0:T(8,128)(2,1)S(1)}, u32[]{:S(2)}, u32[]{:S(2)}) %collective-permute-start.15) | collective-permute-done | bytes 262176 | tf_op jit(solution)/shard_map/ppermute | solution.py:587
  85.4 3.5 %all-to-all-start = ((bf16[4,128,1024]{2,1,0:T(8,128)(2,1)}), bf16[4,128,1024]{2,1,0:T(8,128)(2,1)S(1)}, u32[]{:S(2)}, u32[]{:S(2)}) async-start(bf16[4,128,1024]{2,1,0:T(8,128)(2,1)} %bitcast.17), calls=%async_computation | async-start | bytes 2097152 | tf_op jit(solution)/shard_map/all_to_all | solution.py:595
  89.5 3.7 %collective-permute-start.19 = (bf16[128,512]{1,0:T(8,128)(2,1)}, bf16[128,512]{1,0:T(8,128)(2,1)S(1)}, u32[]{:S(2)}, u32[]{:S(2)}) collective-permute-start(bf16[128,512]{1,0:T(8,128)(2,1)} %get-tuple-element.174), channel_id=1, source_target_pairs={{0,5},{1,4},{2,7},{3,6},{4,1},{5,0},{6,3},{7,2},{8,13},{9,12},{10,... | collective-permute-start | bytes 393224 | tf_op jit(solution)/shard_map/ppermute | solution.py:587
  94.8 1.9 %collective-permute-start.21 = (bf16[128,512]{1,0:T(8,128)(2,1)}, bf16[128,512]{1,0:T(8,128)(2,1)S(1)}, u32[]{:S(2)}, u32[]{:S(2)}) collective-permute-start(bf16[128,512]{1,0:T(8,128)(2,1)} %get-tuple-element.176), channel_id=1, source_target_pairs={{0,7},{1,6},{2,5},{3,4},{4,3},{5,2},{6,1},{7,0},{8,15},{9,14},{10,... | collective-permute-start | bytes 393224 | tf_op jit(solution)/shard_map/ppermute | solution.py:587
  96.7 12.3 %all-to-all-done.refs_4_ = bf16[4,128,1024]{2,1,0:T(8,128)(2,1)S(1)} async-done(((bf16[4,128,1024]{2,1,0:T(8,128)(2,1)}), bf16[4,128,1024]{2,1,0:T(8,128)(2,1)S(1)}, u32[]{:S(2)}, u32[]{:S(2)}) %all-to-all-start) | async-done | bytes 1048608 | tf_op jit(solution)/shard_map/all_to_all | solution.py:595
  110.0 5.9 %final_home.1 = (bf16[128,12288]{1,0:T(8,128)(2,1)}, bf16[4,3,2,512]{3,2,1,0:T(2,128)(2,1)}, f32[4,3,16,512]{3,2,1,0:T(8,128)}) custom-call(bf16[128,12288]{1,0:T(8,128)(2,1)} %bitcast.8, bf16[2,12288]{1,0:T(2,128)(2,1)} %copy-done.3, bf16[128,4096]{1,0:T(8,128)(2,1)} %bitcast.13, f32[3,12288]{1,0:T(4,128)} %taps_ref.3, bf16[4,128,1024]{2,1,0:T(8,128)(2,1)} %copy-done.11), custom_call_target="tpu_custom_call" | custom-call | flops 7864320 | bytes 4194304 | tf_op jit(solution)/shard_map/final_home/pallas_call | solution.py:518
  121.9 3.9 %final_other.1 = (bf16[128,12288]{1,0:T(8,128)(2,1)}, bf16[4,3,2,512]{3,2,1,0:T(2,128)(2,1)}, f32[4,3,16,512]{3,2,1,0:T(8,128)S(1)}) custom-call(bf16[128,12288]{1,0:T(8,128)(2,1)S(1)} %bitcast.10, bf16[2,12288]{1,0:T(2,128)(2,1)S(1)} %copy-done.4, bf16[128,4096]{1,0:T(8,128)(2,1)S(1)} %bitcast.15, ...), custom_call_target="tpu_custom_call", output_to_operand_aliasing={{0}: (12, {})} | custom-call | flops 7864320 | bytes 4194304 | tf_op jit(solution)/shard_map/final_other/pallas_call | solution.py:518
  125.8 4.1 %collective-permute-done.23.edge_ref = bf16[2,4,3,2,512]{4,3,2,1,0:T(2,128)(2,1)S(1)} collective-permute-done((bf16[2,4,3,2,512]{4,3,2,1,0:T(2,128)(2,1)S(1)}, bf16[2,4,3,2,512]{4,3,2,1,0:T(2,128)(2,1)S(1)}, u32[]{:S(2)}, u32[]{:S(2)}) %collective-permute-start.23) | collective-permute-done | bytes 49184 | tf_op jit(solution)/shard_map/ppermute | solution.py:675
  130.0 1.7 %fix.1 = (bf16[128,12288]{1,0:T(8,128)(2,1)}, f32[256,512]{1,0:T(8,128)}) custom-call(f32[3,12288]{1,0:T(4,128)S(1)} %copy-done.2, bf16[2,4,3,2,512]{4,3,2,1,0:T(2,128)(2,1)S(1)} %collective-permute-done.23.edge_ref, f32[4,3,16,512]{3,2,1,0:T(8,128)S(1)} %copy-done.5, ...), custom_call_target="tpu_custom_call", output_to_operand_aliasing={{0}: (6, {})} | custom-call | flops 1572864 | bytes 1572864 | tf_op jit(solution)/shard_map/fix/pallas_call | solution.py:568
  (89 shorter events, 18.8 us)
Async XLA Ops:
  1.6 8.6 %collective-permute-start = (bf16[2,12288]{1,0:T(2,128)(2,1)S(1)}, bf16[2,12288]{1,0:T(2,128)(2,1)S(1)}, u32[]{:S(2)}, u32[]{:S(2)}) collective-permute-start(bf16[2,12288]{1,0:T(2,128)(2,1)S(1)} %slice_bitcast_fusion), channel_id=1, source_target_pairs={{0,1},{1,2},{2,3},{3,4},{4,5},{5,6},{6,7},{8,9},{9,10},{10,11},{11... | collective-permute-start | bytes 147464 | tf_op jit(solution)/shard_map/ppermute | solution.py:675
  7.6 22.4 %collective-permute-start.4 = (bf16[256,512]{1,0:T(8,128)(2,1)S(1)}, bf16[256,512]{1,0:T(8,128)(2,1)S(1)}, u32[]{:S(2)}, u32[]{:S(2)}) collective-permute-start(bf16[256,512]{1,0:T(8,128)(2,1)S(1)} %multiply_convert_fusion), channel_id=1, source_target_pairs={{0,4},{1,5},{2,6},{3,7},{4,0},{5,1},{6,2},{7,3},{8,12},{9,13},{10,... | collective-permute-start | bytes 786440 | tf_op jit(solution)/shard_map/ppermute | solution.py:619
  15.6 14.4 %collective-permute-start.1 = (bf16[128,1024]{1,0:T(8,128)(2,1)}, bf16[128,1024]{1,0:T(8,128)(2,1)S(1)}, u32[]{:S(2)}, u32[]{:S(2)}) collective-permute-start(bf16[128,1024]{1,0:T(8,128)(2,1)} %get-tuple-element.118), channel_id=1, source_target_pairs={{0,1},{1,0},{2,3},{3,2},{4,5},{5,4},{6,7},{7,6},{8,9},{9,8},{10,11... | collective-permute-start | bytes 786440 | tf_op jit(solution)/shard_map/ppermute | solution.py:587
  17.2 12.8 %collective-permute-start.2 = (bf16[128,1024]{1,0:T(8,128)(2,1)}, bf16[128,1024]{1,0:T(8,128)(2,1)S(1)}, u32[]{:S(2)}, u32[]{:S(2)}) collective-permute-start(bf16[128,1024]{1,0:T(8,128)(2,1)} %get-tuple-element.119), channel_id=1, source_target_pairs={{0,2},{1,3},{2,0},{3,1},{4,6},{5,7},{6,4},{7,5},{8,10},{9,11},{10,... | collective-permute-start | bytes 786440 | tf_op jit(solution)/shard_map/ppermute | solution.py:587
  17.6 16.6 %collective-permute-start.3 = (bf16[128,1024]{1,0:T(8,128)(2,1)}, bf16[128,1024]{1,0:T(8,128)(2,1)S(1)}, u32[]{:S(2)}, u32[]{:S(2)}) collective-permute-start(bf16[128,1024]{1,0:T(8,128)(2,1)} %get-tuple-element.120), channel_id=1, source_target_pairs={{0,3},{1,2},{2,1},{3,0},{4,7},{5,6},{6,5},{7,4},{8,11},{9,10},{10,... | collective-permute-start | bytes 786440 | tf_op jit(solution)/shard_map/ppermute | solution.py:587
  34.2 22.1 %collective-permute-start.6 = (bf16[128,1024]{1,0:T(8,128)(2,1)}, bf16[128,1024]{1,0:T(8,128)(2,1)S(1)}, u32[]{:S(2)}, u32[]{:S(2)}) collective-permute-start(bf16[128,1024]{1,0:T(8,128)(2,1)} %get-tuple-element.140), channel_id=1, source_target_pairs={{0,1},{1,0},{2,3},{3,2},{4,5},{5,4},{6,7},{7,6},{8,9},{9,8},{10,11... | collective-permute-start | bytes 786440 | tf_op jit(solution)/shard_map/ppermute | solution.py:587
  34.7 21.6 %collective-permute-start.7 = (bf16[128,1024]{1,0:T(8,128)(2,1)}, bf16[128,1024]{1,0:T(8,128)(2,1)S(1)}, u32[]{:S(2)}, u32[]{:S(2)}) collective-permute-start(bf16[128,1024]{1,0:T(8,128)(2,1)} %get-tuple-element.141), channel_id=1, source_target_pairs={{0,2},{1,3},{2,0},{3,1},{4,6},{5,7},{6,4},{7,5},{8,10},{9,11},{10,... | collective-permute-start | bytes 786440 | tf_op jit(solution)/shard_map/ppermute | solution.py:587
  34.7 21.6 %collective-permute-start.8 = (bf16[128,1024]{1,0:T(8,128)(2,1)}, bf16[128,1024]{1,0:T(8,128)(2,1)S(1)}, u32[]{:S(2)}, u32[]{:S(2)}) collective-permute-start(bf16[128,1024]{1,0:T(8,128)(2,1)} %get-tuple-element.142), channel_id=1, source_target_pairs={{0,3},{1,2},{2,1},{3,0},{4,7},{5,6},{6,5},{7,4},{8,11},{9,10},{10,... | collective-permute-start | bytes 786440 | tf_op jit(solution)/shard_map/ppermute | solution.py:587
  37.7 16.0 %collective-permute-start.10 = (bf16[128,512]{1,0:T(8,128)(2,1)S(1)}, bf16[128,512]{1,0:T(8,128)(2,1)S(1)}, u32[]{:S(2)}, u32[]{:S(2)}) collective-permute-start(bf16[128,512]{1,0:T(8,128)(2,1)S(1)} %copy-done.21), channel_id=1, source_target_pairs={{0,7},{1,6},{2,5},{3,4},{4,3},{5,2},{6,1},{7,0},{8,15},{9,14},{10,... | collective-permute-start | bytes 393224 | tf_op jit(solution)/shard_map/ppermute | solution.py:587
  41.1 15.1 %collective-permute-start.9 = (bf16[128,512]{1,0:T(8,128)(2,1)S(1)}, bf16[128,512]{1,0:T(8,128)(2,1)S(1)}, u32[]{:S(2)}, u32[]{:S(2)}) collective-permute-start(bf16[128,512]{1,0:T(8,128)(2,1)S(1)} %copy-done.20), channel_id=1, source_target_pairs={{0,6},{1,7},{2,4},{3,5},{4,2},{5,3},{6,0},{7,1},{8,14},{9,15},{10,... | collective-permute-start | bytes 393224 | tf_op jit(solution)/shard_map/ppermute | solution.py:587
  56.4 11.3 %collective-permute-start.11 = (bf16[128,512]{1,0:T(8,128)(2,1)S(1)}, bf16[128,512]{1,0:T(8,128)(2,1)S(1)}, u32[]{:S(2)}, u32[]{:S(2)}) collective-permute-start(bf16[128,512]{1,0:T(8,128)(2,1)S(1)} %copy-done.17), channel_id=1, source_target_pairs={{0,4},{1,5},{2,6},{3,7},{4,0},{5,1},{6,2},{7,3},{8,12},{9,13},{10,... | collective-permute-start | bytes 393224 | tf_op jit(solution)/shard_map/ppermute | solution.py:587
  56.5 15.1 %collective-permute-start.12 = (bf16[128,512]{1,0:T(8,128)(2,1)S(1)}, bf16[128,512]{1,0:T(8,128)(2,1)S(1)}, u32[]{:S(2)}, u32[]{:S(2)}) collective-permute-start(bf16[128,512]{1,0:T(8,128)(2,1)S(1)} %copy-done.16), channel_id=1, source_target_pairs={{0,5},{1,4},{2,7},{3,6},{4,1},{5,0},{6,3},{7,2},{8,13},{9,12},{10,... | collective-permute-start | bytes 393224 | tf_op jit(solution)/shard_map/ppermute | solution.py:587
  59.3 22.9 %collective-permute-start.13 = (bf16[128,1024]{1,0:T(8,128)(2,1)S(1)}, bf16[128,1024]{1,0:T(8,128)(2,1)S(1)}, u32[]{:S(2)}, u32[]{:S(2)}) collective-permute-start(bf16[128,1024]{1,0:T(8,128)(2,1)S(1)} %get-tuple-element.164), channel_id=1, source_target_pairs={{0,1},{1,0},{2,3},{3,2},{4,5},{5,4},{6,7},{7,6},{8,9},{9,8},{10,11... | collective-permute-start | bytes 786440 | tf_op jit(solution)/shard_map/ppermute | solution.py:587
  60.9 21.3 %collective-permute-start.14 = (bf16[128,1024]{1,0:T(8,128)(2,1)S(1)}, bf16[128,1024]{1,0:T(8,128)(2,1)S(1)}, u32[]{:S(2)}, u32[]{:S(2)}) collective-permute-start(bf16[128,1024]{1,0:T(8,128)(2,1)S(1)} %get-tuple-element.165), channel_id=1, source_target_pairs={{0,2},{1,3},{2,0},{3,1},{4,6},{5,7},{6,4},{7,5},{8,10},{9,11},{10,... | collective-permute-start | bytes 786440 | tf_op jit(solution)/shard_map/ppermute | solution.py:587
  60.9 24.5 %collective-permute-start.15 = (bf16[128,1024]{1,0:T(8,128)(2,1)S(1)}, bf16[128,1024]{1,0:T(8,128)(2,1)S(1)}, u32[]{:S(2)}, u32[]{:S(2)}) collective-permute-start(bf16[128,1024]{1,0:T(8,128)(2,1)S(1)} %get-tuple-element.166), channel_id=1, source_target_pairs={{0,3},{1,2},{2,1},{3,0},{4,7},{5,6},{6,5},{7,4},{8,11},{9,10},{10,... | collective-permute-start | bytes 786440 | tf_op jit(solution)/shard_map/ppermute | solution.py:587
  67.7 17.7 %collective-permute-start.17 = (bf16[256,512]{1,0:T(8,128)(2,1)S(1)}, bf16[256,512]{1,0:T(8,128)(2,1)S(1)}, u32[]{:S(2)}, u32[]{:S(2)}) collective-permute-start(bf16[256,512]{1,0:T(8,128)(2,1)S(1)} %add_convert_fusion), channel_id=1, source_target_pairs={{0,4},{1,5},{2,6},{3,7},{4,0},{5,1},{6,2},{7,3},{8,12},{9,13},{10,... | collective-permute-start | bytes 786440 | tf_op jit(solution)/shard_map/ppermute | solution.py:638
  85.4 23.6 %all-to-all-start = ((bf16[4,128,1024]{2,1,0:T(8,128)(2,1)}), bf16[4,128,1024]{2,1,0:T(8,128)(2,1)S(1)}, u32[]{:S(2)}, u32[]{:S(2)}) async-start(bf16[4,128,1024]{2,1,0:T(8,128)(2,1)} %bitcast.17), calls=%async_computation | async-start | bytes 2097152 | tf_op jit(solution)/shard_map/all_to_all | solution.py:595
  88.9 27.0 %collective-permute-start.22 = (f32[512,512]{1,0:T(8,128)}, f32[512,512]{1,0:T(8,128)}, u32[]{:S(2)}, u32[]{:S(2)}) collective-permute-start(f32[512,512]{1,0:T(8,128)} %get-tuple-element.178), channel_id=1, source_target_pairs={{0,8},{8,0},{16,24},{24,16},{1,9},{9,1},{17,25},{25,17},{2,10},{10... | collective-permute-start | bytes 3145736 | tf_op jit(solution)/shard_map/ppermute | solution.py:645
  89.0 28.6 %collective-permute-start.18 = (bf16[128,512]{1,0:T(8,128)(2,1)}, bf16[128,512]{1,0:T(8,128)(2,1)S(1)}, u32[]{:S(2)}, u32[]{:S(2)}) collective-permute-start(bf16[128,512]{1,0:T(8,128)(2,1)} %get-tuple-element.173), channel_id=1, source_target_pairs={{0,4},{1,5},{2,6},{3,7},{4,0},{5,1},{6,2},{7,3},{8,12},{9,13},{10,... | collective-permute-start | bytes 393224 | tf_op jit(solution)/shard_map/ppermute | solution.py:587
  89.5 28.1 %collective-permute-start.19 = (bf16[128,512]{1,0:T(8,128)(2,1)}, bf16[128,512]{1,0:T(8,128)(2,1)S(1)}, u32[]{:S(2)}, u32[]{:S(2)}) collective-permute-start(bf16[128,512]{1,0:T(8,128)(2,1)} %get-tuple-element.174), channel_id=1, source_target_pairs={{0,5},{1,4},{2,7},{3,6},{4,1},{5,0},{6,3},{7,2},{8,13},{9,12},{10,... | collective-permute-start | bytes 393224 | tf_op jit(solution)/shard_map/ppermute | solution.py:587
  93.2 24.4 %collective-permute-start.20 = (bf16[128,512]{1,0:T(8,128)(2,1)}, bf16[128,512]{1,0:T(8,128)(2,1)S(1)}, u32[]{:S(2)}, u32[]{:S(2)}) collective-permute-start(bf16[128,512]{1,0:T(8,128)(2,1)} %get-tuple-element.175), channel_id=1, source_target_pairs={{0,6},{1,7},{2,4},{3,5},{4,2},{5,3},{6,0},{7,1},{8,14},{9,15},{10,... | collective-permute-start | bytes 393224 | tf_op jit(solution)/shard_map/ppermute | solution.py:587
  94.8 22.8 %collective-permute-start.21 = (bf16[128,512]{1,0:T(8,128)(2,1)}, bf16[128,512]{1,0:T(8,128)(2,1)S(1)}, u32[]{:S(2)}, u32[]{:S(2)}) collective-permute-start(bf16[128,512]{1,0:T(8,128)(2,1)} %get-tuple-element.176), channel_id=1, source_target_pairs={{0,7},{1,6},{2,5},{3,4},{4,3},{5,2},{6,1},{7,0},{8,15},{9,14},{10,... | collective-permute-start | bytes 393224 | tf_op jit(solution)/shard_map/ppermute | solution.py:587
  119.1 10.9 %collective-permute-start.24 = (bf16[256,512]{1,0:T(8,128)(2,1)S(1)}, bf16[256,512]{1,0:T(8,128)(2,1)S(1)}, u32[]{:S(2)}, u32[]{:S(2)}) collective-permute-start(bf16[256,512]{1,0:T(8,128)(2,1)S(1)} %dynamic-slice_convert_fusion), channel_id=1, source_target_pairs={{0,16},{8,24},{16,0},{24,8},{1,17},{9,25},{17,1},{25,9},{2,18},{10... | collective-permute-start | bytes 786440 | tf_op jit(solution)/shard_map/ppermute | solution.py:660
  120.6 9.3 %collective-permute-start.23 = (bf16[2,4,3,2,512]{4,3,2,1,0:T(2,128)(2,1)S(1)}, bf16[2,4,3,2,512]{4,3,2,1,0:T(2,128)(2,1)S(1)}, u32[]{:S(2)}, u32[]{:S(2)}) collective-permute-start(bf16[2,4,3,2,512]{4,3,2,1,0:T(2,128)(2,1)S(1)} %edge_other.1), channel_id=1, source_target_pairs={{1,0},{2,1},{3,2},{4,3},{5,4},{6,5},{7,6},{9,8},{10,9},{11,10},{12... | collective-permute-start | bytes 147464 | tf_op jit(solution)/shard_map/ppermute | solution.py:675
  (26 other events, 323.5 us)
